TPU v7x, 32 devices: a whole 2x2x4 slice. The times are simulated.
32 devices in a mesh: parts: 2 (over y), row: 4 (over z), col: 2 (over x), rep: 2 (over core).
Axes of the slice: x: 2, y: 2, z: 4, core: 2. Of those that a mesh axis runs over, the one named last changes fastest.
Arguments:
- samples: float32 [192, 4096], P('parts', ('row', 'col', 'rep')), parts along dimension 0, may hold values from -6 to 6
- diag_tiles: float32 [32, 256, 256], P(('parts', 'row', 'col', 'rep')), parts along dimension 0, may hold values from -1 to 2, as said below
- omega_slots: float32 [8, 4, 8, 256, 256], P(('parts', 'row'), ('col', 'rep')), parts along dimension 0, may hold values from -1 to 1, as said below
- tile_pos: int32 [8, 4, 8, 2], P(('parts', 'row'), ('col', 'rep')), parts along dimension 0, may hold values from 0 to 3, as said below
- tile_count: int32 [8, 4], P(('parts', 'row'), ('col', 'rep')), parts along dimension 0, may hold values from 0 to 8, as said below
Outputs:
- new_slots: float32 [8, 4, 8, 256, 256], P(('parts', 'row'), ('col', 'rep')), parts along dimension 0
- new_diag: float32 [32, 256, 256], P(('parts', 'row', 'col', 'rep')), parts along dimension 0
There are 2 independent parts, one for each index of `parts`. A program takes and returns all parts, laid end to end along the dimension named above; each array names one. Nothing has to cross between parts.
Inputs may be any that keep to these rules, and one draw needn't show every extreme that they name: `tile_pos`: live slots of a cell name distinct blocks. The pattern and Omega are symmetric: slot s of cell (b, a) names the transposed block of slot s of cell (a, b) and holds its tile transposed, with the same count; in a cell (a, a) the slots 2k and 2k + 1 hold a block and its transpose, never a diagonal block. `tile_count`: equal for cells (a, b) and (b, a), even for cells (a, a); some cell holds 8 in every draw. `omega_slots`: symmetric as a whole matrix together with the slots (see tile_pos). `diag_tiles`: each block is symmetric, with diagonal entries from 1 to 2.
All inputs are finite; a program needn't handle non-finite values.
Results may differ from a plain program's by a relative error of at most 0.0001.
Values sent between devices are 32-bit elements; how exact they have to be, the bound alone decides.
No kernel may reach another device: no remote copies, remote signals or barrier semaphores. Data moves between devices by JAX's collectives and lax.ppermute only.
A program may use at most 64 MiB of HBM per device.

v0:
```python
import jax
import jax.numpy as jnp
from jax import lax
from jax.sharding import PartitionSpec as P

highest = lax.Precision.HIGHEST
step_size = 1.0
penalty = 0.1


def from_root(block, axis, holder):
    block = jnp.where(lax.axis_index(axis) == holder, block, jnp.zeros_like(block))
    return lax.psum(block, axis)


def soft_limit(values):
    limit_value = step_size * penalty
    return values - jnp.clip(values, -limit_value, limit_value)


def product(left, right):
    return jnp.dot(left, right, precision=highest, preferred_element_type=jnp.float32)


def on_device(samples, diag_tiles, omega_slots, tile_pos, tile_count):
    groups = lax.axis_size(("col", "rep"))
    own_col = lax.axis_index(("col", "rep"))
    sample_count, tile_side = samples.shape
    slot_total = omega_slots.shape[2]
    row_panel = lax.all_gather(samples, ("col", "rep"), axis=1, tiled=True)
    col_panel = from_root(row_panel, "row", own_col)
    row_blocks = row_panel.reshape(sample_count, groups, tile_side)
    col_blocks = col_panel.reshape(sample_count, groups, tile_side)
    slot_tiles = omega_slots.reshape(slot_total, tile_side, tile_side)
    tile_place = tile_pos.reshape(slot_total, 2)
    alive_mask = (jnp.arange(slot_total) < tile_count.reshape(())).astype(jnp.float32)
    row_pick = jax.nn.one_hot(tile_place[:, 0], groups, dtype=jnp.float32)
    panel_cols = jnp.take(col_blocks, tile_place[:, 1], axis=1)
    slot_terms = (
        jnp.einsum("nsk,stk->snt", panel_cols, slot_tiles, precision=highest)
        * alive_mask[:, None, None]
    )
    diag_tile = diag_tiles[0]
    diag_term = product(samples, diag_tile)
    own_image = (
        lax.psum_scatter(
            jnp.einsum("sg,snt->gnt", row_pick, slot_terms, precision=highest),
            ("col", "rep"),
            scatter_dimension=0,
            tiled=True,
        )[0]
        + diag_term
    )
    image_group = lax.all_gather(own_image[None], ("col", "rep"), axis=0, tiled=True)
    image_other = from_root(image_group, "row", own_col)
    panel_rows = jnp.take(row_blocks, tile_place[:, 0], axis=1)
    image_rows = jnp.take(image_group, tile_place[:, 0], axis=0)
    image_cols = jnp.take(image_other, tile_place[:, 1], axis=0)
    gradient = jnp.einsum("nsk,snt->skt", panel_rows, image_cols, precision=highest)
    gradient = gradient + jnp.einsum("snk,nst->skt", image_rows, panel_cols, precision=highest)
    gradient = gradient / (2.0 * sample_count)
    new_slots = soft_limit(slot_tiles - step_size * gradient) * alive_mask[:, None, None]
    new_slots = new_slots.reshape(omega_slots.shape)
    identity = jnp.eye(tile_side, dtype=jnp.float32)
    diag_gradient = (product(samples.T, own_image) + product(own_image.T, samples)) / (
        2.0 * sample_count
    )
    diag_gradient = diag_gradient - identity / jnp.diagonal(diag_tile)[None, :]
    shifted = diag_tile - step_size * diag_gradient
    new_diag = (identity * shifted + (1.0 - identity) * soft_limit(shifted))[None]
    return (new_slots, new_diag)


def solution(mesh):
    placed = (
        P("parts", ("row", "col", "rep")),
        P(("parts", "row", "col", "rep"), None, None),
        P(("parts", "row"), ("col", "rep"), None, None, None),
        P(("parts", "row"), ("col", "rep"), None, None),
        P(("parts", "row"), ("col", "rep")),
    )
    return jax.shard_map(
        on_device,
        mesh=mesh,
        in_specs=placed,
        out_specs=(
            P(("parts", "row"), ("col", "rep"), None, None, None),
            P(("parts", "row", "col", "rep"), None, None),
        ),
        check_vma=False,
    )
```

profile of v0, /device:TPU:6, one launch (start us, length us, event | category | flops | bytes accessed | tf_op | source)
XLA Modules:
  0.0 143.1 jit_solution(12529719390816591339)
XLA Ops:
  7.2 0.0 all-reduce.3.cloned.1.call-start
  7.2 6.5 %all_gather.6 = f32[96,1024]{1,0:T(8,128)S(1)} all-gather(f32[96,256]{1,0:T(8,128)} %param.9), channel_id=1, replica_groups=mesh['parts'=2,'row'=4,'col'=2,'rep'=2] {'col','rep'}, dimensions={1}, use_global_device_ids=true | all-gather | bytes 491520 | tf_op jit(solution)/shard_map/all_gather | solution.py:30
  13.8 0.8 copy.24
  14.6 0.0 all-reduce.3.cloned.1.call-update
  14.6 0.0 reduce-scatter.2.cloned.1.call-start
  14.7 0.5 compare_and_fusion.1
  15.9 0.5 slice_bitcast_fusion
  16.4 36.4 %all-reduce.3.cloned.1.call-done = f32[96,4,256]{2,0,1:T(8,128)} async-done(((f32[96,4,256]{2,0,1:T(8,128)}), f32[96,4,256]{2,0,1:T(8,128)}) %all-reduce.3.cloned.1.call-update) | async-done | bytes 393232 | tf_op jit(solution)/shard_map/psum | solution.py:13
  52.9 1.6 %gather_fusion.2 = f32[8,96,256]{2,1,0:T(8,128)S(1)} fusion(f32[96,4,256]{2,0,1:T(8,128)} %all-reduce.3.cloned.1.call-done, s32[1024]{0:T(1024)S(1)} %pad_clamp_fusion), kind=kCustom, calls=%fused_computation.2.clone | custom fusion | bytes 1572896 | tf_op jit(solution)/shard_map/jit(_take)/gather | solution.py:38
  54.5 2.1 %fusion.4 = f32[8,96,256]{2,1,0:T(8,128)S(1)} fusion(f32[1,1,8,256,256]{4,3,2,1,0:T(8,128)S(1)} %copy-done.1, f32[8,96,256]{2,1,0:T(8,128)S(1)} %gather_fusion.2, f32[8]{0:T(128)S(1)} %compare_convert_fusion, pred[8]{0:T(512)(128)(4,1)S(1)} %get-tuple-element.8), kind=kOutput, calls=%fused_computation.11 | convolution fusion | flops 604372992 | bytes 3670056 | tf_op jit(solution)/shard_map/nsk,stk->snt/dot_general | solution.py:40
  56.7 0.9 fusion.11
  57.6 0.8 copy.16
  58.4 0.0 reduce-scatter.2.cloned.1.call-update
  58.4 0.0 all-reduce.5.cloned.1.call-start
  58.5 1.0 copy.25
  59.5 0.7 pad_clamp_fusion.1
  60.2 1.5 %gather_fusion.1 = f32[8,96,256]{2,1,0:T(8,128)} fusion(f32[96,4,256]{2,0,1:T(8,128)S(1)} %bitcast.65, s32[1024]{0:T(1024)S(1)} %pad_clamp_fusion.1), kind=kCustom, calls=%fused_computation.clone | custom fusion | bytes 1572896 | tf_op jit(solution)/shard_map/jit(_take)/gather | solution.py:56
  61.7 2.9 %gather_fusion = f32[256]{0:T(256)} fusion(f32[256,256]{1,0:T(8,128)S(1)} %bitcast.62, s32[256]{0:T(256)S(1)} %bitcast.61), kind=kCustom, calls=%fused_computation.4 | custom fusion | bytes 4096 | tf_op jit(solution)/shard_map/jit(diagonal)/cond/branch_0_fun/gather | solution.py:68
  64.5 13.7 %reduce-scatter.2.cloned.1.call-done = f32[1,96,256]{2,1,0:T(8,128)} async-done(((f32[4,96,256]{2,1,0:T(8,128)}), f32[1,96,256]{2,1,0:T(8,128)}) %reduce-scatter.2.cloned.1.call-update) | async-done | bytes 98320 | tf_op jit(solution)/shard_map/reduce_scatter | solution.py:46
  78.3 1.2 convolution_add_fusion
  79.5 0.6 copy-done.4
  80.1 6.4 %all-gather = f32[384,256]{1,0:T(8,128)S(1)} all-gather(f32[96,256]{1,0:T(8,128)S(1)} %convolution_add_fusion), channel_id=2, replica_groups=mesh['parts'=2,'row'=4,'col'=2,'rep'=2] {'col','rep'}, dimensions={0}, use_global_device_ids=true | all-gather | bytes 491520 | tf_op jit(solution)/shard_map/all_gather | solution.py:54
  86.6 0.8 broadcast_select_fusion
  87.3 1.5 %gather_fusion.4 = f32[8,96,256]{2,1,0:T(8,128)} fusion(f32[4,96,256]{2,1,0:T(8,128)S(1)} %bitcast.64, s32[1024]{0:T(1024)S(1)} %pad_clamp_fusion.1), kind=kCustom, calls=%fused_computation.3.clone | custom fusion | bytes 1572896 | tf_op jit(solution)/shard_map/jit(_take)/gather | solution.py:57
  88.9 0.0 all-reduce.5.cloned.1.call-update
  88.9 1.4 fusion.39
  90.3 0.8 copy.17
  91.1 1.7 %fusion.30 = f32[1,256,256]{2,1,0:T(8,128)} fusion(f32[256,256]{1,0:T(8,128)S(1)} %fusion.39, f32[256,256]{0,1:T(8,128)} %copy.17, f32[256]{0:T(256)} %gather_fusion, f32[1,256,256]{2,1,0:T(8,128)S(1)} %copy-done), kind=kLoop, calls=%fused_computation.41 | loop fusion | flops 851968 | bytes 1049600 | tf_op jit(solution)/shard_map/broadcast_in_dim | solution.py:70
  92.8 34.0 %all-reduce.5.cloned.1.call-done = f32[4,96,256]{2,1,0:T(8,128)} async-done(((f32[4,96,256]{2,1,0:T(8,128)}), f32[4,96,256]{2,1,0:T(8,128)}) %all-reduce.5.cloned.1.call-update) | async-done | bytes 393232 | tf_op jit(solution)/shard_map/psum | solution.py:13
  126.9 2.5 %gather_fusion.3 = f32[8,96,256]{2,1,0:T(8,128)} fusion(f32[4,96,256]{2,1,0:T(8,128)} %all-reduce.5.cloned.1.call-done, s32[1024]{0:T(1024)S(1)} %pad_clamp_fusion), kind=kCustom, calls=%fused_computation.1.clone | custom fusion | bytes 1572896 | tf_op jit(solution)/shard_map/jit(_take)/gather | solution.py:58
  129.3 3.5 %fusion.9 = f32[8,256,256]{2,1,0:T(8,128)S(1)} fusion(f32[8,96,256]{2,1,0:T(8,128)} %gather_fusion.3, f32[8,96,256]{2,1,0:T(8,128)} %gather_fusion.1, pred[8]{0:T(512)(128)(4,1)S(1)} %get-tuple-element.8, pred[8]{0:T(512)(128)(4,1)S(1)} %get-tuple-element.4), kind=kOutput, calls=%fused_computation.15 | convolution fusion | flops 604372992 | bytes 3670032 | tf_op jit(solution)/shard_map/nsk,snt->skt/dot_general | solution.py:59
  132.8 3.8 %fusion.1 = f32[1,1,8,256,256]{4,3,2,1,0:T(8,128)} fusion(f32[1,1,8,256,256]{4,3,2,1,0:T(8,128)S(1)} %copy-done.1, f32[8,256,256]{2,1,0:T(8,128)S(1)} %fusion.9, f32[8]{0:T(128)S(1)} %copy-done.6, f32[8,96,256]{2,1,0:T(8,128)S(1)} %copy-done.3, f32[8,96,256]{2,1,0:T(8,128)S(1)} %gather_fusion.2, pred[8]{0:T(512)(128)(4,1)S(1)} %get-tuple-element.8, ...), kind=kOutput, calls=%fused_computation.7 | convolution fusion | flops 607518720 | bytes 7864368 | tf_op jit(solution)/shard_map/snk,nst->skt/dot_general | solution.py:60
  (21 shorter events, 0.1 us)
Async XLA Ops:
  7.2 7.5 %copy-start.7 = (s32[1,1,8,2]{2,3,1,0:T(2,128)S(1)}, s32[1,1,8,2]{2,3,1,0:T(2,128)}, u32[]{:S(2)}) copy-start(s32[1,1,8,2]{2,3,1,0:T(2,128)} %param.12) | copy-start | bytes 196
  7.2 47.3 %copy-start.1 = (f32[1,1,8,256,256]{4,3,2,1,0:T(8,128)S(1)}, f32[1,1,8,256,256]{4,3,2,1,0:T(8,128)}, u32[]{:S(2)}) copy-start(f32[1,1,8,256,256]{4,3,2,1,0:T(8,128)} %param.11) | copy-start | bytes 6291460
  7.2 45.7 %all-reduce.3.cloned.1.call-start = ((), (), s32[]{:S(2)}) async-start(), calls=%async_computation.1 | async-start | bytes 786432 | tf_op jit(solution)/shard_map/psum | solution.py:13
  13.7 42.9 %copy-start.2 = (f32[96,1024]{1,0:T(8,128)}, f32[96,1024]{1,0:T(8,128)S(1)}, u32[]{:S(2)}) copy-start(f32[96,1024]{1,0:T(8,128)S(1)} %all_gather.6) | copy-start | bytes 1179652
  14.6 63.7 %reduce-scatter.2.cloned.1.call-start = ((), (), s32[]{:S(2)}) async-start(), calls=%async_computation.2 | async-start | bytes 491520 | tf_op jit(solution)/shard_map/reduce_scatter | solution.py:46
  15.9 40.8 %copy-start.5 = (f32[8]{0:T(128)}, f32[8]{0:T(128)S(1)}, u32[]{:S(2)}) copy-start(f32[8]{0:T(128)S(1)} %compare_convert_fusion) | copy-start | bytes 100
  54.5 2.2 %copy-start.8 = (s32[8]{0:T(128)S(1)}, s32[8]{0:T(128)}, u32[]{:S(2)}) copy-start(s32[8]{0:T(128)} %slice_bitcast_fusion) | copy-start | bytes 100
  56.7 5.0 %copy-start = (f32[1,256,256]{2,1,0:T(8,128)S(1)}, f32[1,256,256]{2,1,0:T(8,128)}, u32[]{:S(2)}) copy-start(f32[1,256,256]{2,1,0:T(8,128)} %param.10) | copy-start | bytes 786436
  58.4 68.4 %all-reduce.5.cloned.1.call-start = ((), (), s32[]{:S(2)}) async-start(), calls=%async_computation.3 | async-start | bytes 786432 | tf_op jit(solution)/shard_map/psum | solution.py:13
  79.5 0.6 copy-start.4
  129.3 3.5 %copy-start.3 = (f32[8,96,256]{2,1,0:T(8,128)S(1)}, f32[8,96,256]{2,1,0:T(8,128)}, u32[]{:S(2)}) copy-start(f32[8,96,256]{2,1,0:T(8,128)} %gather_fusion.4) | copy-start | bytes 2359300
  129.3 3.5 %copy-start.6 = (f32[8]{0:T(128)S(1)}, f32[8]{0:T(128)}, u32[]{:S(2)}) copy-start(f32[8]{0:T(128)} %copy-done.5) | copy-start | bytes 100
Sparse Core Ops, SparseCore 0:
  14.7 38.0 all-reduce.2
  58.6 19.6 reduce-scatter.1
  89.0 37.7 all-reduce.4
where the time goes:
time: 145 us; the launch traced here: 143 us
  waiting for transfers between devices  84.2 us (58%)
  local copies, waits for them, and re-layouts  14.7 us (10%)
  between operations  14.6 us (10%)
  blocking collectives  12.9 us (9%)
  matrix products  12.9 us (9%)
  other arithmetic  3.75 us (3%)
    psum x2, waiting for transfers between devices, from_root(): return lax.psum(block, axis)  70.5 us
    reduce_scatter x1, waiting for transfers between devices, on_device(): lax.psum_scatter(jnp.einsum('sg,snt->gnt', row_pick, slot_terms, precisio...  13.7 us
    all_gather x1, blocking collectives, on_device(): row_panel = lax.all_gather(samples, ('col', 'rep'), axis=1, tiled=True)  6.49 us
    all_gather x1, blocking collectives, on_device(): lax.all_gather(own_image[None], ('col', 'rep'), axis=0, tiled=True)  6.44 us
    dot_general x1, matrix products, on_device(): jnp.einsum('snk,nst->skt', image_rows, panel_cols, precision=highest)  3.79 us
    dot_general x1, matrix products, on_device(): jnp.einsum('nsk,snt->skt', panel_rows, image_cols, precision=highest)  3.46 us
  transfers between devices with their start and end apart: 3, of which 3 were waited for; matrix products, arithmetic and copies ran while one was open for 8% of the time, Pallas kernels for 0%

commit v1 on v0

v1 whole, which is shorter than its diff:
```python
import functools

import jax
import jax.numpy as jnp
from jax import lax
from jax.experimental import pallas as pl
from jax.experimental.pallas import tpu as pltpu
from jax.sharding import PartitionSpec as P

step_size = 1.0
penalty = 0.1
grid_axes = ("row", "col", "rep")
line_axes = ("col", "rep")
f32 = jnp.float32
bf16 = jnp.bfloat16
vmem = pl.BlockSpec(memory_space=pltpu.VMEM)
smem = pl.BlockSpec(memory_space=pltpu.SMEM)


def halves(values):
    high = values.astype(bf16)
    return high, (values - high.astype(f32)).astype(bf16)


def dot(left, right, dims):
    return lax.dot_general(left, right, (dims, ((), ())), preferred_element_type=f32)


def soft_limit(values):
    limit_value = step_size * penalty
    return values - jnp.clip(values, -limit_value, limit_value)


def split_kernel(tiles, high, low):
    high[...], low[...] = halves(tiles[...])


def split_tiles(tiles):
    slots, side, _ = tiles.shape
    block = pl.BlockSpec((1, side, side), lambda s: (s, 0, 0))
    shape = jax.ShapeDtypeStruct(tiles.shape, bf16)
    return pl.pallas_call(
        split_kernel,
        grid=(slots,),
        out_shape=(shape, shape),
        in_specs=[block],
        out_specs=(block, block),
        name="split_tiles",
    )(tiles)


def partial_kernel(groups, place, count, samples, diag, high, low, *refs):
    pieces = refs[:groups]
    kept, sent, panel, total = refs[groups:]
    row = lax.axis_index("row")
    col = lax.axis_index("col")
    rep = lax.axis_index("rep")
    rows = samples.shape[0]
    for turn in range(groups):
        block = lax.rem(row + turn, groups)
        panel[block, :rows], panel[block, rows:] = halves(pieces[turn][...])
    total[...] = jnp.zeros_like(total)

    def term(x_high, both, w_high, w_low, dims):
        wide = dot(both, w_high, dims)
        return wide[:rows] + wide[rows:] + dot(x_high, w_low, dims)

    own_high, own_low = halves(samples[...])
    total[col * 2 + rep] = term(
        own_high, jnp.concatenate([own_high, own_low], axis=0), *halves(diag[0]), ((1,), (0,))
    )
    for slot in range(high.shape[0]):

        @pl.when(slot < count[0, 0])
        def _():
            source = panel.at[place[slot, 1]]
            total[place[slot, 0]] += term(
                source[:rows], source[...], high[slot], low[slot], ((1,), (1,))
            )

    for pair in range(groups // 2):
        kept[pair] = total[2 * pair + rep]
        sent[pair] = total[2 * pair + 1 - rep]


def partial_image(place, count, samples, diag, high, low, pieces):
    groups = len(pieces)
    rows, side = samples.shape
    shape = jax.ShapeDtypeStruct((groups // 2, rows, side), f32)
    return pl.pallas_call(
        functools.partial(partial_kernel, groups),
        out_shape=(shape, shape),
        in_specs=[smem, smem] + [vmem] * (4 + groups),
        out_specs=(vmem, vmem),
        scratch_shapes=[
            pltpu.VMEM((groups, 2 * rows, side), bf16),
            pltpu.VMEM((groups, rows, side), f32),
        ],
        compiler_params=pltpu.CompilerParams(vmem_limit_bytes=48 * 2**20),
        name="partial_image",
    )(place, count, samples, diag, high, low, *pieces)


def panels_kernel(groups, own_image, other_image, *refs):
    row_pieces, col_pieces = refs[:groups], refs[groups : 2 * groups]
    left_high, left_low, right_high, right_low = refs[2 * groups :]
    row = lax.axis_index("row")
    own = lax.axis_index("col") * 2 + lax.axis_index("rep")
    rep = lax.axis_index("rep")
    rows = own_image.shape[1]
    for turn in range(groups):
        block = lax.rem(own + groups - turn, groups)
        high, low = halves(row_pieces[turn][...].T)
        left_high[block, :, :rows], left_low[block, :, :rows] = high, low
        block = lax.rem(row + turn, groups)
        right_high[block], right_low[block] = halves(col_pieces[turn][...])
    for pair in range(groups // 2):
        for parity, image in ((rep, own_image), (1 - rep, other_image)):
            high, low = halves(image[pair].T)
            block = 2 * pair + parity
            left_high[block, :, rows:], left_low[block, :, rows:] = high, low


def early_panels(own_image, other_image, row_pieces, col_pieces):
    groups = len(row_pieces)
    _, rows, side = own_image.shape
    left = jax.ShapeDtypeStruct((groups, side, 2 * rows), bf16)
    right = jax.ShapeDtypeStruct((groups, rows, side), bf16)
    return pl.pallas_call(
        functools.partial(panels_kernel, groups),
        out_shape=(left, left, right, right),
        in_specs=[vmem] * (2 + 2 * groups),
        out_specs=(vmem,) * 4,
        compiler_params=pltpu.CompilerParams(vmem_limit_bytes=48 * 2**20),
        name="early_panels",
    )(own_image, other_image, *row_pieces, *col_pieces)


def slots_kernel(
    groups, place, count, left_high, left_low, x_high, x_low, first, second, tiles, out, high, low
):
    slot = pl.program_id(0)
    half = groups // 2
    rows = x_high.shape[1]

    @pl.when(slot == 0)
    def _():
        turned = lax.div(lax.axis_index("row"), half)
        for pair in range(half):
            for turn, piece in enumerate((first, second)):
                block = 2 * pair + lax.rem(turned + turn, 2)
                high[block, :rows], low[block, :rows] = halves(piece[pair])
        for block in range(groups):
            high[block, rows:] = x_high[block]
            low[block, rows:] = x_low[block]

    alive = slot < count[0, 0]

    @pl.when(alive)
    def _():
        left, right = place[slot, 0], place[slot, 1]
        dims = ((1,), (0,))
        gradient = dot(left_high[left], high[right], dims)
        gradient += dot(left_low[left], high[right], dims)
        gradient += dot(left_high[left], low[right], dims)
        out[0] = soft_limit(tiles[0] - gradient * (step_size / (2.0 * rows)))

    @pl.when(jnp.logical_not(alive))
    def _():
        out[...] = jnp.zeros_like(out)


def update_slots(place, count, left_high, left_low, x_high, x_low, first, second, tiles):
    groups, rows, side = x_high.shape
    block = pl.BlockSpec((1, side, side), lambda s: (s, 0, 0))
    return pl.pallas_call(
        functools.partial(slots_kernel, groups),
        grid=(tiles.shape[0],),
        out_shape=jax.ShapeDtypeStruct(tiles.shape, f32),
        in_specs=[smem, smem] + [vmem] * 6 + [block],
        out_specs=block,
        scratch_shapes=[pltpu.VMEM((groups, 2 * rows, side), bf16)] * 2,
        compiler_params=pltpu.CompilerParams(vmem_limit_bytes=48 * 2**20),
        name="update_slots",
    )(place, count, left_high, left_low, x_high, x_low, first, second, tiles)


def diag_kernel(samples, image, tiles, out):
    rows, side = samples.shape
    own = image[lax.axis_index("col")]
    left_high, left_low = halves(samples[...].T)
    right_high, right_low = halves(own)
    dims = ((1,), (0,))
    one_side = dot(left_high, right_high, dims) + dot(left_low, right_high, dims)
    one_side += dot(left_high, right_low, dims)
    tile = tiles[0]
    row = lax.broadcasted_iota(jnp.int32, (side, side), 0)
    on_diag = row == lax.broadcasted_iota(jnp.int32, (side, side), 1)
    gradient = (one_side + one_side.T) * (1.0 / (2.0 * rows))
    shifted = tile - step_size * gradient
    inverse = step_size / jnp.where(on_diag, tile, 1.0)
    out[0] = jnp.where(on_diag, shifted + inverse, soft_limit(shifted))


def update_diag(samples, image, tiles):
    return pl.pallas_call(
        diag_kernel,
        out_shape=jax.ShapeDtypeStruct(tiles.shape, f32),
        in_specs=[vmem] * 3,
        out_specs=vmem,
        name="update_diag",
    )(samples, image, tiles)


def on_device(samples, diag_tiles, omega_slots, tile_pos, tile_count):
    groups = lax.axis_size(line_axes)
    cols = lax.axis_size("col")
    slots, side = omega_slots.shape[2], omega_slots.shape[3]
    tiles = omega_slots.reshape(slots, side, side)
    place = tile_pos.reshape(slots, 2)
    span = range(groups)

    def from_row_line(turn):
        return [
            (line * groups + j, (j - turn) % groups * groups + line) for line in span for j in span
        ]

    def around(size, turn):
        return [(j, (j + turn) % size) for j in range(size)]

    col_pieces = [lax.ppermute(samples, grid_axes, from_row_line(turn)) for turn in span]
    row_pieces = [samples] + [
        lax.ppermute(samples, line_axes, around(groups, turn)) for turn in span[1:]
    ]
    high, low = split_tiles(tiles)
    kept, sent = partial_image(place, tile_count, samples, diag_tiles, high, low, col_pieces)
    chip = kept + lax.ppermute(sent, "rep", around(2, 1))
    image = chip
    for turn in range(1, cols):
        image = image + lax.ppermute(chip, "col", around(cols, turn))

    def to_row(turn):
        return [
            (line * groups + x * 2 + r, ((r + turn) % 2 * cols + x) * groups + line)
            for line in span
            for x in range(cols)
            for r in range(2)
        ]

    first, second = [lax.ppermute(image, grid_axes, to_row(turn)) for turn in range(2)]
    other = lax.ppermute(image, "rep", around(2, 1))
    panels = early_panels(image, other, row_pieces, col_pieces)
    new_diag = update_diag(samples, image, diag_tiles)
    new_slots = update_slots(place, tile_count, *panels, first, second, tiles)
    return new_slots.reshape(omega_slots.shape), new_diag


def solution(mesh):
    placed = (
        P("parts", ("row", "col", "rep")),
        P(("parts", "row", "col", "rep"), None, None),
        P(("parts", "row"), ("col", "rep"), None, None, None),
        P(("parts", "row"), ("col", "rep"), None, None),
        P(("parts", "row"), ("col", "rep")),
    )
    return jax.shard_map(
        on_device,
        mesh=mesh,
        in_specs=placed,
        out_specs=(
            P(("parts", "row"), ("col", "rep"), None, None, None),
            P(("parts", "row", "col", "rep"), None, None),
        ),
        check_vma=False,
    )
```

time: 145 us -> 57.7 us (0.40)
  the two profiles are of different devices: /device:TPU:6 before, /device:TPU:0 now
where the time goes in v1:
time: 57.7 us
  starting transfers between devices  18.8 us (33%)
  Pallas kernels  17.1 us (30%)
  waiting for transfers between devices  15.2 us (26%)
  local copies, waits for them, and re-layouts  5.01 us (9%)
  between operations  1.46 us (3%)
    ppermute x4, starting transfers between devices, on_device(): lax.ppermute(samples, grid_axes, from_row_line(turn))  10.3 us
    ppermute x1, waiting for transfers between devices, on_device(): image = image + lax.ppermute(chip, 'col', around(cols, turn))  6.95 us
    ppermute x3, waiting for transfers between devices, on_device(): lax.ppermute(samples, line_axes, around(groups, turn))  6.84 us
    pallas_call x1, Pallas kernels, split_tiles(): pl.pallas_call(split_kernel, grid=(slots,), out_shape=(shape, shape), in_...  5.64 us
    ppermute x2, starting transfers between devices, on_device(): lax.ppermute(image, grid_axes, to_row(turn))  5.12 us
    pallas_call x1, Pallas kernels, update_slots(): pl.pallas_call(functools.partial(slots_kernel, groups), grid=(tiles.shape...  4.95 us
    unnamed x22, local copies, waits for them, and re-layouts  4.93 us
    pallas_call x1, Pallas kernels, partial_image(): pl.pallas_call(functools.partial(partial_kernel, groups), out_shape=(shap...  2.76 us
  transfers between devices with their start and end apart: 12, of which 4 were waited for; matrix products, arithmetic and copies ran while one was open for 0% of the time, Pallas kernels for 16%

profile of v1, /device:TPU:0, one launch (start us, length us, event | category | flops | bytes accessed | tf_op | source)
XLA Modules:
  0.0 57.7 jit_solution(17463259354927509272)
XLA Ops:
  0.6 0.0 copy-start.6
  0.7 0.0 copy-start.3
  0.7 1.7 %collective-permute-start = (f32[96,256]{1,0:T(8,128)}, f32[96,256]{1,0:T(8,128)S(1)}, u32[]{:S(2)}, u32[]{:S(2)}) collective-permute-start(f32[96,256]{1,0:T(8,128)} %samples.3), channel_id=1, source_target_pairs={{0,0},{1,4},{2,8},{3,12},{4,1},{5,5},{6,9},{7,13},{8,2},{9,6},{10,... | collective-permute-start | bytes 294920 | tf_op jit(solution)/shard_map/ppermute | solution.py:231
  2.3 6.1 %collective-permute-start.1 = (f32[96,256]{1,0:T(8,128)}, f32[96,256]{1,0:T(8,128)S(1)}, u32[]{:S(2)}, u32[]{:S(2)}) collective-permute-start(f32[96,256]{1,0:T(8,128)} %samples.3), channel_id=1, source_target_pairs={{0,12},{1,0},{2,4},{3,8},{4,13},{5,1},{6,5},{7,9},{8,14},{9,2},{10... | collective-permute-start | bytes 294920 | tf_op jit(solution)/shard_map/ppermute | solution.py:231
  8.4 0.9 %collective-permute-start.2 = (f32[96,256]{1,0:T(8,128)}, f32[96,256]{1,0:T(8,128)S(1)}, u32[]{:S(2)}, u32[]{:S(2)}) collective-permute-start(f32[96,256]{1,0:T(8,128)} %samples.3), channel_id=1, source_target_pairs={{0,8},{1,12},{2,0},{3,4},{4,9},{5,13},{6,1},{7,5},{8,10},{9,14},{1... | collective-permute-start | bytes 294920 | tf_op jit(solution)/shard_map/ppermute | solution.py:231
  9.3 1.6 %collective-permute-start.3 = (f32[96,256]{1,0:T(8,128)}, f32[96,256]{1,0:T(8,128)S(1)}, u32[]{:S(2)}, u32[]{:S(2)}) collective-permute-start(f32[96,256]{1,0:T(8,128)} %samples.3), channel_id=1, source_target_pairs={{0,4},{1,8},{2,12},{3,0},{4,5},{5,9},{6,13},{7,1},{8,6},{9,10},{10... | collective-permute-start | bytes 294920 | tf_op jit(solution)/shard_map/ppermute | solution.py:231
  10.9 5.6 %split_tiles.1 = (bf16[8,256,256]{2,1,0:T(8,128)(2,1)}, bf16[8,256,256]{2,1,0:T(8,128)(2,1)}) custom-call(f32[8,256,256]{2,1,0:T(8,128)} %bitcast.3), custom_call_target="tpu_custom_call" | custom-call | tf_op jit(solution)/shard_map/split_tiles/pallas_call | solution.py:42
  16.6 0.1 copy.8.place
  17.3 0.0 collective-permute-done.1.refs_1_.refs_5_
  17.3 0.0 collective-permute-done.2.refs_2_.refs_6_
  17.4 0.0 copy-start.4
  17.4 1.2 %copy-done.4 = bf16[8,256,256]{2,1,0:T(8,128)(2,1)S(1)} copy-done((bf16[8,256,256]{2,1,0:T(8,128)(2,1)S(1)}, bf16[8,256,256]{2,1,0:T(8,128)(2,1)}, u32[]{:S(2)}) %copy-start.4) | copy-done | bytes 1048600
  18.6 1.2 %copy-done.5 = bf16[8,256,256]{2,1,0:T(8,128)(2,1)S(1)} copy-done((bf16[8,256,256]{2,1,0:T(8,128)(2,1)S(1)}, bf16[8,256,256]{2,1,0:T(8,128)(2,1)}, u32[]{:S(2)}) %copy-start.5) | copy-done | bytes 1048600
  19.8 2.8 %partial_image.1 = (f32[2,96,256]{2,1,0:T(8,128)S(1)}, f32[2,96,256]{2,1,0:T(8,128)S(1)}) custom-call(s32[8,2]{1,0:T(8,128)S(1)} %copy.8.place, s32[1,1]{1,0:T(1,128)S(6)} %copy.9.count, f32[96,256]{1,0:T(8,128)S(1)} %copy-done.6, f32[1,256,256]{2,1,0:T(8,128)S(1)} %copy-done.3, bf16[8,256,256]{2,1,0:T(8,128)(2,1)S(1)} %copy-done.4, ...), custom_call_target="tpu_custom_call" | custom-call | tf_op jit(solution)/shard_map/partial_image/pallas_call | solution.py:90
  22.6 0.0 copy-start
  22.6 0.1 collective-permute-start.4
  22.7 1.4 %collective-permute-done.4 = f32[2,96,256]{2,1,0:T(8,128)S(1)} collective-permute-done((f32[2,96,256]{2,1,0:T(8,128)S(1)}, f32[2,96,256]{2,1,0:T(8,128)S(1)}, u32[]{:S(2)}, u32[]{:S(2)}) %collective-permute-start.4) | collective-permute-done | bytes 196640 | tf_op jit(solution)/shard_map/ppermute | solution.py:237
  24.1 0.9 %collective-permute-start.5 = (f32[2,96,256]{2,1,0:T(8,128)S(1)}, f32[2,96,256]{2,1,0:T(8,128)S(1)}, u32[]{:S(2)}, u32[]{:S(2)}) collective-permute-start(f32[2,96,256]{2,1,0:T(8,128)S(1)} %add.6), channel_id=1, source_target_pairs={{0,2},{2,0},{1,3},{3,1},{4,6},{6,4},{5,7},{7,5},{8,10},{10,8},{9,1... | collective-permute-start | bytes 589832 | tf_op jit(solution)/shard_map/ppermute | solution.py:240
  25.0 7.0 %collective-permute-done.5 = f32[2,96,256]{2,1,0:T(8,128)S(1)} collective-permute-done((f32[2,96,256]{2,1,0:T(8,128)S(1)}, f32[2,96,256]{2,1,0:T(8,128)S(1)}, u32[]{:S(2)}, u32[]{:S(2)}) %collective-permute-start.5) | collective-permute-done | bytes 196640 | tf_op jit(solution)/shard_map/ppermute | solution.py:240
  32.0 0.0 copy-start.1
  32.0 0.1 collective-permute-start.6
  32.1 0.7 %collective-permute-start.10 = (f32[2,96,256]{2,1,0:T(8,128)S(1)}, f32[2,96,256]{2,1,0:T(8,128)S(1)}, u32[]{:S(2)}, u32[]{:S(2)}) collective-permute-start(f32[2,96,256]{2,1,0:T(8,128)S(1)} %add.7.own_image.image), channel_id=1, source_target_pairs={{0,0},{1,8},{2,4},{3,12},{4,1},{5,9},{6,5},{7,13},{8,2},{9,10},{10... | collective-permute-start | bytes 589832 | tf_op jit(solution)/shard_map/ppermute | solution.py:250
  32.7 4.4 %collective-permute-start.11 = (f32[2,96,256]{2,1,0:T(8,128)S(1)}, f32[2,96,256]{2,1,0:T(8,128)S(1)}, u32[]{:S(2)}, u32[]{:S(2)}) collective-permute-start(f32[2,96,256]{2,1,0:T(8,128)S(1)} %add.7.own_image.image), channel_id=1, source_target_pairs={{0,8},{1,0},{2,12},{3,4},{4,9},{5,1},{6,13},{7,5},{8,10},{9,2},{10... | collective-permute-start | bytes 589832 | tf_op jit(solution)/shard_map/ppermute | solution.py:250
  37.2 2.5 %collective-permute-start.8 = (f32[96,256]{1,0:T(8,128)S(1)}, f32[96,256]{1,0:T(8,128)}, u32[]{:S(2)}, u32[]{:S(2)}) collective-permute-start(f32[96,256]{1,0:T(8,128)S(1)} %copy-done.6), channel_id=1, source_target_pairs={{0,2},{1,3},{2,0},{3,1},{4,6},{5,7},{6,4},{7,5},{8,10},{9,11},{10,... | collective-permute-start | bytes 294920 | tf_op jit(solution)/shard_map/ppermute | solution.py:233
  39.6 0.6 %copy-done.8 = f32[96,256]{1,0:T(8,128)} copy-done((f32[96,256]{1,0:T(8,128)}, f32[96,256]{1,0:T(8,128)S(1)}, u32[]{:S(2)}) %copy-start.8) | copy-done | bytes 98328
  40.3 2.2 %update_diag.1 = f32[1,256,256]{2,1,0:T(8,128)} custom-call(f32[96,256]{1,0:T(8,128)} %samples.3, f32[2,96,256]{2,1,0:T(8,128)} %copy-done.1, f32[1,256,256]{2,1,0:T(8,128)} %tiles.1), custom_call_target="tpu_custom_call" | custom-call | tf_op jit(solution)/shard_map/update_diag/pallas_call | solution.py:206
  42.5 5.8 %collective-permute-done.8.refs_2_ = f32[96,256]{1,0:T(8,128)} collective-permute-done((f32[96,256]{1,0:T(8,128)S(1)}, f32[96,256]{1,0:T(8,128)}, u32[]{:S(2)}, u32[]{:S(2)}) %collective-permute-start.8) | collective-permute-done | bytes 98336 | tf_op jit(solution)/shard_map/ppermute | solution.py:233
  48.3 1.1 %collective-permute-done.9.refs_3_ = f32[96,256]{1,0:T(8,128)} collective-permute-done((f32[96,256]{1,0:T(8,128)S(1)}, f32[96,256]{1,0:T(8,128)}, u32[]{:S(2)}, u32[]{:S(2)}) %collective-permute-start.9) | collective-permute-done | bytes 98336 | tf_op jit(solution)/shard_map/ppermute | solution.py:233
  49.3 0.9 %copy-done.2 = f32[2,96,256]{2,1,0:T(8,128)S(1)} copy-done((f32[2,96,256]{2,1,0:T(8,128)S(1)}, f32[2,96,256]{2,1,0:T(8,128)}, u32[]{:S(2)}) %copy-start.2) | copy-done | bytes 196632
  50.3 0.9 %copy-done.9 = f32[96,256]{1,0:T(8,128)S(1)} copy-done((f32[96,256]{1,0:T(8,128)S(1)}, f32[96,256]{1,0:T(8,128)}, u32[]{:S(2)}) %copy-start.9) | copy-done | bytes 98328
  51.1 1.6 %early_panels.1 = (bf16[4,256,192]{2,1,0:T(8,128)(2,1)S(1)}, bf16[4,256,192]{2,1,0:T(8,128)(2,1)S(1)}, bf16[4,96,256]{2,1,0:T(8,128)(2,1)S(1)}, bf16[4,96,256]{2,1,0:T(8,128)(2,1)S(1)}) custom-call(f32[2,96,256]{2,1,0:T(8,128)S(1)} %copy-done.2, f32[2,96,256]{2,1,0:T(8,128)S(1)} %collective-permute-done.6.other_image, f32[96,256]{1,0:T(8,128)S(1)} %copy-done.7, ...), custom_call_target="tpu_custom_call" | custom-call | tf_op jit(solution)/shard_map/early_panels/pallas_call | solution.py:129
  52.7 4.9 %update_slots.1 = f32[8,256,256]{2,1,0:T(8,128)} custom-call(s32[8,2]{1,0:T(8,128)S(1)} %copy.8.place, s32[1,1]{1,0:T(1,128)S(6)} %copy.9.count, bf16[4,256,192]{2,1,0:T(8,128)(2,1)S(1)} %get-tuple-element.14.left_high, bf16[4,256,192]{2,1,0:T(8,128)(2,1)S(1)} %get-tuple-element.15.left_low, bf16[4,96,256]{2,1,0:T(8,128)(2,1)S(1)} %get-tuple-element.16.x_high, ...), custom_call_target="tpu_custom_call" | custom-call | tf_op jit(solution)/shard_map/update_slots/pallas_call | solution.py:176
  (22 shorter events, 0.1 us)
Async XLA Ops:
  0.6 16.7 %copy-start.6 = (f32[96,256]{1,0:T(8,128)S(1)}, f32[96,256]{1,0:T(8,128)}, u32[]{:S(2)}) copy-start(f32[96,256]{1,0:T(8,128)} %samples.3) | copy-start | bytes 294916
  0.6 15.9 %copy-start.10 = (s32[1,1,8,2]{2,3,1,0:T(2,128)S(1)}, s32[1,1,8,2]{2,3,1,0:T(2,128)}, u32[]{:S(2)}) copy-start(s32[1,1,8,2]{2,3,1,0:T(2,128)} %param.8) | copy-start | bytes 196
  0.7 16.7 %copy-start.3 = (f32[1,256,256]{2,1,0:T(8,128)S(1)}, f32[1,256,256]{2,1,0:T(8,128)}, u32[]{:S(2)}) copy-start(f32[1,256,256]{2,1,0:T(8,128)} %tiles.1) | copy-start | bytes 786436
  0.7 16.6 %collective-permute-start = (f32[96,256]{1,0:T(8,128)}, f32[96,256]{1,0:T(8,128)S(1)}, u32[]{:S(2)}, u32[]{:S(2)}) collective-permute-start(f32[96,256]{1,0:T(8,128)} %samples.3), channel_id=1, source_target_pairs={{0,0},{1,4},{2,8},{3,12},{4,1},{5,5},{6,9},{7,13},{8,2},{9,6},{10,... | collective-permute-start | bytes 294920 | tf_op jit(solution)/shard_map/ppermute | solution.py:231
  2.3 15.0 %collective-permute-start.1 = (f32[96,256]{1,0:T(8,128)}, f32[96,256]{1,0:T(8,128)S(1)}, u32[]{:S(2)}, u32[]{:S(2)}) collective-permute-start(f32[96,256]{1,0:T(8,128)} %samples.3), channel_id=1, source_target_pairs={{0,12},{1,0},{2,4},{3,8},{4,13},{5,1},{6,5},{7,9},{8,14},{9,2},{10... | collective-permute-start | bytes 294920 | tf_op jit(solution)/shard_map/ppermute | solution.py:231
  8.4 8.9 %collective-permute-start.2 = (f32[96,256]{1,0:T(8,128)}, f32[96,256]{1,0:T(8,128)S(1)}, u32[]{:S(2)}, u32[]{:S(2)}) collective-permute-start(f32[96,256]{1,0:T(8,128)} %samples.3), channel_id=1, source_target_pairs={{0,8},{1,12},{2,0},{3,4},{4,9},{5,13},{6,1},{7,5},{8,10},{9,14},{1... | collective-permute-start | bytes 294920 | tf_op jit(solution)/shard_map/ppermute | solution.py:231
  9.3 8.0 %collective-permute-start.3 = (f32[96,256]{1,0:T(8,128)}, f32[96,256]{1,0:T(8,128)S(1)}, u32[]{:S(2)}, u32[]{:S(2)}) collective-permute-start(f32[96,256]{1,0:T(8,128)} %samples.3), channel_id=1, source_target_pairs={{0,4},{1,8},{2,12},{3,0},{4,5},{5,9},{6,13},{7,1},{8,6},{9,10},{10... | collective-permute-start | bytes 294920 | tf_op jit(solution)/shard_map/ppermute | solution.py:231
  17.4 1.2 %copy-start.4 = (bf16[8,256,256]{2,1,0:T(8,128)(2,1)S(1)}, bf16[8,256,256]{2,1,0:T(8,128)(2,1)}, u32[]{:S(2)}) copy-start(bf16[8,256,256]{2,1,0:T(8,128)(2,1)} %get-tuple-element.10.high) | copy-start | bytes 3145732
  18.6 1.2 %copy-start.5 = (bf16[8,256,256]{2,1,0:T(8,128)(2,1)S(1)}, bf16[8,256,256]{2,1,0:T(8,128)(2,1)}, u32[]{:S(2)}) copy-start(bf16[8,256,256]{2,1,0:T(8,128)(2,1)} %get-tuple-element.11.low) | copy-start | bytes 3145732
  19.8 29.5 %copy-start.7 = (f32[96,256]{1,0:T(8,128)S(1)}, f32[96,256]{1,0:T(8,128)}, u32[]{:S(2)}) copy-start(f32[96,256]{1,0:T(8,128)} %samples.3) | copy-start | bytes 294916
  22.6 30.2 %copy-start = (f32[1,1,8,256,256]{4,3,2,1,0:T(8,128)S(1)}, f32[1,1,8,256,256]{4,3,2,1,0:T(8,128)}, u32[]{:S(2)}) copy-start(f32[1,1,8,256,256]{4,3,2,1,0:T(8,128)} %param.7) | copy-start | bytes 6291460
  22.6 1.5 %collective-permute-start.4 = (f32[2,96,256]{2,1,0:T(8,128)S(1)}, f32[2,96,256]{2,1,0:T(8,128)S(1)}, u32[]{:S(2)}, u32[]{:S(2)}) collective-permute-start(f32[2,96,256]{2,1,0:T(8,128)S(1)} %get-tuple-element.13), channel_id=1, source_target_pairs={{0,1},{1,0},{2,3},{3,2},{4,5},{5,4},{6,7},{7,6},{8,9},{9,8},{10,11... | collective-permute-start | bytes 589832 | tf_op jit(solution)/shard_map/ppermute | solution.py:237
  24.1 7.8 %collective-permute-start.5 = (f32[2,96,256]{2,1,0:T(8,128)S(1)}, f32[2,96,256]{2,1,0:T(8,128)S(1)}, u32[]{:S(2)}, u32[]{:S(2)}) collective-permute-start(f32[2,96,256]{2,1,0:T(8,128)S(1)} %add.6), channel_id=1, source_target_pairs={{0,2},{2,0},{1,3},{3,1},{4,6},{6,4},{5,7},{7,5},{8,10},{10,8},{9,1... | collective-permute-start | bytes 589832 | tf_op jit(solution)/shard_map/ppermute | solution.py:240
  25.0 14.7 %collective-permute-start.7 = (f32[96,256]{1,0:T(8,128)S(1)}, f32[96,256]{1,0:T(8,128)S(1)}, u32[]{:S(2)}, u32[]{:S(2)}) collective-permute-start(f32[96,256]{1,0:T(8,128)S(1)} %copy-done.6), channel_id=1, source_target_pairs={{0,1},{1,2},{2,3},{3,0},{4,5},{5,6},{6,7},{7,4},{8,9},{9,10},{10,1... | collective-permute-start | bytes 294920 | tf_op jit(solution)/shard_map/ppermute | solution.py:233
  32.0 8.3 %copy-start.1 = (f32[2,96,256]{2,1,0:T(8,128)}, f32[2,96,256]{2,1,0:T(8,128)S(1)}, u32[]{:S(2)}) copy-start(f32[2,96,256]{2,1,0:T(8,128)S(1)} %add.7.own_image.image) | copy-start | bytes 589828
  32.0 17.3 %collective-permute-start.6 = (f32[2,96,256]{2,1,0:T(8,128)S(1)}, f32[2,96,256]{2,1,0:T(8,128)S(1)}, u32[]{:S(2)}, u32[]{:S(2)}) collective-permute-start(f32[2,96,256]{2,1,0:T(8,128)S(1)} %add.7.own_image.image), channel_id=1, source_target_pairs={{0,1},{1,0},{2,3},{3,2},{4,5},{5,4},{6,7},{7,6},{8,9},{9,8},{10,11... | collective-permute-start | bytes 589832 | tf_op jit(solution)/shard_map/ppermute | solution.py:251
  32.1 20.6 %collective-permute-start.10 = (f32[2,96,256]{2,1,0:T(8,128)S(1)}, f32[2,96,256]{2,1,0:T(8,128)S(1)}, u32[]{:S(2)}, u32[]{:S(2)}) collective-permute-start(f32[2,96,256]{2,1,0:T(8,128)S(1)} %add.7.own_image.image), channel_id=1, source_target_pairs={{0,0},{1,8},{2,4},{3,12},{4,1},{5,9},{6,5},{7,13},{8,2},{9,10},{10... | collective-permute-start | bytes 589832 | tf_op jit(solution)/shard_map/ppermute | solution.py:250
  32.7 20.0 %collective-permute-start.11 = (f32[2,96,256]{2,1,0:T(8,128)S(1)}, f32[2,96,256]{2,1,0:T(8,128)S(1)}, u32[]{:S(2)}, u32[]{:S(2)}) collective-permute-start(f32[2,96,256]{2,1,0:T(8,128)S(1)} %add.7.own_image.image), channel_id=1, source_target_pairs={{0,8},{1,0},{2,12},{3,4},{4,9},{5,1},{6,13},{7,5},{8,10},{9,2},{10... | collective-permute-start | bytes 589832 | tf_op jit(solution)/shard_map/ppermute | solution.py:250
  37.2 11.1 %collective-permute-start.8 = (f32[96,256]{1,0:T(8,128)S(1)}, f32[96,256]{1,0:T(8,128)}, u32[]{:S(2)}, u32[]{:S(2)}) collective-permute-start(f32[96,256]{1,0:T(8,128)S(1)} %copy-done.6), channel_id=1, source_target_pairs={{0,2},{1,3},{2,0},{3,1},{4,6},{5,7},{6,4},{7,5},{8,10},{9,11},{10,... | collective-permute-start | bytes 294920 | tf_op jit(solution)/shard_map/ppermute | solution.py:233
  39.6 0.6 %copy-start.8 = (f32[96,256]{1,0:T(8,128)}, f32[96,256]{1,0:T(8,128)S(1)}, u32[]{:S(2)}) copy-start(f32[96,256]{1,0:T(8,128)S(1)} %collective-permute-done.7.refs_1_) | copy-start | bytes 294916
  40.3 9.0 %collective-permute-start.9 = (f32[96,256]{1,0:T(8,128)S(1)}, f32[96,256]{1,0:T(8,128)}, u32[]{:S(2)}, u32[]{:S(2)}) collective-permute-start(f32[96,256]{1,0:T(8,128)S(1)} %copy-done.6), channel_id=1, source_target_pairs={{0,3},{1,0},{2,1},{3,2},{4,7},{5,4},{6,5},{7,6},{8,11},{9,8},{10,9... | collective-permute-start | bytes 294920 | tf_op jit(solution)/shard_map/ppermute | solution.py:233
  49.3 0.9 %copy-start.2 = (f32[2,96,256]{2,1,0:T(8,128)S(1)}, f32[2,96,256]{2,1,0:T(8,128)}, u32[]{:S(2)}) copy-start(f32[2,96,256]{2,1,0:T(8,128)} %copy-done.1) | copy-start | bytes 589828
  50.2 0.9 %copy-start.9 = (f32[96,256]{1,0:T(8,128)S(1)}, f32[96,256]{1,0:T(8,128)}, u32[]{:S(2)}) copy-start(f32[96,256]{1,0:T(8,128)} %copy-done.8) | copy-start | bytes 294916

commit v2 on v1

v2 whole, which is shorter than its diff:
```python
import functools

import jax
import jax.numpy as jnp
from jax import lax
from jax.experimental import pallas as pl
from jax.experimental.pallas import tpu as pltpu
from jax.sharding import PartitionSpec as P

step_size = 1.0
penalty = 0.1
grid_axes = ("row", "col", "rep")
line_axes = ("col", "rep")
f32 = jnp.float32
bf16 = jnp.bfloat16
vmem = pl.BlockSpec(memory_space=pltpu.VMEM)
smem = pl.BlockSpec(memory_space=pltpu.SMEM)
room = pltpu.CompilerParams(vmem_limit_bytes=24 * 2**20)


def halves(values):
    high = values.astype(bf16)
    return high, (values - high.astype(f32)).astype(bf16)


def dot(left, right, dims):
    return lax.dot_general(left, right, (dims, ((), ())), preferred_element_type=f32)


def soft_limit(values):
    limit_value = step_size * penalty
    return values - jnp.clip(values, -limit_value, limit_value)


def prepare_kernel(groups, tiles, *refs):
    pieces = refs[:groups]
    high, low, left_high, left_low = refs[groups:]
    own = lax.axis_index("col") * 2 + lax.axis_index("rep")
    for slot in range(tiles.shape[0]):
        high[slot], low[slot] = halves(tiles[slot])
    for turn in range(groups):
        block = lax.rem(own + groups - turn, groups)
        left_high[block], left_low[block] = halves(pieces[turn][...].T)


def prepare(tiles, pieces):
    groups = len(pieces)
    rows, side = pieces[0].shape
    tile = jax.ShapeDtypeStruct(tiles.shape, bf16)
    left = jax.ShapeDtypeStruct((groups, side, rows), bf16)
    return pl.pallas_call(
        functools.partial(prepare_kernel, groups),
        out_shape=(tile, tile, left, left),
        in_specs=[vmem] * (1 + groups),
        out_specs=(vmem,) * 4,
        compiler_params=room,
        name="prepare",
    )(tiles, *pieces)


def partial_kernel(groups, place, count, samples, diag, high, low, *refs):
    pieces = refs[:groups]
    kept, sent, panel, total = refs[groups:]
    row = lax.axis_index("row")
    col = lax.axis_index("col")
    rep = lax.axis_index("rep")
    rows = samples.shape[0]
    for turn in range(groups):
        block = lax.rem(row + turn, groups)
        panel[block, :rows], panel[block, rows:] = halves(pieces[turn][...])
    total[...] = jnp.zeros_like(total)

    def term(x_high, both, w_high, w_low, dims):
        wide = dot(both, w_high, dims)
        return wide[:rows] + wide[rows:] + dot(x_high, w_low, dims)

    own_high, own_low = halves(samples[...])
    total[col * 2 + rep] = term(
        own_high, jnp.concatenate([own_high, own_low], axis=0), *halves(diag[0]), ((1,), (0,))
    )
    for slot in range(high.shape[0]):
        source = panel.at[place[1, slot]]
        value = term(source[:rows], source[...], high[slot], low[slot], ((1,), (1,)))
        total[place[0, slot]] += jnp.where(slot < count[0, 0], value, 0.0)
    for pair in range(groups // 2):
        kept[pair] = total[2 * pair + rep]
        sent[pair] = total[2 * pair + 1 - rep]


def partial_image(place, count, samples, diag, high, low, pieces):
    groups = len(pieces)
    rows, side = samples.shape
    shape = jax.ShapeDtypeStruct((groups // 2, rows, side), f32)
    panel = jax.ShapeDtypeStruct((groups, 2 * rows, side), bf16)
    return pl.pallas_call(
        functools.partial(partial_kernel, groups),
        out_shape=(shape, shape, panel),
        in_specs=[smem, smem] + [vmem] * (4 + groups),
        out_specs=(vmem, vmem, vmem),
        scratch_shapes=[pltpu.VMEM((groups, rows, side), f32)],
        compiler_params=room,
        name="partial_image",
    )(place, count, samples, diag, high, low, *pieces)


def left_kernel(own_image, other_image, x_high, x_low, high, low):
    rep = lax.axis_index("rep")
    rows = own_image.shape[1]
    half = high.shape[2] // 2
    for block in range(high.shape[0]):
        for out, part in ((high, x_high), (low, x_low)):
            out[block] = jnp.zeros(out.shape[1:], bf16)
            out[block, :, :rows] = part[block]
    for pair in range(own_image.shape[0]):
        for parity, image in ((rep, own_image), (1 - rep, other_image)):
            block = 2 * pair + parity
            image_high, image_low = halves(image[pair].T)
            high[block, :, half : half + rows] = image_high
            low[block, :, half : half + rows] = image_low


def left_panels(own_image, other_image, x_high, x_low):
    groups, side, rows = x_high.shape
    depth = 2 * -(-rows // 128) * 128
    left = jax.ShapeDtypeStruct((groups, side, depth), bf16)
    return pl.pallas_call(
        left_kernel,
        out_shape=(left, left),
        in_specs=[vmem] * 4,
        out_specs=(vmem,) * 2,
        compiler_params=room,
        name="left_panels",
    )(own_image, other_image, x_high, x_low)


def slots_kernel(
    place, count, left_high, left_low, panel, first, second, tiles, out, high, low, ready, sems
):
    groups = panel.shape[0]
    rows = panel.shape[1] // 2
    half = high.shape[1] // 2
    turned = lax.div(lax.axis_index("row"), groups // 2)
    for ref in (high, low):
        for start in (rows, half + rows):
            blank = jnp.zeros((groups, half - rows, high.shape[2]), bf16)
            ref[:, start : start + half - rows] = blank
    for pair in range(groups // 2):
        for turn, piece in enumerate((first, second)):
            block = 2 * pair + lax.rem(turned + turn, 2)
            high[block, :rows], low[block, :rows] = halves(piece[pair])
    high[:, half : half + rows] = panel[:, :rows]
    low[:, half : half + rows] = panel[:, rows:]
    dims = ((1,), (0,))
    copies = []
    for slot in range(tiles.shape[0]):
        left, right = place[0, slot], place[1, slot]
        gradient = dot(left_high[left], high[right], dims)
        gradient += dot(left_low[left], high[right], dims)
        gradient += dot(left_high[left], low[right], dims)
        value = soft_limit(tiles[slot] - gradient * (step_size / (2.0 * rows)))
        ready[slot] = jnp.where(slot < count[0, 0], value, 0.0)
        copies.append(pltpu.make_async_copy(ready.at[slot], out.at[slot], sems.at[slot]))
        copies[-1].start()
    for copy in copies:
        copy.wait()


def update_slots(place, count, left_high, left_low, panel, first, second, tiles):
    slots, side, _ = tiles.shape
    groups, _, depth = left_high.shape
    return pl.pallas_call(
        slots_kernel,
        out_shape=jax.ShapeDtypeStruct(tiles.shape, f32),
        in_specs=[smem, smem] + [vmem] * 6,
        out_specs=pl.BlockSpec(memory_space=pl.ANY),
        scratch_shapes=[
            pltpu.VMEM((groups, depth, side), bf16),
            pltpu.VMEM((groups, depth, side), bf16),
            pltpu.VMEM(tiles.shape, f32),
            pltpu.SemaphoreType.DMA((slots,)),
        ],
        compiler_params=room,
        name="update_slots",
    )(place, count, left_high, left_low, panel, first, second, tiles)


def diag_kernel(samples, image, tiles, out):
    rows, side = samples.shape
    own = image[lax.axis_index("col")]
    left_high, left_low = halves(samples[...].T)
    right_high, right_low = halves(own)
    dims = ((1,), (0,))
    one_side = dot(left_high, right_high, dims) + dot(left_low, right_high, dims)
    one_side += dot(left_high, right_low, dims)
    tile = tiles[0]
    row = lax.broadcasted_iota(jnp.int32, (side, side), 0)
    on_diag = row == lax.broadcasted_iota(jnp.int32, (side, side), 1)
    gradient = (one_side + one_side.T) * (1.0 / (2.0 * rows))
    shifted = tile - step_size * gradient
    inverse = step_size / jnp.where(on_diag, tile, 1.0)
    out[0] = jnp.where(on_diag, shifted + inverse, soft_limit(shifted))


def update_diag(samples, image, tiles):
    return pl.pallas_call(
        diag_kernel,
        out_shape=jax.ShapeDtypeStruct(tiles.shape, f32),
        in_specs=[vmem] * 3,
        out_specs=vmem,
        name="update_diag",
    )(samples, image, tiles)


def on_device(samples, diag_tiles, omega_slots, tile_pos, tile_count):
    groups = lax.axis_size(line_axes)
    cols = lax.axis_size("col")
    slots, side = omega_slots.shape[2], omega_slots.shape[3]
    tiles = omega_slots.reshape(slots, side, side)
    place = tile_pos.reshape(slots, 2).T
    span = range(groups)

    def from_row_line(turn):
        return [
            (line * groups + j, (j - turn) % groups * groups + line) for line in span for j in span
        ]

    def around(size, turn):
        return [(j, (j + turn) % size) for j in range(size)]

    col_pieces = [lax.ppermute(samples, grid_axes, from_row_line(turn)) for turn in span]
    row_pieces = [samples] + [
        lax.ppermute(samples, line_axes, around(groups, turn)) for turn in span[1:]
    ]
    high, low, *left_x = prepare(tiles, row_pieces)
    kept, sent, panel = partial_image(
        place, tile_count, samples, diag_tiles, high, low, col_pieces
    )
    chip = kept + lax.ppermute(sent, "rep", around(2, 1))
    image = chip
    for turn in range(1, cols):
        image = image + lax.ppermute(chip, "col", around(cols, turn))

    def to_row(turn):
        return [
            (line * groups + x * 2 + r, ((r + turn) % 2 * cols + x) * groups + line)
            for line in span
            for x in range(cols)
            for r in range(2)
        ]

    first, second = [lax.ppermute(image, grid_axes, to_row(turn)) for turn in range(2)]
    other = lax.ppermute(image, "rep", around(2, 1))
    left = left_panels(image, other, *left_x)
    new_diag = update_diag(samples, image, diag_tiles)
    new_slots = update_slots(place, tile_count, *left, panel, first, second, tiles)
    return new_slots.reshape(omega_slots.shape), new_diag


def solution(mesh):
    placed = (
        P("parts", ("row", "col", "rep")),
        P(("parts", "row", "col", "rep"), None, None),
        P(("parts", "row"), ("col", "rep"), None, None, None),
        P(("parts", "row"), ("col", "rep"), None, None),
        P(("parts", "row"), ("col", "rep")),
    )
    return jax.shard_map(
        on_device,
        mesh=mesh,
        in_specs=placed,
        out_specs=(
            P(("parts", "row"), ("col", "rep"), None, None, None),
            P(("parts", "row", "col", "rep"), None, None),
        ),
        check_vma=False,
    )
```

time: 57.7 us -> 51 us (0.88)
  the two profiles are of different devices: /device:TPU:0 before, /device:TPU:1 now
where the time goes in v2:
time: 51 us; the launch traced here: 50.7 us
  starting transfers between devices  21.5 us (42%)
  waiting for transfers between devices  16.4 us (32%)
  Pallas kernels  7.58 us (15%)
  local copies, waits for them, and re-layouts  3.7 us (7%)
  between operations  1.45 us (3%)
    ppermute x2, waiting for transfers between devices, on_device(): lax.ppermute(image, grid_axes, to_row(turn))  10.3 us
    ppermute x4, starting transfers between devices, on_device(): lax.ppermute(samples, grid_axes, from_row_line(turn))  7.75 us
    ppermute x1, waiting for transfers between devices, on_device(): image = image + lax.ppermute(chip, 'col', around(cols, turn))  4.97 us
    ppermute x2, starting transfers between devices, on_device(): lax.ppermute(image, grid_axes, to_row(turn))  3.87 us
    unnamed x14, local copies, waits for them, and re-layouts  3.7 us
    ppermute x1, starting transfers between devices, on_device(): image = image + lax.ppermute(chip, 'col', around(cols, turn))  3.47 us
    ppermute x3, starting transfers between devices, on_device(): lax.ppermute(samples, line_axes, around(groups, turn))  3.13 us
    pallas_call x1, Pallas kernels, update_slots(): pl.pallas_call(slots_kernel, out_shape=jax.ShapeDtypeStruct(tiles.shape,...  3.08 us
  transfers between devices with their start and end apart: 12, of which 4 were waited for; matrix products, arithmetic and copies ran while one was open for 0% of the time, Pallas kernels for 6%

profile of v2, /device:TPU:1, one launch (start us, length us, event | category | flops | bytes accessed | tf_op | source)
XLA Modules:
  0.0 50.7 jit_solution(11226879072556275743)
XLA Ops:
  0.6 2.7 %collective-permute-start = (f32[96,256]{1,0:T(8,128)}, f32[96,256]{1,0:T(8,128)S(1)}, u32[]{:S(2)}, u32[]{:S(2)}) collective-permute-start(f32[96,256]{1,0:T(8,128)} %samples.3), channel_id=1, source_target_pairs={{0,1},{1,2},{2,3},{3,0},{4,5},{5,6},{6,7},{7,4},{8,9},{9,10},{10,1... | collective-permute-start | bytes 294920 | tf_op jit(solution)/shard_map/ppermute | solution.py:232
  3.3 0.0 collective-permute-start.1
  3.3 0.5 collective-permute-start.2
  3.8 4.5 %collective-permute-start.3 = (f32[96,256]{1,0:T(8,128)}, f32[96,256]{1,0:T(8,128)S(1)}, u32[]{:S(2)}, u32[]{:S(2)}) collective-permute-start(f32[96,256]{1,0:T(8,128)} %samples.3), channel_id=1, source_target_pairs={{0,0},{1,4},{2,8},{3,12},{4,1},{5,5},{6,9},{7,13},{8,2},{9,6},{10,... | collective-permute-start | bytes 294920 | tf_op jit(solution)/shard_map/ppermute | solution.py:230
  8.2 0.1 collective-permute-start.4
  8.3 2.1 %collective-permute-start.5 = (f32[96,256]{1,0:T(8,128)}, f32[96,256]{1,0:T(8,128)S(1)}, u32[]{:S(2)}, u32[]{:S(2)}) collective-permute-start(f32[96,256]{1,0:T(8,128)} %samples.3), channel_id=1, source_target_pairs={{0,8},{1,12},{2,0},{3,4},{4,9},{5,13},{6,1},{7,5},{8,10},{9,14},{1... | collective-permute-start | bytes 294920 | tf_op jit(solution)/shard_map/ppermute | solution.py:230
  10.4 0.0 collective-permute-done.1.refs_2_
  10.4 1.1 %collective-permute-start.6 = (f32[96,256]{1,0:T(8,128)}, f32[96,256]{1,0:T(8,128)S(1)}, u32[]{:S(2)}, u32[]{:S(2)}) collective-permute-start(f32[96,256]{1,0:T(8,128)} %samples.3), channel_id=1, source_target_pairs={{0,4},{1,8},{2,12},{3,0},{4,5},{5,9},{6,13},{7,1},{8,6},{9,10},{10... | collective-permute-start | bytes 294920 | tf_op jit(solution)/shard_map/ppermute | solution.py:230
  12.2 0.0 copy-start
  12.2 1.6 %copy-done = f32[1,1,8,256,256]{4,3,2,1,0:T(8,128)S(1)} copy-done((f32[1,1,8,256,256]{4,3,2,1,0:T(8,128)S(1)}, f32[1,1,8,256,256]{4,3,2,1,0:T(8,128)}, u32[]{:S(2)}) %copy-start) | copy-done | bytes 2097176
  13.8 0.9 %copy-done.5 = f32[96,256]{1,0:T(8,128)S(1)} copy-done((f32[96,256]{1,0:T(8,128)S(1)}, f32[96,256]{1,0:T(8,128)}, u32[]{:S(2)}) %copy-start.5) | copy-done | bytes 98328
  14.7 0.6 %prepare.1 = (bf16[8,256,256]{2,1,0:T(8,128)(2,1)S(1)}, bf16[8,256,256]{2,1,0:T(8,128)(2,1)S(1)}, bf16[4,256,96]{2,1,0:T(8,128)(2,1)S(1)}, bf16[4,256,96]{2,1,0:T(8,128)(2,1)S(1)}) custom-call(f32[8,256,256]{2,1,0:T(8,128)S(1)} %bitcast.5, f32[96,256]{1,0:T(8,128)S(1)} %copy-done.5, f32[96,256]{1,0:T(8,128)S(1)} %collective-permute-done.refs_1_, ...), custom_call_target="tpu_custom_call" | custom-call | tf_op jit(solution)/shard_map/prepare/pallas_call | solution.py:51
  15.3 0.0 collective-permute-done.3.refs_0_
  15.3 0.0 collective-permute-done.5.refs_2_
  15.4 0.0 collective-permute-done.6.refs_3_
  15.4 0.3 copy-done.4
  15.6 1.4 %partial_image.1 = (f32[2,96,256]{2,1,0:T(8,128)S(1)}, f32[2,96,256]{2,1,0:T(8,128)S(1)}, bf16[4,192,256]{2,1,0:T(8,128)(2,1)S(1)}) custom-call(s32[2,8]{1,0:T(2,128)S(1)} %bitcast.7, s32[1,1]{1,0:T(1,128)S(6)} %copy.7.count, f32[96,256]{1,0:T(8,128)S(1)} %copy-done.5, f32[1,256,256]{2,1,0:T(8,128)S(1)} %copy-done.4, ...), custom_call_target="tpu_custom_call" | custom-call | tf_op jit(solution)/shard_map/partial_image/pallas_call | solution.py:95
  17.1 0.0 copy-start.1
  17.1 2.4 %collective-permute-start.7 = (f32[2,96,256]{2,1,0:T(8,128)S(1)}, f32[2,96,256]{2,1,0:T(8,128)S(1)}, u32[]{:S(2)}, u32[]{:S(2)}) collective-permute-start(f32[2,96,256]{2,1,0:T(8,128)S(1)} %get-tuple-element.14), channel_id=1, source_target_pairs={{0,1},{1,0},{2,3},{3,2},{4,5},{5,4},{6,7},{7,6},{8,9},{9,8},{10,11... | collective-permute-start | bytes 589832 | tf_op jit(solution)/shard_map/ppermute | solution.py:238
  19.4 1.1 %collective-permute-done.7 = f32[2,96,256]{2,1,0:T(8,128)S(1)} collective-permute-done((f32[2,96,256]{2,1,0:T(8,128)S(1)}, f32[2,96,256]{2,1,0:T(8,128)S(1)}, u32[]{:S(2)}, u32[]{:S(2)}) %collective-permute-start.7) | collective-permute-done | bytes 196640 | tf_op jit(solution)/shard_map/ppermute | solution.py:238
  20.5 3.5 %collective-permute-start.8 = (f32[2,96,256]{2,1,0:T(8,128)S(1)}, f32[2,96,256]{2,1,0:T(8,128)S(1)}, u32[]{:S(2)}, u32[]{:S(2)}) collective-permute-start(f32[2,96,256]{2,1,0:T(8,128)S(1)} %add.6), channel_id=1, source_target_pairs={{0,2},{2,0},{1,3},{3,1},{4,6},{6,4},{5,7},{7,5},{8,10},{10,8},{9,1... | collective-permute-start | bytes 589832 | tf_op jit(solution)/shard_map/ppermute | solution.py:241
  24.0 5.0 %collective-permute-done.8 = f32[2,96,256]{2,1,0:T(8,128)S(1)} collective-permute-done((f32[2,96,256]{2,1,0:T(8,128)S(1)}, f32[2,96,256]{2,1,0:T(8,128)S(1)}, u32[]{:S(2)}, u32[]{:S(2)}) %collective-permute-start.8) | collective-permute-done | bytes 196640 | tf_op jit(solution)/shard_map/ppermute | solution.py:241
  29.0 0.0 copy-start.2
  29.0 0.9 %collective-permute-start.9 = (f32[2,96,256]{2,1,0:T(8,128)S(1)}, f32[2,96,256]{2,1,0:T(8,128)S(1)}, u32[]{:S(2)}, u32[]{:S(2)}) collective-permute-start(f32[2,96,256]{2,1,0:T(8,128)S(1)} %add.7.own_image.image), channel_id=1, source_target_pairs={{0,1},{1,0},{2,3},{3,2},{4,5},{5,4},{6,7},{7,6},{8,9},{9,8},{10,11... | collective-permute-start | bytes 589832 | tf_op jit(solution)/shard_map/ppermute | solution.py:252
  30.0 3.8 %collective-permute-start.10 = (f32[2,96,256]{2,1,0:T(8,128)S(1)}, f32[2,96,256]{2,1,0:T(8,128)}, u32[]{:S(2)}, u32[]{:S(2)}) collective-permute-start(f32[2,96,256]{2,1,0:T(8,128)S(1)} %add.7.own_image.image), channel_id=1, source_target_pairs={{0,0},{1,8},{2,4},{3,12},{4,1},{5,9},{6,5},{7,13},{8,2},{9,10},{10... | collective-permute-start | bytes 589832 | tf_op jit(solution)/shard_map/ppermute | solution.py:251
  33.8 0.1 collective-permute-start.11
  33.9 2.2 %update_diag.1 = f32[1,256,256]{2,1,0:T(8,128)} custom-call(f32[96,256]{1,0:T(8,128)} %samples.3, f32[2,96,256]{2,1,0:T(8,128)} %copy-done.2, f32[1,256,256]{2,1,0:T(8,128)} %tiles.1), custom_call_target="tpu_custom_call" | custom-call | tf_op jit(solution)/shard_map/update_diag/pallas_call | solution.py:205
  36.1 0.9 %copy-done.3 = f32[2,96,256]{2,1,0:T(8,128)S(1)} copy-done((f32[2,96,256]{2,1,0:T(8,128)S(1)}, f32[2,96,256]{2,1,0:T(8,128)}, u32[]{:S(2)}) %copy-start.3) | copy-done | bytes 196632
  37.0 0.3 left_panels.1
  37.3 8.8 %collective-permute-done.10.first = f32[2,96,256]{2,1,0:T(8,128)} collective-permute-done((f32[2,96,256]{2,1,0:T(8,128)S(1)}, f32[2,96,256]{2,1,0:T(8,128)}, u32[]{:S(2)}, u32[]{:S(2)}) %collective-permute-start.10) | collective-permute-done | bytes 196640 | tf_op jit(solution)/shard_map/ppermute | solution.py:251
  46.1 1.5 %collective-permute-done.11.second = f32[2,96,256]{2,1,0:T(8,128)} collective-permute-done((f32[2,96,256]{2,1,0:T(8,128)S(1)}, f32[2,96,256]{2,1,0:T(8,128)}, u32[]{:S(2)}, u32[]{:S(2)}) %collective-permute-start.11) | collective-permute-done | bytes 196640 | tf_op jit(solution)/shard_map/ppermute | solution.py:251
  47.6 3.1 %update_slots.1 = f32[8,256,256]{2,1,0:T(8,128)} custom-call(s32[2,8]{1,0:T(2,128)S(1)} %bitcast.8, s32[1,1]{1,0:T(1,128)S(6)} %copy.7.count, bf16[4,256,256]{2,1,0:T(8,128)(2,1)S(1)} %get-tuple-element.17.left_high, bf16[4,256,256]{2,1,0:T(8,128)(2,1)S(1)} %get-tuple-element.18.left_low, bf16[4,192,256]{2,1,0:T(8,128)(2,1)S(1)} %get-tuple-element.19.panel, ...), custom_call_target="tpu_custom_call" | custom-call | tf_op jit(solution)/shard_map/update_slots/pallas_call | solution.py:171
  (13 shorter events, 0.1 us)
Async XLA Ops:
  0.6 14.7 %copy-start.6 = (s32[1,1,8,2]{2,3,1,0:T(2,128)S(1)}, s32[1,1,8,2]{2,3,1,0:T(2,128)}, u32[]{:S(2)}) copy-start(s32[1,1,8,2]{2,3,1,0:T(2,128)} %param.8) | copy-start | bytes 196
  0.6 7.7 %collective-permute-start = (f32[96,256]{1,0:T(8,128)}, f32[96,256]{1,0:T(8,128)S(1)}, u32[]{:S(2)}, u32[]{:S(2)}) collective-permute-start(f32[96,256]{1,0:T(8,128)} %samples.3), channel_id=1, source_target_pairs={{0,1},{1,2},{2,3},{3,0},{4,5},{5,6},{6,7},{7,4},{8,9},{9,10},{10,1... | collective-permute-start | bytes 294920 | tf_op jit(solution)/shard_map/ppermute | solution.py:232
  3.3 7.1 %collective-permute-start.1 = (f32[96,256]{1,0:T(8,128)}, f32[96,256]{1,0:T(8,128)S(1)}, u32[]{:S(2)}, u32[]{:S(2)}) collective-permute-start(f32[96,256]{1,0:T(8,128)} %samples.3), channel_id=1, source_target_pairs={{0,2},{1,3},{2,0},{3,1},{4,6},{5,7},{6,4},{7,5},{8,10},{9,11},{10,... | collective-permute-start | bytes 294920 | tf_op jit(solution)/shard_map/ppermute | solution.py:232
  3.3 8.9 %collective-permute-start.2 = (f32[96,256]{1,0:T(8,128)}, f32[96,256]{1,0:T(8,128)S(1)}, u32[]{:S(2)}, u32[]{:S(2)}) collective-permute-start(f32[96,256]{1,0:T(8,128)} %samples.3), channel_id=1, source_target_pairs={{0,3},{1,0},{2,1},{3,2},{4,7},{5,4},{6,5},{7,6},{8,11},{9,8},{10,9... | collective-permute-start | bytes 294920 | tf_op jit(solution)/shard_map/ppermute | solution.py:232
  3.8 11.6 %collective-permute-start.3 = (f32[96,256]{1,0:T(8,128)}, f32[96,256]{1,0:T(8,128)S(1)}, u32[]{:S(2)}, u32[]{:S(2)}) collective-permute-start(f32[96,256]{1,0:T(8,128)} %samples.3), channel_id=1, source_target_pairs={{0,0},{1,4},{2,8},{3,12},{4,1},{5,5},{6,9},{7,13},{8,2},{9,6},{10,... | collective-permute-start | bytes 294920 | tf_op jit(solution)/shard_map/ppermute | solution.py:230
  8.2 7.1 %collective-permute-start.4 = (f32[96,256]{1,0:T(8,128)}, f32[96,256]{1,0:T(8,128)S(1)}, u32[]{:S(2)}, u32[]{:S(2)}) collective-permute-start(f32[96,256]{1,0:T(8,128)} %samples.3), channel_id=1, source_target_pairs={{0,12},{1,0},{2,4},{3,8},{4,13},{5,1},{6,5},{7,9},{8,14},{9,2},{10... | collective-permute-start | bytes 294920 | tf_op jit(solution)/shard_map/ppermute | solution.py:230
  8.3 7.0 %collective-permute-start.5 = (f32[96,256]{1,0:T(8,128)}, f32[96,256]{1,0:T(8,128)S(1)}, u32[]{:S(2)}, u32[]{:S(2)}) collective-permute-start(f32[96,256]{1,0:T(8,128)} %samples.3), channel_id=1, source_target_pairs={{0,8},{1,12},{2,0},{3,4},{4,9},{5,13},{6,1},{7,5},{8,10},{9,14},{1... | collective-permute-start | bytes 294920 | tf_op jit(solution)/shard_map/ppermute | solution.py:230
  10.4 4.9 %collective-permute-start.6 = (f32[96,256]{1,0:T(8,128)}, f32[96,256]{1,0:T(8,128)S(1)}, u32[]{:S(2)}, u32[]{:S(2)}) collective-permute-start(f32[96,256]{1,0:T(8,128)} %samples.3), channel_id=1, source_target_pairs={{0,4},{1,8},{2,12},{3,0},{4,5},{5,9},{6,13},{7,1},{8,6},{9,10},{10... | collective-permute-start | bytes 294920 | tf_op jit(solution)/shard_map/ppermute | solution.py:230
  12.2 1.6 %copy-start = (f32[1,1,8,256,256]{4,3,2,1,0:T(8,128)S(1)}, f32[1,1,8,256,256]{4,3,2,1,0:T(8,128)}, u32[]{:S(2)}) copy-start(f32[1,1,8,256,256]{4,3,2,1,0:T(8,128)} %param.7) | copy-start | bytes 6291460
  13.8 0.9 %copy-start.5 = (f32[96,256]{1,0:T(8,128)S(1)}, f32[96,256]{1,0:T(8,128)}, u32[]{:S(2)}) copy-start(f32[96,256]{1,0:T(8,128)} %samples.3) | copy-start | bytes 294916
  14.7 0.9 %copy-start.4 = (f32[1,256,256]{2,1,0:T(8,128)S(1)}, f32[1,256,256]{2,1,0:T(8,128)}, u32[]{:S(2)}) copy-start(f32[1,256,256]{2,1,0:T(8,128)} %tiles.1) | copy-start | bytes 786436
  17.1 30.5 %copy-start.1 = (f32[1,1,8,256,256]{4,3,2,1,0:T(8,128)S(1)}, f32[1,1,8,256,256]{4,3,2,1,0:T(8,128)}, u32[]{:S(2)}) copy-start(f32[1,1,8,256,256]{4,3,2,1,0:T(8,128)} %param.7) | copy-start | bytes 6291460
  17.1 3.4 %collective-permute-start.7 = (f32[2,96,256]{2,1,0:T(8,128)S(1)}, f32[2,96,256]{2,1,0:T(8,128)S(1)}, u32[]{:S(2)}, u32[]{:S(2)}) collective-permute-start(f32[2,96,256]{2,1,0:T(8,128)S(1)} %get-tuple-element.14), channel_id=1, source_target_pairs={{0,1},{1,0},{2,3},{3,2},{4,5},{5,4},{6,7},{7,6},{8,9},{9,8},{10,11... | collective-permute-start | bytes 589832 | tf_op jit(solution)/shard_map/ppermute | solution.py:238
  20.5 8.4 %collective-permute-start.8 = (f32[2,96,256]{2,1,0:T(8,128)S(1)}, f32[2,96,256]{2,1,0:T(8,128)S(1)}, u32[]{:S(2)}, u32[]{:S(2)}) collective-permute-start(f32[2,96,256]{2,1,0:T(8,128)S(1)} %add.6), channel_id=1, source_target_pairs={{0,2},{2,0},{1,3},{3,1},{4,6},{6,4},{5,7},{7,5},{8,10},{10,8},{9,1... | collective-permute-start | bytes 589832 | tf_op jit(solution)/shard_map/ppermute | solution.py:241
  29.0 4.8 %copy-start.2 = (f32[2,96,256]{2,1,0:T(8,128)}, f32[2,96,256]{2,1,0:T(8,128)S(1)}, u32[]{:S(2)}) copy-start(f32[2,96,256]{2,1,0:T(8,128)S(1)} %add.7.own_image.image) | copy-start | bytes 589828
  29.0 7.0 %collective-permute-start.9 = (f32[2,96,256]{2,1,0:T(8,128)S(1)}, f32[2,96,256]{2,1,0:T(8,128)S(1)}, u32[]{:S(2)}, u32[]{:S(2)}) collective-permute-start(f32[2,96,256]{2,1,0:T(8,128)S(1)} %add.7.own_image.image), channel_id=1, source_target_pairs={{0,1},{1,0},{2,3},{3,2},{4,5},{5,4},{6,7},{7,6},{8,9},{9,8},{10,11... | collective-permute-start | bytes 589832 | tf_op jit(solution)/shard_map/ppermute | solution.py:252
  30.0 16.1 %collective-permute-start.10 = (f32[2,96,256]{2,1,0:T(8,128)S(1)}, f32[2,96,256]{2,1,0:T(8,128)}, u32[]{:S(2)}, u32[]{:S(2)}) collective-permute-start(f32[2,96,256]{2,1,0:T(8,128)S(1)} %add.7.own_image.image), channel_id=1, source_target_pairs={{0,0},{1,8},{2,4},{3,12},{4,1},{5,9},{6,5},{7,13},{8,2},{9,10},{10... | collective-permute-start | bytes 589832 | tf_op jit(solution)/shard_map/ppermute | solution.py:251
  33.8 13.8 %collective-permute-start.11 = (f32[2,96,256]{2,1,0:T(8,128)S(1)}, f32[2,96,256]{2,1,0:T(8,128)}, u32[]{:S(2)}, u32[]{:S(2)}) collective-permute-start(f32[2,96,256]{2,1,0:T(8,128)S(1)} %add.7.own_image.image), channel_id=1, source_target_pairs={{0,8},{1,0},{2,12},{3,4},{4,9},{5,1},{6,13},{7,5},{8,10},{9,2},{10... | collective-permute-start | bytes 589832 | tf_op jit(solution)/shard_map/ppermute | solution.py:251
  36.1 0.9 %copy-start.3 = (f32[2,96,256]{2,1,0:T(8,128)S(1)}, f32[2,96,256]{2,1,0:T(8,128)}, u32[]{:S(2)}) copy-start(f32[2,96,256]{2,1,0:T(8,128)} %copy-done.2) | copy-start | bytes 589828

commit v3 on v2

v3 whole, which is shorter than its diff:
```python
import functools

import jax
import jax.numpy as jnp
from jax import lax
from jax.experimental import pallas as pl
from jax.experimental.pallas import tpu as pltpu
from jax.sharding import PartitionSpec as P

step_size = 1.0
penalty = 0.1
grid_axes = ("row", "col", "rep")
line_axes = ("col", "rep")
f32 = jnp.float32
bf16 = jnp.bfloat16
vmem = pl.BlockSpec(memory_space=pltpu.VMEM)
smem = pl.BlockSpec(memory_space=pltpu.SMEM)
hbm = pl.BlockSpec(memory_space=pltpu.HBM)
room = pltpu.CompilerParams(vmem_limit_bytes=24 * 2**20)


def halves(values):
    high = values.astype(bf16)
    return high, (values - high.astype(f32)).astype(bf16)


def dot(left, right, dims):
    return lax.dot_general(left, right, (dims, ((), ())), preferred_element_type=f32)


def soft_limit(values):
    limit_value = step_size * penalty
    return values - jnp.clip(values, -limit_value, limit_value)


def prepare_kernel(samples, diag, tiles, own, own_diag, held, high, low, sems):
    slots = tiles.shape[0]
    copies = [
        pltpu.make_async_copy(tiles.at[slot], held.at[slot], sems.at[slot])
        for slot in range(slots)
    ]
    copies.append(pltpu.make_async_copy(samples, own, sems.at[slots]))
    copies.append(pltpu.make_async_copy(diag, own_diag, sems.at[slots + 1]))
    for copy in copies:
        copy.start()
    for slot in range(slots):
        copies[slot].wait()
        high[slot], low[slot] = halves(held[slot])
    copies[slots].wait()
    copies[slots + 1].wait()


def prepare(samples, diag, tiles):
    held = [jax.ShapeDtypeStruct(x.shape, f32) for x in (samples, diag, tiles)]
    half = jax.ShapeDtypeStruct(tiles.shape, bf16)
    return pl.pallas_call(
        prepare_kernel,
        out_shape=(*held, half, half),
        in_specs=[hbm] * 3,
        out_specs=(vmem,) * 5,
        scratch_shapes=[pltpu.SemaphoreType.DMA((tiles.shape[0] + 2,))],
        compiler_params=room,
        name="prepare",
    )(samples, diag, tiles)


def partial_kernel(groups, place, count, samples, diag, high, low, *refs):
    pieces = refs[:groups]
    beside = refs[groups:-4]
    kept, sent, panel, total = refs[-4:]
    row = lax.axis_index("row")
    col = lax.axis_index("col")
    rep = lax.axis_index("rep")
    rows = samples.shape[0]
    for turn in range(groups):
        block = lax.rem(row + turn, groups)
        panel[block, :rows], panel[block, rows:] = halves(pieces[turn][...])
    total[...] = jnp.zeros_like(total)

    def term(x_high, both, w_high, w_low, dims):
        wide = dot(both, w_high, dims)
        return wide[:rows] + wide[rows:] + dot(x_high, w_low, dims)

    own_high, own_low = halves(samples[...])
    total[col * 2 + rep] = term(
        own_high, jnp.concatenate([own_high, own_low], axis=0), *halves(diag[0]), ((1,), (0,))
    )
    for slot in range(high.shape[0]):
        source = panel.at[place[1, slot]]
        value = term(source[:rows], source[...], high[slot], low[slot], ((1,), (1,)))
        total[place[0, slot]] += jnp.where(slot < count[0, 0], value, 0.0)
    for pair in range(groups // 2):
        kept[pair] = total[2 * pair + rep]
        sent[pair] = total[2 * pair + 1 - rep]
    for turn, piece in enumerate((samples, *beside)):
        sent[groups // 2 + turn] = piece[...]


def partial_image(place, count, samples, diag, high, low, pieces, beside):
    groups = len(pieces)
    rows, side = samples.shape
    kept = jax.ShapeDtypeStruct((groups // 2, rows, side), f32)
    sent = jax.ShapeDtypeStruct((groups, rows, side), f32)
    panel = jax.ShapeDtypeStruct((groups, 2 * rows, side), bf16)
    return pl.pallas_call(
        functools.partial(partial_kernel, groups),
        out_shape=(kept, sent, panel),
        in_specs=[smem, smem] + [vmem] * (3 + groups + groups // 2),
        out_specs=(vmem, vmem, vmem),
        scratch_shapes=[pltpu.VMEM((groups, rows, side), f32)],
        compiler_params=room,
        name="partial_image",
    )(place, count, samples, diag, high, low, *pieces, *beside)


def middle_kernel(own_image, other_image, samples, diag, swapped, *refs):
    beside = refs[:-5]
    high, low, new_diag, shifted, sem = refs[-5:]
    pairs = own_image.shape[0]
    rep = lax.axis_index("rep")
    col = lax.axis_index("col")
    rows, side = samples.shape
    half = high.shape[2] // 2
    blank = jnp.zeros((side, half - rows), bf16)
    for turn, piece in enumerate((samples, *beside)):
        line = 2 * lax.rem(col + pairs - turn, pairs)
        for block, values in ((line + rep, piece[...]), (line + 1 - rep, swapped[pairs + turn])):
            for ref, part in zip((high, low), halves(values.T)):
                ref[block, :, :rows] = part
                ref[block, :, rows:half] = blank
                ref[block, :, half + rows :] = blank
    left_high, left_low = halves(samples[...].T)
    right_high, right_low = halves(own_image[col])
    dims = ((1,), (0,))
    one_side = dot(left_high, right_high, dims) + dot(left_low, right_high, dims)
    one_side += dot(left_high, right_low, dims)
    tile = diag[0]
    line = lax.broadcasted_iota(jnp.int32, (side, side), 0)
    on_diag = line == lax.broadcasted_iota(jnp.int32, (side, side), 1)
    gradient = (one_side + one_side.T) * (1.0 / (2.0 * rows))
    moved = tile - step_size * gradient
    inverse = step_size / jnp.where(on_diag, tile, 1.0)
    shifted[0] = jnp.where(on_diag, moved + inverse, soft_limit(moved))
    copy = pltpu.make_async_copy(shifted, new_diag, sem)
    copy.start()
    for pair in range(pairs):
        for parity, image in ((rep, own_image), (1 - rep, other_image)):
            block = 2 * pair + parity
            image_high, image_low = halves(image[pair].T)
            high[block, :, half : half + rows] = image_high
            low[block, :, half : half + rows] = image_low
    copy.wait()


def middle(own_image, other_image, samples, diag, swapped, beside):
    groups = swapped.shape[0]
    rows, side = samples.shape
    depth = 2 * -(-rows // 128) * 128
    left = jax.ShapeDtypeStruct((groups, side, depth), bf16)
    return pl.pallas_call(
        middle_kernel,
        out_shape=(left, left, jax.ShapeDtypeStruct(diag.shape, f32)),
        in_specs=[vmem] * (5 + len(beside)),
        out_specs=(vmem, vmem, hbm),
        scratch_shapes=[pltpu.VMEM(diag.shape, f32), pltpu.SemaphoreType.DMA],
        compiler_params=room,
        name="middle",
    )(own_image, other_image, samples, diag, swapped, *beside)


def slots_kernel(
    place, count, left_high, left_low, panel, first, second, tiles, out, high, low, ready, sems
):
    groups = panel.shape[0]
    rows = panel.shape[1] // 2
    half = high.shape[1] // 2
    parity = lax.rem(lax.axis_index("row"), 2)
    for ref in (high, low):
        for start in (rows, half + rows):
            blank = jnp.zeros((groups, half - rows, high.shape[2]), bf16)
            ref[:, start : start + half - rows] = blank
    for pair in range(groups // 2):
        for turn, piece in enumerate((first, second)):
            block = 2 * pair + (1 - parity if turn else parity)
            high[block, :rows], low[block, :rows] = halves(piece[pair])
    high[:, half : half + rows] = panel[:, :rows]
    low[:, half : half + rows] = panel[:, rows:]
    dims = ((1,), (0,))
    copies = []
    for slot in range(tiles.shape[0]):
        left, right = place[0, slot], place[1, slot]
        gradient = dot(left_high[left], high[right], dims)
        gradient += dot(left_low[left], high[right], dims)
        gradient += dot(left_high[left], low[right], dims)
        value = soft_limit(tiles[slot] - gradient * (step_size / (2.0 * rows)))
        ready[slot] = jnp.where(slot < count[0, 0], value, 0.0)
        copies.append(pltpu.make_async_copy(ready.at[slot], out.at[slot], sems.at[slot]))
        copies[-1].start()
    for copy in copies:
        copy.wait()


def update_slots(place, count, left_high, left_low, panel, first, second, tiles):
    slots, side, _ = tiles.shape
    groups, _, depth = left_high.shape
    return pl.pallas_call(
        slots_kernel,
        out_shape=jax.ShapeDtypeStruct(tiles.shape, f32),
        in_specs=[smem, smem] + [vmem] * 6,
        out_specs=hbm,
        scratch_shapes=[
            pltpu.VMEM((groups, depth, side), bf16),
            pltpu.VMEM((groups, depth, side), bf16),
            pltpu.VMEM(tiles.shape, f32),
            pltpu.SemaphoreType.DMA((slots,)),
        ],
        compiler_params=room,
        name="update_slots",
    )(place, count, left_high, left_low, panel, first, second, tiles)


def on_device(samples, diag_tiles, omega_slots, tile_pos, tile_count):
    groups = lax.axis_size(line_axes)
    cols = lax.axis_size("col")
    slots, side = omega_slots.shape[2], omega_slots.shape[3]
    tiles = omega_slots.reshape(slots, side, side)
    place = tile_pos.reshape(slots, 2).T
    span = range(groups)

    def from_row_line(turn):
        return [
            (line * groups + j, (j - turn) % groups * groups + line) for line in span for j in span
        ]

    def around(size, turn):
        return [(j, (j + turn) % size) for j in range(size)]

    col_pieces = [lax.ppermute(samples, grid_axes, from_row_line(turn)) for turn in span]
    beside = [lax.ppermute(samples, "col", around(cols, turn)) for turn in range(1, cols)]
    own, own_diag, held, high, low = prepare(samples, diag_tiles, tiles)
    kept, sent, panel = partial_image(
        place, tile_count, own, own_diag, high, low, col_pieces, beside
    )
    swapped = lax.ppermute(sent, "rep", around(2, 1))
    chip = kept + swapped[:cols]
    image = chip
    for turn in range(1, cols):
        image = image + lax.ppermute(chip, "col", around(cols, turn))

    def to_row(turn):
        return [
            (line * groups + j, (groups - 1 - j if turn else j) * groups + line)
            for line in span
            for j in span
        ]

    first, second = [lax.ppermute(image, grid_axes, to_row(turn)) for turn in range(2)]
    other = lax.ppermute(image, "rep", around(2, 1))
    left_high, left_low, new_diag = middle(
        image, other, own, own_diag, swapped, beside
    )
    new_slots = update_slots(
        place, tile_count, left_high, left_low, panel, first, second, held
    )
    return new_slots.reshape(omega_slots.shape), new_diag


def solution(mesh):
    placed = (
        P("parts", ("row", "col", "rep")),
        P(("parts", "row", "col", "rep"), None, None),
        P(("parts", "row"), ("col", "rep"), None, None, None),
        P(("parts", "row"), ("col", "rep"), None, None),
        P(("parts", "row"), ("col", "rep")),
    )
    return jax.shard_map(
        on_device,
        mesh=mesh,
        in_specs=placed,
        out_specs=(
            P(("parts", "row"), ("col", "rep"), None, None, None),
            P(("parts", "row", "col", "rep"), None, None),
        ),
        check_vma=False,
    )
```

time: 51 us -> 44.4 us (0.87)
  the two profiles are of different devices: /device:TPU:1 before, /device:TPU:6 now
where the time goes in v3:
time: 44.4 us; the launch traced here: 44.1 us
  starting transfers between devices  17.3 us (39%)
  waiting for transfers between devices  15.9 us (36%)
  Pallas kernels  5.99 us (13%)
  local copies, waits for them, and re-layouts  3.43 us (8%)
  between operations  1.44 us (3%)
    ppermute x4, starting transfers between devices, on_device(): lax.ppermute(samples, grid_axes, from_row_line(turn))  10.5 us
    ppermute x2, waiting for transfers between devices, on_device(): lax.ppermute(image, grid_axes, to_row(turn))  7.25 us
    ppermute x1, waiting for transfers between devices, on_device(): image = image + lax.ppermute(chip, 'col', around(cols, turn))  6.93 us
    ppermute x2, starting transfers between devices, on_device(): lax.ppermute(image, grid_axes, to_row(turn))  6.48 us
    unnamed x8, local copies, waits for them, and re-layouts  3.43 us
    pallas_call x1, Pallas kernels, update_slots(): pl.pallas_call(slots_kernel, out_shape=jax.ShapeDtypeStruct(tiles.shape,...  2.59 us
    ppermute x1, waiting for transfers between devices, on_device(): swapped = lax.ppermute(sent, 'rep', around(2, 1))  1.71 us
    pallas_call x1, Pallas kernels, partial_image(): pl.pallas_call(functools.partial(partial_kernel, groups), out_shape=(kept...  1.43 us
  transfers between devices with their start and end apart: 10, of which 4 were waited for; matrix products, arithmetic and copies ran while one was open for 0% of the time, Pallas kernels for 4%

profile of v3, /device:TPU:6, one launch (start us, length us, event | category | flops | bytes accessed | tf_op | source)
XLA Modules:
  0.0 44.1 jit_solution(4136254660847485439)
XLA Ops:
  0.6 0.0 copy-start.3
  0.6 0.6 %collective-permute-start.2 = (f32[96,256]{1,0:T(8,128)}, f32[96,256]{1,0:T(8,128)S(1)}, u32[]{:S(2)}, u32[]{:S(2)}) collective-permute-start(f32[96,256]{1,0:T(8,128)} %samples.1), channel_id=1, source_target_pairs={{0,8},{1,12},{2,0},{3,4},{4,9},{5,13},{6,1},{7,5},{8,10},{9,14},{1... | collective-permute-start | bytes 294920 | tf_op jit(solution)/shard_map/ppermute | solution.py:238
  1.2 2.0 %collective-permute-start.1 = (f32[96,256]{1,0:T(8,128)}, f32[96,256]{1,0:T(8,128)S(1)}, u32[]{:S(2)}, u32[]{:S(2)}) collective-permute-start(f32[96,256]{1,0:T(8,128)} %samples.1), channel_id=1, source_target_pairs={{0,12},{1,0},{2,4},{3,8},{4,13},{5,1},{6,5},{7,9},{8,14},{9,2},{10... | collective-permute-start | bytes 294920 | tf_op jit(solution)/shard_map/ppermute | solution.py:238
  3.3 4.5 %collective-permute-start = (f32[96,256]{1,0:T(8,128)}, f32[96,256]{1,0:T(8,128)S(1)}, u32[]{:S(2)}, u32[]{:S(2)}) collective-permute-start(f32[96,256]{1,0:T(8,128)} %samples.1), channel_id=1, source_target_pairs={{0,0},{1,4},{2,8},{3,12},{4,1},{5,5},{6,9},{7,13},{8,2},{9,6},{10,... | collective-permute-start | bytes 294920 | tf_op jit(solution)/shard_map/ppermute | solution.py:238
  7.7 0.1 collective-permute-start.4
  7.8 3.4 %collective-permute-start.3 = (f32[96,256]{1,0:T(8,128)}, f32[96,256]{1,0:T(8,128)S(1)}, u32[]{:S(2)}, u32[]{:S(2)}) collective-permute-start(f32[96,256]{1,0:T(8,128)} %samples.1), channel_id=1, source_target_pairs={{0,4},{1,8},{2,12},{3,0},{4,5},{5,9},{6,13},{7,1},{8,6},{9,10},{10... | collective-permute-start | bytes 294920 | tf_op jit(solution)/shard_map/ppermute | solution.py:238
  11.9 0.0 copy-start
  11.9 1.6 %copy-done = f32[1,1,8,256,256]{4,3,2,1,0:T(8,128)S(1)} copy-done((f32[1,1,8,256,256]{4,3,2,1,0:T(8,128)S(1)}, f32[1,1,8,256,256]{4,3,2,1,0:T(8,128)}, u32[]{:S(2)}) %copy-start) | copy-done | bytes 2097176
  13.5 0.0 copy-start.1
  13.5 0.9 %copy-done.1 = f32[1,256,256]{2,1,0:T(8,128)S(1)} copy-done((f32[1,256,256]{2,1,0:T(8,128)S(1)}, f32[1,256,256]{2,1,0:T(8,128)}, u32[]{:S(2)}) %copy-start.1) | copy-done | bytes 262168
  14.4 0.0 copy-start.2
  14.4 0.9 %copy-done.2 = f32[96,256]{1,0:T(8,128)S(1)} copy-done((f32[96,256]{1,0:T(8,128)S(1)}, f32[96,256]{1,0:T(8,128)}, u32[]{:S(2)}) %copy-start.2) | copy-done | bytes 98328
  15.3 0.7 %prepare.1 = (f32[96,256]{1,0:T(8,128)S(1)}, f32[1,256,256]{2,1,0:T(8,128)S(1)}, f32[8,256,256]{2,1,0:T(8,128)S(1)}, bf16[8,256,256]{2,1,0:T(8,128)(2,1)S(1)}, bf16[8,256,256]{2,1,0:T(8,128)(2,1)S(1)}) custom-call(f32[96,256]{1,0:T(8,128)S(1)} %copy-done.2, f32[1,256,256]{2,1,0:T(8,128)S(1)} %copy-done.1, f32[8,256,256]{2,1,0:T(8,128)S(1)} %bitcast.5), custom_call_target="tpu_custom_call" | custom-call | tf_op jit(solution)/shard_map/prepare/pallas_call | solution.py:56
  16.0 0.0 collective-permute-done.2.refs_2_
  16.1 0.0 collective-permute-done.1.refs_1_
  16.1 0.0 collective-permute-done.refs_0_
  16.1 0.0 collective-permute-done.4.refs_4_.refs_0_
  16.1 0.0 collective-permute-done.3.refs_3_
  16.1 0.0 copy-done.3
  16.1 1.4 %partial_image.1 = (f32[2,96,256]{2,1,0:T(8,128)S(1)}, f32[4,96,256]{2,1,0:T(8,128)S(1)}, bf16[4,192,256]{2,1,0:T(8,128)(2,1)S(1)}) custom-call(s32[2,8]{1,0:T(2,128)S(1)} %bitcast.6, s32[1,1]{1,0:T(1,128)S(6)} %copy.7.count, f32[96,256]{1,0:T(8,128)S(1)} %get-tuple-element.13.samples, f32[1,256,256]{2,1,0:T(8,128)S(1)} %get-tuple-element.14.diag, ...), custom_call_target="tpu_custom_call" | custom-call | tf_op jit(solution)/shard_map/partial_image/pallas_call | solution.py:105
  17.5 0.1 collective-permute-start.5
  17.6 1.7 %collective-permute-done.5.swapped = f32[4,96,256]{2,1,0:T(8,128)S(1)} collective-permute-done((f32[4,96,256]{2,1,0:T(8,128)S(1)}, f32[4,96,256]{2,1,0:T(8,128)S(1)}, u32[]{:S(2)}, u32[]{:S(2)}) %collective-permute-start.5) | collective-permute-done | bytes 393248 | tf_op jit(solution)/shard_map/ppermute | solution.py:244
  19.4 0.1 collective-permute-start.6
  19.4 6.9 %collective-permute-done.6 = f32[2,96,256]{2,1,0:T(8,128)S(1)} collective-permute-done((f32[2,96,256]{2,1,0:T(8,128)S(1)}, f32[2,96,256]{2,1,0:T(8,128)S(1)}, u32[]{:S(2)}, u32[]{:S(2)}) %collective-permute-start.6) | collective-permute-done | bytes 196640 | tf_op jit(solution)/shard_map/ppermute | solution.py:248
  26.4 0.1 collective-permute-start.7
  26.5 0.8 %collective-permute-start.9 = (f32[2,96,256]{2,1,0:T(8,128)S(1)}, f32[2,96,256]{2,1,0:T(8,128)S(1)}, u32[]{:S(2)}, u32[]{:S(2)}) collective-permute-start(f32[2,96,256]{2,1,0:T(8,128)S(1)} %add.7.own_image), channel_id=1, source_target_pairs={{0,12},{1,8},{2,4},{3,0},{4,13},{5,9},{6,5},{7,1},{8,14},{9,10},{1... | collective-permute-start | bytes 589832 | tf_op jit(solution)/shard_map/ppermute | solution.py:257
  27.3 5.7 %collective-permute-start.8 = (f32[2,96,256]{2,1,0:T(8,128)S(1)}, f32[2,96,256]{2,1,0:T(8,128)S(1)}, u32[]{:S(2)}, u32[]{:S(2)}) collective-permute-start(f32[2,96,256]{2,1,0:T(8,128)S(1)} %add.7.own_image), channel_id=1, source_target_pairs={{0,0},{1,4},{2,8},{3,12},{4,1},{5,5},{6,9},{7,13},{8,2},{9,6},{10,... | collective-permute-start | bytes 589832 | tf_op jit(solution)/shard_map/ppermute | solution.py:257
  33.0 0.0 collective-permute-done.7.other_image
  33.0 1.3 %middle.1 = (bf16[4,256,256]{2,1,0:T(8,128)(2,1)S(1)}, bf16[4,256,256]{2,1,0:T(8,128)(2,1)S(1)}, f32[1,256,256]{2,1,0:T(8,128)}) custom-call(f32[2,96,256]{2,1,0:T(8,128)S(1)} %add.7.own_image, f32[2,96,256]{2,1,0:T(8,128)S(1)} %collective-permute-done.7.other_image, f32[96,256]{1,0:T(8,128)S(1)} %get-tuple-element.13.samples, ...), custom_call_target="tpu_custom_call" | custom-call | tf_op jit(solution)/shard_map/middle/pallas_call | solution.py:160
  34.2 4.5 %collective-permute-done.9.second = f32[2,96,256]{2,1,0:T(8,128)S(1)} collective-permute-done((f32[2,96,256]{2,1,0:T(8,128)S(1)}, f32[2,96,256]{2,1,0:T(8,128)S(1)}, u32[]{:S(2)}, u32[]{:S(2)}) %collective-permute-start.9) | collective-permute-done | bytes 196640 | tf_op jit(solution)/shard_map/ppermute | solution.py:257
  38.8 2.7 %collective-permute-done.8.first = f32[2,96,256]{2,1,0:T(8,128)S(1)} collective-permute-done((f32[2,96,256]{2,1,0:T(8,128)S(1)}, f32[2,96,256]{2,1,0:T(8,128)S(1)}, u32[]{:S(2)}, u32[]{:S(2)}) %collective-permute-start.8) | collective-permute-done | bytes 196640 | tf_op jit(solution)/shard_map/ppermute | solution.py:257
  41.5 2.6 %update_slots.1 = f32[8,256,256]{2,1,0:T(8,128)} custom-call(s32[2,8]{1,0:T(2,128)S(1)} %bitcast.7, s32[1,1]{1,0:T(1,128)S(6)} %copy.7.count, bf16[4,256,256]{2,1,0:T(8,128)(2,1)S(1)} %get-tuple-element.19.left_high, bf16[4,256,256]{2,1,0:T(8,128)(2,1)S(1)} %get-tuple-element.20.left_low, bf16[4,192,256]{2,1,0:T(8,128)(2,1)S(1)} %get-tuple-element.21.panel, ...), custom_call_target="tpu_custom_call" | custom-call | tf_op jit(solution)/shard_map/update_slots/pallas_call | solution.py:206
  (2 shorter events, 0.1 us)
Async XLA Ops:
  0.6 15.5 %copy-start.3 = (s32[1,1,8,2]{2,3,1,0:T(2,128)S(1)}, s32[1,1,8,2]{2,3,1,0:T(2,128)}, u32[]{:S(2)}) copy-start(s32[1,1,8,2]{2,3,1,0:T(2,128)} %param.8) | copy-start | bytes 196
  0.6 15.4 %collective-permute-start.2 = (f32[96,256]{1,0:T(8,128)}, f32[96,256]{1,0:T(8,128)S(1)}, u32[]{:S(2)}, u32[]{:S(2)}) collective-permute-start(f32[96,256]{1,0:T(8,128)} %samples.1), channel_id=1, source_target_pairs={{0,8},{1,12},{2,0},{3,4},{4,9},{5,13},{6,1},{7,5},{8,10},{9,14},{1... | collective-permute-start | bytes 294920 | tf_op jit(solution)/shard_map/ppermute | solution.py:238
  1.2 14.8 %collective-permute-start.1 = (f32[96,256]{1,0:T(8,128)}, f32[96,256]{1,0:T(8,128)S(1)}, u32[]{:S(2)}, u32[]{:S(2)}) collective-permute-start(f32[96,256]{1,0:T(8,128)} %samples.1), channel_id=1, source_target_pairs={{0,12},{1,0},{2,4},{3,8},{4,13},{5,1},{6,5},{7,9},{8,14},{9,2},{10... | collective-permute-start | bytes 294920 | tf_op jit(solution)/shard_map/ppermute | solution.py:238
  3.3 12.8 %collective-permute-start = (f32[96,256]{1,0:T(8,128)}, f32[96,256]{1,0:T(8,128)S(1)}, u32[]{:S(2)}, u32[]{:S(2)}) collective-permute-start(f32[96,256]{1,0:T(8,128)} %samples.1), channel_id=1, source_target_pairs={{0,0},{1,4},{2,8},{3,12},{4,1},{5,5},{6,9},{7,13},{8,2},{9,6},{10,... | collective-permute-start | bytes 294920 | tf_op jit(solution)/shard_map/ppermute | solution.py:238
  7.7 8.3 %collective-permute-start.4 = (f32[96,256]{1,0:T(8,128)}, f32[96,256]{1,0:T(8,128)S(1)}, u32[]{:S(2)}, u32[]{:S(2)}) collective-permute-start(f32[96,256]{1,0:T(8,128)} %samples.1), channel_id=1, source_target_pairs={{0,2},{2,0},{1,3},{3,1},{4,6},{6,4},{5,7},{7,5},{8,10},{10,8},{9,1... | collective-permute-start | bytes 294920 | tf_op jit(solution)/shard_map/ppermute | solution.py:239
  7.8 8.3 %collective-permute-start.3 = (f32[96,256]{1,0:T(8,128)}, f32[96,256]{1,0:T(8,128)S(1)}, u32[]{:S(2)}, u32[]{:S(2)}) collective-permute-start(f32[96,256]{1,0:T(8,128)} %samples.1), channel_id=1, source_target_pairs={{0,4},{1,8},{2,12},{3,0},{4,5},{5,9},{6,13},{7,1},{8,6},{9,10},{10... | collective-permute-start | bytes 294920 | tf_op jit(solution)/shard_map/ppermute | solution.py:238
  11.9 1.6 %copy-start = (f32[1,1,8,256,256]{4,3,2,1,0:T(8,128)S(1)}, f32[1,1,8,256,256]{4,3,2,1,0:T(8,128)}, u32[]{:S(2)}) copy-start(f32[1,1,8,256,256]{4,3,2,1,0:T(8,128)} %param.7) | copy-start | bytes 6291460
  13.5 0.9 %copy-start.1 = (f32[1,256,256]{2,1,0:T(8,128)S(1)}, f32[1,256,256]{2,1,0:T(8,128)}, u32[]{:S(2)}) copy-start(f32[1,256,256]{2,1,0:T(8,128)} %diag.1) | copy-start | bytes 786436
  14.4 0.9 %copy-start.2 = (f32[96,256]{1,0:T(8,128)S(1)}, f32[96,256]{1,0:T(8,128)}, u32[]{:S(2)}) copy-start(f32[96,256]{1,0:T(8,128)} %samples.1) | copy-start | bytes 294916
  17.5 1.8 %collective-permute-start.5 = (f32[4,96,256]{2,1,0:T(8,128)S(1)}, f32[4,96,256]{2,1,0:T(8,128)S(1)}, u32[]{:S(2)}, u32[]{:S(2)}) collective-permute-start(f32[4,96,256]{2,1,0:T(8,128)S(1)} %get-tuple-element.18), channel_id=1, source_target_pairs={{0,1},{1,0},{2,3},{3,2},{4,5},{5,4},{6,7},{7,6},{8,9},{9,8},{10,11... | collective-permute-start | bytes 1179656 | tf_op jit(solution)/shard_map/ppermute | solution.py:244
  19.4 7.0 %collective-permute-start.6 = (f32[2,96,256]{2,1,0:T(8,128)S(1)}, f32[2,96,256]{2,1,0:T(8,128)S(1)}, u32[]{:S(2)}, u32[]{:S(2)}) collective-permute-start(f32[2,96,256]{2,1,0:T(8,128)S(1)} %slice_add_fusion), channel_id=1, source_target_pairs={{0,2},{2,0},{1,3},{3,1},{4,6},{6,4},{5,7},{7,5},{8,10},{10,8},{9,1... | collective-permute-start | bytes 589832 | tf_op jit(solution)/shard_map/ppermute | solution.py:248
  26.4 6.6 %collective-permute-start.7 = (f32[2,96,256]{2,1,0:T(8,128)S(1)}, f32[2,96,256]{2,1,0:T(8,128)S(1)}, u32[]{:S(2)}, u32[]{:S(2)}) collective-permute-start(f32[2,96,256]{2,1,0:T(8,128)S(1)} %add.7.own_image), channel_id=1, source_target_pairs={{0,1},{1,0},{2,3},{3,2},{4,5},{5,4},{6,7},{7,6},{8,9},{9,8},{10,11... | collective-permute-start | bytes 589832 | tf_op jit(solution)/shard_map/ppermute | solution.py:258
  26.5 12.3 %collective-permute-start.9 = (f32[2,96,256]{2,1,0:T(8,128)S(1)}, f32[2,96,256]{2,1,0:T(8,128)S(1)}, u32[]{:S(2)}, u32[]{:S(2)}) collective-permute-start(f32[2,96,256]{2,1,0:T(8,128)S(1)} %add.7.own_image), channel_id=1, source_target_pairs={{0,12},{1,8},{2,4},{3,0},{4,13},{5,9},{6,5},{7,1},{8,14},{9,10},{1... | collective-permute-start | bytes 589832 | tf_op jit(solution)/shard_map/ppermute | solution.py:257
  27.3 14.2 %collective-permute-start.8 = (f32[2,96,256]{2,1,0:T(8,128)S(1)}, f32[2,96,256]{2,1,0:T(8,128)S(1)}, u32[]{:S(2)}, u32[]{:S(2)}) collective-permute-start(f32[2,96,256]{2,1,0:T(8,128)S(1)} %add.7.own_image), channel_id=1, source_target_pairs={{0,0},{1,4},{2,8},{3,12},{4,1},{5,5},{6,9},{7,13},{8,2},{9,6},{10,... | collective-permute-start | bytes 589832 | tf_op jit(solution)/shard_map/ppermute | solution.py:257

commit v4 on v3

--- a/solution.py
+++ b/solution.py
@@ -33,35 +33,38 @@
     return values - jnp.clip(values, -limit_value, limit_value)
 
 
-def prepare_kernel(samples, diag, tiles, own, own_diag, held, high, low, sems):
-    slots = tiles.shape[0]
+def prepare_kernel(*refs):
+    slots = refs[3].shape[0]
+    sources, targets = refs[:4], refs[4:8]
+    high, low, sems = refs[8:]
+    tiles, held = sources[3], targets[3]
     copies = [
         pltpu.make_async_copy(tiles.at[slot], held.at[slot], sems.at[slot])
         for slot in range(slots)
     ]
-    copies.append(pltpu.make_async_copy(samples, own, sems.at[slots]))
-    copies.append(pltpu.make_async_copy(diag, own_diag, sems.at[slots + 1]))
+    for turn in range(3):
+        copies.append(pltpu.make_async_copy(sources[turn], targets[turn], sems.at[slots + turn]))
     for copy in copies:
         copy.start()
     for slot in range(slots):
         copies[slot].wait()
         high[slot], low[slot] = halves(held[slot])
-    copies[slots].wait()
-    copies[slots + 1].wait()
-
-
-def prepare(samples, diag, tiles):
-    held = [jax.ShapeDtypeStruct(x.shape, f32) for x in (samples, diag, tiles)]
-    half = jax.ShapeDtypeStruct(tiles.shape, bf16)
+    for copy in copies[slots:]:
+        copy.wait()
+
+
+def prepare(*arrays):
+    held = [jax.ShapeDtypeStruct(x.shape, x.dtype) for x in arrays]
+    half = jax.ShapeDtypeStruct(arrays[-1].shape, bf16)
     return pl.pallas_call(
         prepare_kernel,
         out_shape=(*held, half, half),
-        in_specs=[hbm] * 3,
-        out_specs=(vmem,) * 5,
-        scratch_shapes=[pltpu.SemaphoreType.DMA((tiles.shape[0] + 2,))],
+        in_specs=[hbm] * 4,
+        out_specs=(smem,) + (vmem,) * 5,
+        scratch_shapes=[pltpu.SemaphoreType.DMA((arrays[-1].shape[0] + 3,))],
         compiler_params=room,
         name="prepare",
-    )(samples, diag, tiles)
+    )(*[pltpu.with_memory_space_constraint(x, pltpu.HBM) for x in arrays])
 
 
 def partial_kernel(groups, place, count, samples, diag, high, low, *refs):
@@ -237,7 +240,7 @@
 
     col_pieces = [lax.ppermute(samples, grid_axes, from_row_line(turn)) for turn in span]
     beside = [lax.ppermute(samples, "col", around(cols, turn)) for turn in range(1, cols)]
-    own, own_diag, held, high, low = prepare(samples, diag_tiles, tiles)
+    place, own, own_diag, held, high, low = prepare(place, samples, diag_tiles, tiles)
     kept, sent, panel = partial_image(
         place, tile_count, own, own_diag, high, low, col_pieces, beside
     )

time: 44.4 us -> 44.3 us (level)
  local copies, waits for them, and re-layouts: 3.43 us -> 0 us
  starting transfers between devices: 17.3 us -> 20.3 us
  Pallas kernels: 5.99 us -> 7.6 us
  waiting for transfers between devices: 15.9 us -> 14.7 us
    unnamed x8 -> x0, local copies, waits for them, and re-layouts: 3.43 us -> none
    pallas_call x1, Pallas kernels: 0.71 us -> 2.31 us  [prepare(): pl.pallas_call(prepare_kernel, out_shape=(*held, half, half), in_specs=[h...]
    ppermute x2, starting transfers between devices: 6.48 us -> 8 us  [on_device(): lax.ppermute(image, grid_axes, to_row(turn))]
    ppermute x1, starting transfers between devices: 0.07 us -> 1.15 us  [on_device(): image = image + lax.ppermute(chip, 'col', around(cols, turn))]
    ppermute x1, waiting for transfers between devices: 6.93 us -> 6.1 us  [on_device(): image = image + lax.ppermute(chip, 'col', around(cols, turn))]
    ppermute x1, starting transfers between devices: 0.07 us -> 0.52 us  [on_device(): swapped = lax.ppermute(sent, 'rep', around(2, 1))]
  transfers between devices with their start and end apart: 10 -> 10, of which waited for: 4 -> 4; matrix products, arithmetic and copies ran while one was open for 0% -> 0% of each run, Pallas kernels for 4% -> 8%
where the time goes in v4:
time: 44.3 us; the launch traced here: 44.1 us
  starting transfers between devices  20.3 us (46%)
  waiting for transfers between devices  14.7 us (33%)
  Pallas kernels  7.6 us (17%)
  between operations  1.4 us (3%)
    ppermute x4, starting transfers between devices, on_device(): lax.ppermute(samples, grid_axes, from_row_line(turn))  10.5 us
    ppermute x2, starting transfers between devices, on_device(): lax.ppermute(image, grid_axes, to_row(turn))  8 us
    ppermute x2, waiting for transfers between devices, on_device(): lax.ppermute(image, grid_axes, to_row(turn))  7.25 us
    ppermute x1, waiting for transfers between devices, on_device(): image = image + lax.ppermute(chip, 'col', around(cols, turn))  6.1 us
    pallas_call x1, Pallas kernels, update_slots(): pl.pallas_call(slots_kernel, out_shape=jax.ShapeDtypeStruct(tiles.shape,...  2.61 us
    pallas_call x1, Pallas kernels, prepare(): pl.pallas_call(prepare_kernel, out_shape=(*held, half, half), in_specs=[h...  2.31 us
    pallas_call x1, Pallas kernels, partial_image(): pl.pallas_call(functools.partial(partial_kernel, groups), out_shape=(kept...  1.43 us
    ppermute x1, waiting for transfers between devices, on_device(): swapped = lax.ppermute(sent, 'rep', around(2, 1))  1.35 us
  transfers between devices with their start and end apart: 10, of which 4 were waited for; matrix products, arithmetic and copies ran while one was open for 0% of the time, Pallas kernels for 8%

profile of v4, /device:TPU:6, one launch (start us, length us, event | category | flops | bytes accessed | tf_op | source)
XLA Modules:
  0.0 44.1 jit_solution(13490568661094360182)
XLA Ops:
  0.6 0.6 %collective-permute-start.2 = (f32[96,256]{1,0:T(8,128)}, f32[96,256]{1,0:T(8,128)S(1)}, u32[]{:S(2)}, u32[]{:S(2)}) collective-permute-start(f32[96,256]{1,0:T(8,128)} %refs_1_.1), channel_id=1, source_target_pairs={{0,8},{1,12},{2,0},{3,4},{4,9},{5,13},{6,1},{7,5},{8,10},{9,14},{1... | collective-permute-start | bytes 294920 | tf_op jit(solution)/shard_map/ppermute | solution.py:241
  1.2 2.0 %collective-permute-start.1 = (f32[96,256]{1,0:T(8,128)}, f32[96,256]{1,0:T(8,128)S(1)}, u32[]{:S(2)}, u32[]{:S(2)}) collective-permute-start(f32[96,256]{1,0:T(8,128)} %refs_1_.1), channel_id=1, source_target_pairs={{0,12},{1,0},{2,4},{3,8},{4,13},{5,1},{6,5},{7,9},{8,14},{9,2},{10... | collective-permute-start | bytes 294920 | tf_op jit(solution)/shard_map/ppermute | solution.py:241
  3.2 4.5 %collective-permute-start = (f32[96,256]{1,0:T(8,128)}, f32[96,256]{1,0:T(8,128)S(1)}, u32[]{:S(2)}, u32[]{:S(2)}) collective-permute-start(f32[96,256]{1,0:T(8,128)} %refs_1_.1), channel_id=1, source_target_pairs={{0,0},{1,4},{2,8},{3,12},{4,1},{5,5},{6,9},{7,13},{8,2},{9,6},{10,... | collective-permute-start | bytes 294920 | tf_op jit(solution)/shard_map/ppermute | solution.py:241
  7.7 0.1 collective-permute-start.4
  7.8 3.4 %collective-permute-start.3 = (f32[96,256]{1,0:T(8,128)}, f32[96,256]{1,0:T(8,128)S(1)}, u32[]{:S(2)}, u32[]{:S(2)}) collective-permute-start(f32[96,256]{1,0:T(8,128)} %refs_1_.1), channel_id=1, source_target_pairs={{0,4},{1,8},{2,12},{3,0},{4,5},{5,9},{6,13},{7,1},{8,6},{9,10},{10... | collective-permute-start | bytes 294920 | tf_op jit(solution)/shard_map/ppermute | solution.py:241
  11.9 2.3 %prepare.1 = (s32[2,8]{1,0:T(2,128)S(1)}, f32[96,256]{1,0:T(8,128)S(1)}, f32[1,256,256]{2,1,0:T(8,128)S(1)}, f32[8,256,256]{2,1,0:T(8,128)S(1)}, bf16[8,256,256]...) custom-call(s32[2,8]{1,0:T(2,128)} %bitcast.7, f32[96,256]{1,0:T(8,128)} %refs_1_.1, f32[1,256,256]{2,1,0:T(8,128)} %refs_2_.1, ...), custom_call_target="tpu_custom_call" | custom-call | tf_op jit(solution)/shard_map/prepare/pallas_call | solution.py:59
  14.2 0.0 collective-permute-done.2.refs_2_
  14.2 0.0 collective-permute-done.1.refs_1_
  14.2 0.0 collective-permute-done.refs_0_
  14.2 0.0 collective-permute-done.4.refs_4_.refs_0_
  14.2 0.0 collective-permute-done.3.refs_3_
  14.2 1.4 %partial_image.1 = (f32[2,96,256]{2,1,0:T(8,128)S(1)}, f32[4,96,256]{2,1,0:T(8,128)S(1)}, bf16[4,192,256]{2,1,0:T(8,128)(2,1)S(1)}) custom-call(s32[2,8]{1,0:T(2,128)S(1)} %get-tuple-element.14.place, s32[1,1]{1,0:T(1,128)S(6)} %copy.7.count, f32[96,256]{1,0:T(8,128)S(1)} %get-tuple-element.15.samples, f32[1,256,256]{2,1,0:T(8,128)S(1)} %get-tuple-element.16.diag, ...), custom_call_target="tpu_custom_call" | custom-call | tf_op jit(solution)/shard_map/partial_image/pallas_call | solution.py:108
  15.7 0.5 %collective-permute-start.5 = (f32[4,96,256]{2,1,0:T(8,128)S(1)}, f32[4,96,256]{2,1,0:T(8,128)S(1)}, u32[]{:S(2)}, u32[]{:S(2)}) collective-permute-start(f32[4,96,256]{2,1,0:T(8,128)S(1)} %get-tuple-element.20), channel_id=1, source_target_pairs={{0,1},{1,0},{2,3},{3,2},{4,5},{5,4},{6,7},{7,6},{8,9},{9,8},{10,11... | collective-permute-start | bytes 1179656 | tf_op jit(solution)/shard_map/ppermute | solution.py:247
  16.2 1.3 %collective-permute-done.5.swapped = f32[4,96,256]{2,1,0:T(8,128)S(1)} collective-permute-done((f32[4,96,256]{2,1,0:T(8,128)S(1)}, f32[4,96,256]{2,1,0:T(8,128)S(1)}, u32[]{:S(2)}, u32[]{:S(2)}) %collective-permute-start.5) | collective-permute-done | bytes 393248 | tf_op jit(solution)/shard_map/ppermute | solution.py:247
  17.6 1.1 %collective-permute-start.6 = (f32[2,96,256]{2,1,0:T(8,128)S(1)}, f32[2,96,256]{2,1,0:T(8,128)S(1)}, u32[]{:S(2)}, u32[]{:S(2)}) collective-permute-start(f32[2,96,256]{2,1,0:T(8,128)S(1)} %slice_add_fusion), channel_id=1, source_target_pairs={{0,2},{2,0},{1,3},{3,1},{4,6},{6,4},{5,7},{7,5},{8,10},{10,8},{9,1... | collective-permute-start | bytes 589832 | tf_op jit(solution)/shard_map/ppermute | solution.py:251
  18.7 6.1 %collective-permute-done.6 = f32[2,96,256]{2,1,0:T(8,128)S(1)} collective-permute-done((f32[2,96,256]{2,1,0:T(8,128)S(1)}, f32[2,96,256]{2,1,0:T(8,128)S(1)}, u32[]{:S(2)}, u32[]{:S(2)}) %collective-permute-start.6) | collective-permute-done | bytes 196640 | tf_op jit(solution)/shard_map/ppermute | solution.py:251
  24.9 0.1 collective-permute-start.7
  24.9 2.3 %collective-permute-start.9 = (f32[2,96,256]{2,1,0:T(8,128)S(1)}, f32[2,96,256]{2,1,0:T(8,128)S(1)}, u32[]{:S(2)}, u32[]{:S(2)}) collective-permute-start(f32[2,96,256]{2,1,0:T(8,128)S(1)} %add.7.own_image), channel_id=1, source_target_pairs={{0,12},{1,8},{2,4},{3,0},{4,13},{5,9},{6,5},{7,1},{8,14},{9,10},{1... | collective-permute-start | bytes 589832 | tf_op jit(solution)/shard_map/ppermute | solution.py:260
  27.2 5.7 %collective-permute-start.8 = (f32[2,96,256]{2,1,0:T(8,128)S(1)}, f32[2,96,256]{2,1,0:T(8,128)S(1)}, u32[]{:S(2)}, u32[]{:S(2)}) collective-permute-start(f32[2,96,256]{2,1,0:T(8,128)S(1)} %add.7.own_image), channel_id=1, source_target_pairs={{0,0},{1,4},{2,8},{3,12},{4,1},{5,5},{6,9},{7,13},{8,2},{9,6},{10,... | collective-permute-start | bytes 589832 | tf_op jit(solution)/shard_map/ppermute | solution.py:260
  33.0 0.0 collective-permute-done.7.other_image
  33.0 1.2 %middle.1 = (bf16[4,256,256]{2,1,0:T(8,128)(2,1)S(1)}, bf16[4,256,256]{2,1,0:T(8,128)(2,1)S(1)}, f32[1,256,256]{2,1,0:T(8,128)}) custom-call(f32[2,96,256]{2,1,0:T(8,128)S(1)} %add.7.own_image, f32[2,96,256]{2,1,0:T(8,128)S(1)} %collective-permute-done.7.other_image, f32[96,256]{1,0:T(8,128)S(1)} %get-tuple-element.15.samples, ...), custom_call_target="tpu_custom_call" | custom-call | tf_op jit(solution)/shard_map/middle/pallas_call | solution.py:163
  34.2 1.8 %collective-permute-done.9.second = f32[2,96,256]{2,1,0:T(8,128)S(1)} collective-permute-done((f32[2,96,256]{2,1,0:T(8,128)S(1)}, f32[2,96,256]{2,1,0:T(8,128)S(1)}, u32[]{:S(2)}, u32[]{:S(2)}) %collective-permute-start.9) | collective-permute-done | bytes 196640 | tf_op jit(solution)/shard_map/ppermute | solution.py:260
  36.1 5.4 %collective-permute-done.8.first = f32[2,96,256]{2,1,0:T(8,128)S(1)} collective-permute-done((f32[2,96,256]{2,1,0:T(8,128)S(1)}, f32[2,96,256]{2,1,0:T(8,128)S(1)}, u32[]{:S(2)}, u32[]{:S(2)}) %collective-permute-start.8) | collective-permute-done | bytes 196640 | tf_op jit(solution)/shard_map/ppermute | solution.py:260
  41.5 2.6 %update_slots.1 = f32[8,256,256]{2,1,0:T(8,128)} custom-call(s32[2,8]{1,0:T(2,128)S(1)} %get-tuple-element.14.place, s32[1,1]{1,0:T(1,128)S(6)} %copy.7.count, bf16[4,256,256]{2,1,0:T(8,128)(2,1)S(1)} %get-tuple-element.21.left_high, bf16[4,256,256]{2,1,0:T(8,128)(2,1)S(1)} %get-tuple-element.22.left_low, bf16[4,192,256]{2,1,0:T(8,128)(2,1)S(1)} %get-tuple-element.23.panel, ...), custom_call_target="tpu_custom_call" | custom-call | tf_op jit(solution)/shard_map/update_slots/pallas_call | solution.py:209
  (2 shorter events, 0.1 us)
Async XLA Ops:
  0.6 13.6 %collective-permute-start.2 = (f32[96,256]{1,0:T(8,128)}, f32[96,256]{1,0:T(8,128)S(1)}, u32[]{:S(2)}, u32[]{:S(2)}) collective-permute-start(f32[96,256]{1,0:T(8,128)} %refs_1_.1), channel_id=1, source_target_pairs={{0,8},{1,12},{2,0},{3,4},{4,9},{5,13},{6,1},{7,5},{8,10},{9,14},{1... | collective-permute-start | bytes 294920 | tf_op jit(solution)/shard_map/ppermute | solution.py:241
  1.2 13.0 %collective-permute-start.1 = (f32[96,256]{1,0:T(8,128)}, f32[96,256]{1,0:T(8,128)S(1)}, u32[]{:S(2)}, u32[]{:S(2)}) collective-permute-start(f32[96,256]{1,0:T(8,128)} %refs_1_.1), channel_id=1, source_target_pairs={{0,12},{1,0},{2,4},{3,8},{4,13},{5,1},{6,5},{7,9},{8,14},{9,2},{10... | collective-permute-start | bytes 294920 | tf_op jit(solution)/shard_map/ppermute | solution.py:241
  3.2 11.0 %collective-permute-start = (f32[96,256]{1,0:T(8,128)}, f32[96,256]{1,0:T(8,128)S(1)}, u32[]{:S(2)}, u32[]{:S(2)}) collective-permute-start(f32[96,256]{1,0:T(8,128)} %refs_1_.1), channel_id=1, source_target_pairs={{0,0},{1,4},{2,8},{3,12},{4,1},{5,5},{6,9},{7,13},{8,2},{9,6},{10,... | collective-permute-start | bytes 294920 | tf_op jit(solution)/shard_map/ppermute | solution.py:241
  7.7 6.5 %collective-permute-start.4 = (f32[96,256]{1,0:T(8,128)}, f32[96,256]{1,0:T(8,128)S(1)}, u32[]{:S(2)}, u32[]{:S(2)}) collective-permute-start(f32[96,256]{1,0:T(8,128)} %refs_1_.1), channel_id=1, source_target_pairs={{0,2},{2,0},{1,3},{3,1},{4,6},{6,4},{5,7},{7,5},{8,10},{10,8},{9,1... | collective-permute-start | bytes 294920 | tf_op jit(solution)/shard_map/ppermute | solution.py:242
  7.8 6.4 %collective-permute-start.3 = (f32[96,256]{1,0:T(8,128)}, f32[96,256]{1,0:T(8,128)S(1)}, u32[]{:S(2)}, u32[]{:S(2)}) collective-permute-start(f32[96,256]{1,0:T(8,128)} %refs_1_.1), channel_id=1, source_target_pairs={{0,4},{1,8},{2,12},{3,0},{4,5},{5,9},{6,13},{7,1},{8,6},{9,10},{10... | collective-permute-start | bytes 294920 | tf_op jit(solution)/shard_map/ppermute | solution.py:241
  15.7 1.9 %collective-permute-start.5 = (f32[4,96,256]{2,1,0:T(8,128)S(1)}, f32[4,96,256]{2,1,0:T(8,128)S(1)}, u32[]{:S(2)}, u32[]{:S(2)}) collective-permute-start(f32[4,96,256]{2,1,0:T(8,128)S(1)} %get-tuple-element.20), channel_id=1, source_target_pairs={{0,1},{1,0},{2,3},{3,2},{4,5},{5,4},{6,7},{7,6},{8,9},{9,8},{10,11... | collective-permute-start | bytes 1179656 | tf_op jit(solution)/shard_map/ppermute | solution.py:247
  17.6 7.2 %collective-permute-start.6 = (f32[2,96,256]{2,1,0:T(8,128)S(1)}, f32[2,96,256]{2,1,0:T(8,128)S(1)}, u32[]{:S(2)}, u32[]{:S(2)}) collective-permute-start(f32[2,96,256]{2,1,0:T(8,128)S(1)} %slice_add_fusion), channel_id=1, source_target_pairs={{0,2},{2,0},{1,3},{3,1},{4,6},{6,4},{5,7},{7,5},{8,10},{10,8},{9,1... | collective-permute-start | bytes 589832 | tf_op jit(solution)/shard_map/ppermute | solution.py:251
  24.9 8.1 %collective-permute-start.7 = (f32[2,96,256]{2,1,0:T(8,128)S(1)}, f32[2,96,256]{2,1,0:T(8,128)S(1)}, u32[]{:S(2)}, u32[]{:S(2)}) collective-permute-start(f32[2,96,256]{2,1,0:T(8,128)S(1)} %add.7.own_image), channel_id=1, source_target_pairs={{0,1},{1,0},{2,3},{3,2},{4,5},{5,4},{6,7},{7,6},{8,9},{9,8},{10,11... | collective-permute-start | bytes 589832 | tf_op jit(solution)/shard_map/ppermute | solution.py:261
  24.9 11.1 %collective-permute-start.9 = (f32[2,96,256]{2,1,0:T(8,128)S(1)}, f32[2,96,256]{2,1,0:T(8,128)S(1)}, u32[]{:S(2)}, u32[]{:S(2)}) collective-permute-start(f32[2,96,256]{2,1,0:T(8,128)S(1)} %add.7.own_image), channel_id=1, source_target_pairs={{0,12},{1,8},{2,4},{3,0},{4,13},{5,9},{6,5},{7,1},{8,14},{9,10},{1... | collective-permute-start | bytes 589832 | tf_op jit(solution)/shard_map/ppermute | solution.py:260
  27.2 14.2 %collective-permute-start.8 = (f32[2,96,256]{2,1,0:T(8,128)S(1)}, f32[2,96,256]{2,1,0:T(8,128)S(1)}, u32[]{:S(2)}, u32[]{:S(2)}) collective-permute-start(f32[2,96,256]{2,1,0:T(8,128)S(1)} %add.7.own_image), channel_id=1, source_target_pairs={{0,0},{1,4},{2,8},{3,12},{4,1},{5,5},{6,9},{7,13},{8,2},{9,6},{10,... | collective-permute-start | bytes 589832 | tf_op jit(solution)/shard_map/ppermute | solution.py:260

commit v5 on v4

--- a/solution.py
+++ b/solution.py
@@ -76,7 +76,8 @@
     rep = lax.axis_index("rep")
     rows = samples.shape[0]
     for turn in range(groups):
-        block = lax.rem(row + turn, groups)
+        spot = lax.rem(row + turn, groups)
+        block = 2 * lax.rem(spot, groups // 2) + lax.div(spot, groups // 2)
         panel[block, :rows], panel[block, rows:] = halves(pieces[turn][...])
     total[...] = jnp.zeros_like(total)
 
@@ -177,7 +178,7 @@
     groups = panel.shape[0]
     rows = panel.shape[1] // 2
     half = high.shape[1] // 2
-    parity = lax.rem(lax.axis_index("row"), 2)
+    parity = lax.div(lax.axis_index("row"), groups // 2)
     for ref in (high, low):
         for start in (rows, half + rows):
             blank = jnp.zeros((groups, half - rows, high.shape[2]), bf16)
@@ -232,7 +233,9 @@
 
     def from_row_line(turn):
         return [
-            (line * groups + j, (j - turn) % groups * groups + line) for line in span for j in span
+            (line * groups + j, (j // 2 + cols * (j % 2) - turn) % groups * groups + line)
+            for line in span
+            for j in span
         ]
 
     def around(size, turn):
@@ -252,9 +255,9 @@
 
     def to_row(turn):
         return [
-            (line * groups + j, (groups - 1 - j if turn else j) * groups + line)
+            (line * groups + j, (groups - 1 - spot if turn else spot) * groups + line)
             for line in span
-            for j in span
+            for j, spot in enumerate(x + cols * r for x in range(cols) for r in range(2))
         ]
 
     first, second = [lax.ppermute(image, grid_axes, to_row(turn)) for turn in range(2)]

time: 44.3 us -> 47.2 us (1.065)
  starting transfers between devices: 20.3 us -> 22.9 us
    ppermute x4, starting transfers between devices: 10.5 us -> 13.7 us  [on_device(): lax.ppermute(samples, grid_axes, from_row_line(turn))]
    ppermute x4, waiting for transfers between devices: 0.01 us -> 0.64 us  [on_device(): lax.ppermute(samples, grid_axes, from_row_line(turn))]
    ppermute x2, waiting for transfers between devices: 7.25 us -> 6.76 us  [on_device(): lax.ppermute(image, grid_axes, to_row(turn))]
  transfers between devices with their start and end apart: 10 -> 10, of which waited for: 4 -> 5; matrix products, arithmetic and copies ran while one was open for 0% -> 0% of each run, Pallas kernels for 8% -> 8%
where the time goes in v5:
time: 47.2 us; the launch traced here: 47 us
  starting transfers between devices  22.9 us (49%)
  waiting for transfers between devices  14.9 us (32%)
  Pallas kernels  7.6 us (16%)
  between operations  1.41 us (3%)
    ppermute x4, starting transfers between devices, on_device(): lax.ppermute(samples, grid_axes, from_row_line(turn))  13.7 us
    ppermute x2, starting transfers between devices, on_device(): lax.ppermute(image, grid_axes, to_row(turn))  7.82 us
    ppermute x2, waiting for transfers between devices, on_device(): lax.ppermute(image, grid_axes, to_row(turn))  6.76 us
    ppermute x1, waiting for transfers between devices, on_device(): image = image + lax.ppermute(chip, 'col', around(cols, turn))  5.83 us
    pallas_call x1, Pallas kernels, update_slots(): pl.pallas_call(slots_kernel, out_shape=jax.ShapeDtypeStruct(tiles.shape,...  2.62 us
    pallas_call x1, Pallas kernels, prepare(): pl.pallas_call(prepare_kernel, out_shape=(*held, half, half), in_specs=[h...  2.31 us
    ppermute x1, waiting for transfers between devices, on_device(): swapped = lax.ppermute(sent, 'rep', around(2, 1))  1.71 us
    pallas_call x1, Pallas kernels, partial_image(): pl.pallas_call(functools.partial(partial_kernel, groups), out_shape=(kept...  1.43 us
  transfers between devices with their start and end apart: 10, of which 5 were waited for; matrix products, arithmetic and copies ran while one was open for 0% of the time, Pallas kernels for 8%

profile of v5, /device:TPU:6, one launch (start us, length us, event | category | flops | bytes accessed | tf_op | source)
XLA Modules:
  0.0 47.0 jit_solution(10074869299545140829)
XLA Ops:
  0.6 3.6 %collective-permute-start.2 = (f32[96,256]{1,0:T(8,128)}, f32[96,256]{1,0:T(8,128)S(1)}, u32[]{:S(2)}, u32[]{:S(2)}) collective-permute-start(f32[96,256]{1,0:T(8,128)} %refs_1_.1), channel_id=1, source_target_pairs={{0,8},{1,0},{2,12},{3,4},{4,9},{5,1},{6,13},{7,5},{8,10},{9,2},{10... | collective-permute-start | bytes 294920 | tf_op jit(solution)/shard_map/ppermute | solution.py:244
  4.3 1.9 %collective-permute-start.1 = (f32[96,256]{1,0:T(8,128)}, f32[96,256]{1,0:T(8,128)S(1)}, u32[]{:S(2)}, u32[]{:S(2)}) collective-permute-start(f32[96,256]{1,0:T(8,128)} %refs_1_.1), channel_id=1, source_target_pairs={{0,12},{1,4},{2,0},{3,8},{4,13},{5,5},{6,1},{7,9},{8,14},{9,6},{10... | collective-permute-start | bytes 294920 | tf_op jit(solution)/shard_map/ppermute | solution.py:244
  6.2 2.8 %collective-permute-start = (f32[96,256]{1,0:T(8,128)}, f32[96,256]{1,0:T(8,128)S(1)}, u32[]{:S(2)}, u32[]{:S(2)}) collective-permute-start(f32[96,256]{1,0:T(8,128)} %refs_1_.1), channel_id=1, source_target_pairs={{0,0},{1,8},{2,4},{3,12},{4,1},{5,9},{6,5},{7,13},{8,2},{9,10},{10... | collective-permute-start | bytes 294920 | tf_op jit(solution)/shard_map/ppermute | solution.py:244
  9.0 0.1 collective-permute-start.4
  9.1 5.3 %collective-permute-start.3 = (f32[96,256]{1,0:T(8,128)}, f32[96,256]{1,0:T(8,128)S(1)}, u32[]{:S(2)}, u32[]{:S(2)}) collective-permute-start(f32[96,256]{1,0:T(8,128)} %refs_1_.1), channel_id=1, source_target_pairs={{0,4},{1,12},{2,8},{3,0},{4,5},{5,13},{6,9},{7,1},{8,6},{9,14},{10... | collective-permute-start | bytes 294920 | tf_op jit(solution)/shard_map/ppermute | solution.py:244
  15.1 2.3 %prepare.1 = (s32[2,8]{1,0:T(2,128)S(1)}, f32[96,256]{1,0:T(8,128)S(1)}, f32[1,256,256]{2,1,0:T(8,128)S(1)}, f32[8,256,256]{2,1,0:T(8,128)S(1)}, bf16[8,256,256]...) custom-call(s32[2,8]{1,0:T(2,128)} %bitcast.7, f32[96,256]{1,0:T(8,128)} %refs_1_.1, f32[1,256,256]{2,1,0:T(8,128)} %refs_2_.1, ...), custom_call_target="tpu_custom_call" | custom-call | tf_op jit(solution)/shard_map/prepare/pallas_call | solution.py:59
  17.4 0.0 collective-permute-done.2.refs_2_
  17.4 0.0 collective-permute-done.1.refs_1_
  17.4 0.0 collective-permute-done.refs_0_
  17.4 0.0 collective-permute-done.4.refs_4_.refs_0_
  17.5 0.6 %collective-permute-done.3.refs_3_ = f32[96,256]{1,0:T(8,128)S(1)} collective-permute-done((f32[96,256]{1,0:T(8,128)}, f32[96,256]{1,0:T(8,128)S(1)}, u32[]{:S(2)}, u32[]{:S(2)}) %collective-permute-start.3) | collective-permute-done | bytes 98336 | tf_op jit(solution)/shard_map/ppermute | solution.py:244
  18.1 1.4 %partial_image.1 = (f32[2,96,256]{2,1,0:T(8,128)S(1)}, f32[4,96,256]{2,1,0:T(8,128)S(1)}, bf16[4,192,256]{2,1,0:T(8,128)(2,1)S(1)}) custom-call(s32[2,8]{1,0:T(2,128)S(1)} %get-tuple-element.14.place, s32[1,1]{1,0:T(1,128)S(6)} %copy.7.count, f32[96,256]{1,0:T(8,128)S(1)} %get-tuple-element.15.samples, f32[1,256,256]{2,1,0:T(8,128)S(1)} %get-tuple-element.16.diag, ...), custom_call_target="tpu_custom_call" | custom-call | tf_op jit(solution)/shard_map/partial_image/pallas_call | solution.py:109
  19.5 0.1 collective-permute-start.5
  19.6 1.7 %collective-permute-done.5.swapped = f32[4,96,256]{2,1,0:T(8,128)S(1)} collective-permute-done((f32[4,96,256]{2,1,0:T(8,128)S(1)}, f32[4,96,256]{2,1,0:T(8,128)S(1)}, u32[]{:S(2)}, u32[]{:S(2)}) %collective-permute-start.5) | collective-permute-done | bytes 393248 | tf_op jit(solution)/shard_map/ppermute | solution.py:250
  21.3 1.2 %collective-permute-start.6 = (f32[2,96,256]{2,1,0:T(8,128)S(1)}, f32[2,96,256]{2,1,0:T(8,128)S(1)}, u32[]{:S(2)}, u32[]{:S(2)}) collective-permute-start(f32[2,96,256]{2,1,0:T(8,128)S(1)} %slice_add_fusion), channel_id=1, source_target_pairs={{0,2},{2,0},{1,3},{3,1},{4,6},{6,4},{5,7},{7,5},{8,10},{10,8},{9,1... | collective-permute-start | bytes 589832 | tf_op jit(solution)/shard_map/ppermute | solution.py:254
  22.5 5.8 %collective-permute-done.6 = f32[2,96,256]{2,1,0:T(8,128)S(1)} collective-permute-done((f32[2,96,256]{2,1,0:T(8,128)S(1)}, f32[2,96,256]{2,1,0:T(8,128)S(1)}, u32[]{:S(2)}, u32[]{:S(2)}) %collective-permute-start.6) | collective-permute-done | bytes 196640 | tf_op jit(solution)/shard_map/ppermute | solution.py:254
  28.4 0.1 collective-permute-start.7
  28.5 4.9 %collective-permute-start.9 = (f32[2,96,256]{2,1,0:T(8,128)S(1)}, f32[2,96,256]{2,1,0:T(8,128)S(1)}, u32[]{:S(2)}, u32[]{:S(2)}) collective-permute-start(f32[2,96,256]{2,1,0:T(8,128)S(1)} %add.7.own_image), channel_id=1, source_target_pairs={{0,12},{1,4},{2,8},{3,0},{4,13},{5,5},{6,9},{7,1},{8,14},{9,6},{10... | collective-permute-start | bytes 589832 | tf_op jit(solution)/shard_map/ppermute | solution.py:263
  33.3 2.9 %collective-permute-start.8 = (f32[2,96,256]{2,1,0:T(8,128)S(1)}, f32[2,96,256]{2,1,0:T(8,128)S(1)}, u32[]{:S(2)}, u32[]{:S(2)}) collective-permute-start(f32[2,96,256]{2,1,0:T(8,128)S(1)} %add.7.own_image), channel_id=1, source_target_pairs={{0,0},{1,8},{2,4},{3,12},{4,1},{5,9},{6,5},{7,13},{8,2},{9,10},{10... | collective-permute-start | bytes 589832 | tf_op jit(solution)/shard_map/ppermute | solution.py:263
  36.3 0.0 collective-permute-done.7.other_image
  36.3 1.3 %middle.1 = (bf16[4,256,256]{2,1,0:T(8,128)(2,1)S(1)}, bf16[4,256,256]{2,1,0:T(8,128)(2,1)S(1)}, f32[1,256,256]{2,1,0:T(8,128)}) custom-call(f32[2,96,256]{2,1,0:T(8,128)S(1)} %add.7.own_image, f32[2,96,256]{2,1,0:T(8,128)S(1)} %collective-permute-done.7.other_image, f32[96,256]{1,0:T(8,128)S(1)} %get-tuple-element.15.samples, ...), custom_call_target="tpu_custom_call" | custom-call | tf_op jit(solution)/shard_map/middle/pallas_call | solution.py:164
  37.6 0.1 collective-permute-done.9.second
  37.7 6.6 %collective-permute-done.8.first = f32[2,96,256]{2,1,0:T(8,128)S(1)} collective-permute-done((f32[2,96,256]{2,1,0:T(8,128)S(1)}, f32[2,96,256]{2,1,0:T(8,128)S(1)}, u32[]{:S(2)}, u32[]{:S(2)}) %collective-permute-start.8) | collective-permute-done | bytes 196640 | tf_op jit(solution)/shard_map/ppermute | solution.py:263
  44.3 2.6 %update_slots.1 = f32[8,256,256]{2,1,0:T(8,128)} custom-call(s32[2,8]{1,0:T(2,128)S(1)} %get-tuple-element.14.place, s32[1,1]{1,0:T(1,128)S(6)} %copy.7.count, bf16[4,256,256]{2,1,0:T(8,128)(2,1)S(1)} %get-tuple-element.21.left_high, bf16[4,256,256]{2,1,0:T(8,128)(2,1)S(1)} %get-tuple-element.22.left_low, bf16[4,192,256]{2,1,0:T(8,128)(2,1)S(1)} %get-tuple-element.23.panel, ...), custom_call_target="tpu_custom_call" | custom-call | tf_op jit(solution)/shard_map/update_slots/pallas_call | solution.py:210
  (2 shorter events, 0.1 us)
Async XLA Ops:
  0.6 16.8 %collective-permute-start.2 = (f32[96,256]{1,0:T(8,128)}, f32[96,256]{1,0:T(8,128)S(1)}, u32[]{:S(2)}, u32[]{:S(2)}) collective-permute-start(f32[96,256]{1,0:T(8,128)} %refs_1_.1), channel_id=1, source_target_pairs={{0,8},{1,0},{2,12},{3,4},{4,9},{5,1},{6,13},{7,5},{8,10},{9,2},{10... | collective-permute-start | bytes 294920 | tf_op jit(solution)/shard_map/ppermute | solution.py:244
  4.3 13.2 %collective-permute-start.1 = (f32[96,256]{1,0:T(8,128)}, f32[96,256]{1,0:T(8,128)S(1)}, u32[]{:S(2)}, u32[]{:S(2)}) collective-permute-start(f32[96,256]{1,0:T(8,128)} %refs_1_.1), channel_id=1, source_target_pairs={{0,12},{1,4},{2,0},{3,8},{4,13},{5,5},{6,1},{7,9},{8,14},{9,6},{10... | collective-permute-start | bytes 294920 | tf_op jit(solution)/shard_map/ppermute | solution.py:244
  6.2 11.3 %collective-permute-start = (f32[96,256]{1,0:T(8,128)}, f32[96,256]{1,0:T(8,128)S(1)}, u32[]{:S(2)}, u32[]{:S(2)}) collective-permute-start(f32[96,256]{1,0:T(8,128)} %refs_1_.1), channel_id=1, source_target_pairs={{0,0},{1,8},{2,4},{3,12},{4,1},{5,9},{6,5},{7,13},{8,2},{9,10},{10... | collective-permute-start | bytes 294920 | tf_op jit(solution)/shard_map/ppermute | solution.py:244
  9.0 8.5 %collective-permute-start.4 = (f32[96,256]{1,0:T(8,128)}, f32[96,256]{1,0:T(8,128)S(1)}, u32[]{:S(2)}, u32[]{:S(2)}) collective-permute-start(f32[96,256]{1,0:T(8,128)} %refs_1_.1), channel_id=1, source_target_pairs={{0,2},{2,0},{1,3},{3,1},{4,6},{6,4},{5,7},{7,5},{8,10},{10,8},{9,1... | collective-permute-start | bytes 294920 | tf_op jit(solution)/shard_map/ppermute | solution.py:245
  9.1 9.0 %collective-permute-start.3 = (f32[96,256]{1,0:T(8,128)}, f32[96,256]{1,0:T(8,128)S(1)}, u32[]{:S(2)}, u32[]{:S(2)}) collective-permute-start(f32[96,256]{1,0:T(8,128)} %refs_1_.1), channel_id=1, source_target_pairs={{0,4},{1,12},{2,8},{3,0},{4,5},{5,13},{6,9},{7,1},{8,6},{9,14},{10... | collective-permute-start | bytes 294920 | tf_op jit(solution)/shard_map/ppermute | solution.py:244
  19.5 1.8 %collective-permute-start.5 = (f32[4,96,256]{2,1,0:T(8,128)S(1)}, f32[4,96,256]{2,1,0:T(8,128)S(1)}, u32[]{:S(2)}, u32[]{:S(2)}) collective-permute-start(f32[4,96,256]{2,1,0:T(8,128)S(1)} %get-tuple-element.20), channel_id=1, source_target_pairs={{0,1},{1,0},{2,3},{3,2},{4,5},{5,4},{6,7},{7,6},{8,9},{9,8},{10,11... | collective-permute-start | bytes 1179656 | tf_op jit(solution)/shard_map/ppermute | solution.py:250
  21.3 7.0 %collective-permute-start.6 = (f32[2,96,256]{2,1,0:T(8,128)S(1)}, f32[2,96,256]{2,1,0:T(8,128)S(1)}, u32[]{:S(2)}, u32[]{:S(2)}) collective-permute-start(f32[2,96,256]{2,1,0:T(8,128)S(1)} %slice_add_fusion), channel_id=1, source_target_pairs={{0,2},{2,0},{1,3},{3,1},{4,6},{6,4},{5,7},{7,5},{8,10},{10,8},{9,1... | collective-permute-start | bytes 589832 | tf_op jit(solution)/shard_map/ppermute | solution.py:254
  28.4 7.9 %collective-permute-start.7 = (f32[2,96,256]{2,1,0:T(8,128)S(1)}, f32[2,96,256]{2,1,0:T(8,128)S(1)}, u32[]{:S(2)}, u32[]{:S(2)}) collective-permute-start(f32[2,96,256]{2,1,0:T(8,128)S(1)} %add.7.own_image), channel_id=1, source_target_pairs={{0,1},{1,0},{2,3},{3,2},{4,5},{5,4},{6,7},{7,6},{8,9},{9,8},{10,11... | collective-permute-start | bytes 589832 | tf_op jit(solution)/shard_map/ppermute | solution.py:264
  28.5 9.3 %collective-permute-start.9 = (f32[2,96,256]{2,1,0:T(8,128)S(1)}, f32[2,96,256]{2,1,0:T(8,128)S(1)}, u32[]{:S(2)}, u32[]{:S(2)}) collective-permute-start(f32[2,96,256]{2,1,0:T(8,128)S(1)} %add.7.own_image), channel_id=1, source_target_pairs={{0,12},{1,4},{2,8},{3,0},{4,13},{5,5},{6,9},{7,1},{8,14},{9,6},{10... | collective-permute-start | bytes 589832 | tf_op jit(solution)/shard_map/ppermute | solution.py:263
  33.3 11.0 %collective-permute-start.8 = (f32[2,96,256]{2,1,0:T(8,128)S(1)}, f32[2,96,256]{2,1,0:T(8,128)S(1)}, u32[]{:S(2)}, u32[]{:S(2)}) collective-permute-start(f32[2,96,256]{2,1,0:T(8,128)S(1)} %add.7.own_image), channel_id=1, source_target_pairs={{0,0},{1,8},{2,4},{3,12},{4,1},{5,9},{6,5},{7,13},{8,2},{9,10},{10... | collective-permute-start | bytes 589832 | tf_op jit(solution)/shard_map/ppermute | solution.py:263

commit v6 on v4

--- a/solution.py
+++ b/solution.py
@@ -33,50 +33,71 @@
     return values - jnp.clip(values, -limit_value, limit_value)
 
 
-def prepare_kernel(*refs):
-    slots = refs[3].shape[0]
-    sources, targets = refs[:4], refs[4:8]
-    high, low, sems = refs[8:]
-    tiles, held = sources[3], targets[3]
+def sample_source(turn, row, own):
+    return 2 * own - row - turn
+
+
+def image_source(turn, row, own):
+    return 2 * own - 1 - row if turn else row - 2 * own
+
+
+def prepare_kernel(groups, place, count, *refs):
+    arrays, (guide, *held), (high, low, sems) = refs[:3], refs[3:7], refs[7:]
+    tiles = held[2]
+    slots = tiles.shape[0]
     copies = [
-        pltpu.make_async_copy(tiles.at[slot], held.at[slot], sems.at[slot])
+        pltpu.make_async_copy(arrays[2].at[slot], tiles.at[slot], sems.at[slot])
         for slot in range(slots)
     ]
-    for turn in range(3):
-        copies.append(pltpu.make_async_copy(sources[turn], targets[turn], sems.at[slots + turn]))
+    for turn in range(2):
+        copies.append(pltpu.make_async_copy(arrays[turn], held[turn], sems.at[slots + turn]))
     for copy in copies:
         copy.start()
     for slot in range(slots):
+        guide[0, slot] = place[0, slot]
+        guide[1, slot] = place[1, slot]
+    row = lax.axis_index("row")
+    own = lax.axis_index("col") * 2 + lax.axis_index("rep")
+    for turn in range(groups):
+        guide[2, turn] = lax.rem(sample_source(turn, row, own) + 4 * groups, groups)
+    for turn in range(2):
+        guide[3, turn] = lax.rem(image_source(turn, row, own) + 4 * groups, 2)
+    guide[4, 0] = count[0, 0]
+    for slot in range(slots):
         copies[slot].wait()
-        high[slot], low[slot] = halves(held[slot])
+        high[slot], low[slot] = halves(tiles[slot])
     for copy in copies[slots:]:
         copy.wait()
 
 
-def prepare(*arrays):
+def prepare(groups, place, count, *arrays):
+    width = max(place.shape[1], groups)
     held = [jax.ShapeDtypeStruct(x.shape, x.dtype) for x in arrays]
     half = jax.ShapeDtypeStruct(arrays[-1].shape, bf16)
     return pl.pallas_call(
-        prepare_kernel,
-        out_shape=(*held, half, half),
-        in_specs=[hbm] * 4,
+        functools.partial(prepare_kernel, groups),
+        out_shape=(pltpu.SMEM((5, width), jnp.int32), *held, half, half),
+        in_specs=[smem] * 2 + [hbm] * 3,
         out_specs=(smem,) + (vmem,) * 5,
-        scratch_shapes=[pltpu.SemaphoreType.DMA((arrays[-1].shape[0] + 3,))],
+        scratch_shapes=[pltpu.SemaphoreType.DMA((arrays[-1].shape[0] + 2,))],
         compiler_params=room,
         name="prepare",
-    )(*[pltpu.with_memory_space_constraint(x, pltpu.HBM) for x in arrays])
-
-
-def partial_kernel(groups, place, count, samples, diag, high, low, *refs):
+    )(
+        place,
+        count,
+        *[pltpu.with_memory_space_constraint(x, pltpu.HBM) for x in arrays],
+    )
+
+
+def partial_kernel(groups, guide, samples, diag, high, low, *refs):
     pieces = refs[:groups]
     beside = refs[groups:-4]
     kept, sent, panel, total = refs[-4:]
-    row = lax.axis_index("row")
     col = lax.axis_index("col")
     rep = lax.axis_index("rep")
     rows = samples.shape[0]
     for turn in range(groups):
-        block = lax.rem(row + turn, groups)
+        block = guide[2, turn]
         panel[block, :rows], panel[block, rows:] = halves(pieces[turn][...])
     total[...] = jnp.zeros_like(total)
 
@@ -89,9 +110,9 @@
         own_high, jnp.concatenate([own_high, own_low], axis=0), *halves(diag[0]), ((1,), (0,))
     )
     for slot in range(high.shape[0]):
-        source = panel.at[place[1, slot]]
+        source = panel.at[guide[1, slot]]
         value = term(source[:rows], source[...], high[slot], low[slot], ((1,), (1,)))
-        total[place[0, slot]] += jnp.where(slot < count[0, 0], value, 0.0)
+        total[guide[0, slot]] += jnp.where(slot < guide[4, 0], value, 0.0)
     for pair in range(groups // 2):
         kept[pair] = total[2 * pair + rep]
         sent[pair] = total[2 * pair + 1 - rep]
@@ -99,7 +120,7 @@
         sent[groups // 2 + turn] = piece[...]
 
 
-def partial_image(place, count, samples, diag, high, low, pieces, beside):
+def partial_image(guide, samples, diag, high, low, pieces, beside):
     groups = len(pieces)
     rows, side = samples.shape
     kept = jax.ShapeDtypeStruct((groups // 2, rows, side), f32)
@@ -108,12 +129,12 @@
     return pl.pallas_call(
         functools.partial(partial_kernel, groups),
         out_shape=(kept, sent, panel),
-        in_specs=[smem, smem] + [vmem] * (3 + groups + groups // 2),
+        in_specs=[smem] + [vmem] * (3 + groups + groups // 2),
         out_specs=(vmem, vmem, vmem),
         scratch_shapes=[pltpu.VMEM((groups, rows, side), f32)],
         compiler_params=room,
         name="partial_image",
-    )(place, count, samples, diag, high, low, *pieces, *beside)
+    )(guide, samples, diag, high, low, *pieces, *beside)
 
 
 def middle_kernel(own_image, other_image, samples, diag, swapped, *refs):
@@ -172,44 +193,43 @@
 
 
 def slots_kernel(
-    place, count, left_high, left_low, panel, first, second, tiles, out, high, low, ready, sems
+    guide, left_high, left_low, panel, first, second, tiles, out, high, low, ready, sems
 ):
     groups = panel.shape[0]
     rows = panel.shape[1] // 2
     half = high.shape[1] // 2
-    parity = lax.rem(lax.axis_index("row"), 2)
     for ref in (high, low):
         for start in (rows, half + rows):
             blank = jnp.zeros((groups, half - rows, high.shape[2]), bf16)
             ref[:, start : start + half - rows] = blank
     for pair in range(groups // 2):
         for turn, piece in enumerate((first, second)):
-            block = 2 * pair + (1 - parity if turn else parity)
+            block = 2 * pair + guide[3, turn]
             high[block, :rows], low[block, :rows] = halves(piece[pair])
     high[:, half : half + rows] = panel[:, :rows]
     low[:, half : half + rows] = panel[:, rows:]
     dims = ((1,), (0,))
     copies = []
     for slot in range(tiles.shape[0]):
-        left, right = place[0, slot], place[1, slot]
+        left, right = guide[0, slot], guide[1, slot]
         gradient = dot(left_high[left], high[right], dims)
         gradient += dot(left_low[left], high[right], dims)
         gradient += dot(left_high[left], low[right], dims)
         value = soft_limit(tiles[slot] - gradient * (step_size / (2.0 * rows)))
-        ready[slot] = jnp.where(slot < count[0, 0], value, 0.0)
+        ready[slot] = jnp.where(slot < guide[4, 0], value, 0.0)
         copies.append(pltpu.make_async_copy(ready.at[slot], out.at[slot], sems.at[slot]))
         copies[-1].start()
     for copy in copies:
         copy.wait()
 
 
-def update_slots(place, count, left_high, left_low, panel, first, second, tiles):
+def update_slots(guide, left_high, left_low, panel, first, second, tiles):
     slots, side, _ = tiles.shape
     groups, _, depth = left_high.shape
     return pl.pallas_call(
         slots_kernel,
         out_shape=jax.ShapeDtypeStruct(tiles.shape, f32),
-        in_specs=[smem, smem] + [vmem] * 6,
+        in_specs=[smem] + [vmem] * 6,
         out_specs=hbm,
         scratch_shapes=[
             pltpu.VMEM((groups, depth, side), bf16),
@@ -219,7 +239,7 @@
         ],
         compiler_params=room,
         name="update_slots",
-    )(place, count, left_high, left_low, panel, first, second, tiles)
+    )(guide, left_high, left_low, panel, first, second, tiles)
 
 
 def on_device(samples, diag_tiles, omega_slots, tile_pos, tile_count):
@@ -230,41 +250,36 @@
     place = tile_pos.reshape(slots, 2).T
     span = range(groups)
 
-    def from_row_line(turn):
+    def links(source, turn):
         return [
-            (line * groups + j, (j - turn) % groups * groups + line) for line in span for j in span
+            (line * groups + source(turn, row, line) % groups, row * groups + line)
+            for line in span
+            for row in span
         ]
 
     def around(size, turn):
         return [(j, (j + turn) % size) for j in range(size)]
 
-    col_pieces = [lax.ppermute(samples, grid_axes, from_row_line(turn)) for turn in span]
+    col_pieces = [
+        lax.ppermute(samples, grid_axes, links(sample_source, turn)) for turn in span
+    ]
     beside = [lax.ppermute(samples, "col", around(cols, turn)) for turn in range(1, cols)]
-    place, own, own_diag, held, high, low = prepare(place, samples, diag_tiles, tiles)
-    kept, sent, panel = partial_image(
-        place, tile_count, own, own_diag, high, low, col_pieces, beside
-    )
+    guide, own, own_diag, held, high, low = prepare(
+        groups, place, tile_count, samples, diag_tiles, tiles
+    )
+    kept, sent, panel = partial_image(guide, own, own_diag, high, low, col_pieces, beside)
     swapped = lax.ppermute(sent, "rep", around(2, 1))
     chip = kept + swapped[:cols]
     image = chip
     for turn in range(1, cols):
         image = image + lax.ppermute(chip, "col", around(cols, turn))
 
-    def to_row(turn):
-        return [
-            (line * groups + j, (groups - 1 - j if turn else j) * groups + line)
-            for line in span
-            for j in span
-        ]
-
-    first, second = [lax.ppermute(image, grid_axes, to_row(turn)) for turn in range(2)]
+    first, second = [
+        lax.ppermute(image, grid_axes, links(image_source, turn)) for turn in range(2)
+    ]
     other = lax.ppermute(image, "rep", around(2, 1))
-    left_high, left_low, new_diag = middle(
-        image, other, own, own_diag, swapped, beside
-    )
-    new_slots = update_slots(
-        place, tile_count, left_high, left_low, panel, first, second, held
-    )
+    left_high, left_low, new_diag = middle(image, other, own, own_diag, swapped, beside)
+    new_slots = update_slots(guide, left_high, left_low, panel, first, second, held)
     return new_slots.reshape(omega_slots.shape), new_diag
 
 

time: 44.3 us -> 41.7 us (0.941)
  starting transfers between devices: 20.3 us -> 17 us
  Pallas kernels: 7.6 us -> 6.48 us
  waiting for transfers between devices: 14.7 us -> 15.5 us
  local copies, waits for them, and re-layouts: 0 us -> 0.67 us
    ppermute x6, starting transfers between devices: 18.5 us -> 16.4 us  [the longest x4 10.5 us: on_device(): lax.ppermute(samples, grid_axes, links(sample_source, turn))]
    ppermute x1, starting transfers between devices: 1.15 us -> 0.44 us  [on_device(): image = image + lax.ppermute(chip, 'col', around(cols, turn))]
    unnamed x0 -> x2, local copies, waits for them, and re-layouts: none -> 0.67 us
    pallas_call x1, Pallas kernels: 1.43 us -> 0.89 us  [partial_image(): pl.pallas_call(functools.partial(partial_kernel, groups), out_shape=(kept...]
    pallas_call x1, Pallas kernels: 2.61 us -> 2.1 us  [update_slots(): pl.pallas_call(slots_kernel, out_shape=jax.ShapeDtypeStruct(tiles.shape,...]
    ppermute x1, waiting for transfers between devices: 6.1 us -> 6.57 us  [on_device(): image = image + lax.ppermute(chip, 'col', around(cols, turn))]
    ppermute x1, starting transfers between devices: 0.52 us -> 0.07 us  [on_device(): swapped = lax.ppermute(sent, 'rep', around(2, 1))]
  transfers between devices with their start and end apart: 10 -> 10, of which waited for: 4 -> 5; matrix products, arithmetic and copies ran while one was open for 0% -> 0% of each run, Pallas kernels for 8% -> 8%
where the time goes in v6:
time: 41.7 us; the launch traced here: 41.2 us
  starting transfers between devices  17 us (41%)
  waiting for transfers between devices  15.5 us (37%)
  Pallas kernels  6.48 us (16%)
  between operations  1.4 us (3%)
  local copies, waits for them, and re-layouts  0.67 us (2%)
    ppermute x4, starting transfers between devices, on_device(): lax.ppermute(samples, grid_axes, links(sample_source, turn))  10.5 us
    ppermute x2, waiting for transfers between devices, on_device(): lax.ppermute(image, grid_axes, links(image_source, turn))  6.98 us
    ppermute x1, waiting for transfers between devices, on_device(): image = image + lax.ppermute(chip, 'col', around(cols, turn))  6.57 us
    ppermute x2, starting transfers between devices, on_device(): lax.ppermute(image, grid_axes, links(image_source, turn))  5.86 us
    pallas_call x1, Pallas kernels, prepare(): pl.pallas_call(functools.partial(prepare_kernel, groups), out_shape=(pltp...  2.25 us
    pallas_call x1, Pallas kernels, update_slots(): pl.pallas_call(slots_kernel, out_shape=jax.ShapeDtypeStruct(tiles.shape,...  2.1 us
    ppermute x1, waiting for transfers between devices, on_device(): swapped = lax.ppermute(sent, 'rep', around(2, 1))  1.71 us
    pallas_call x1, Pallas kernels, middle(): pl.pallas_call(middle_kernel, out_shape=(left, left, jax.ShapeDtypeStruct...  1.25 us
  transfers between devices with their start and end apart: 10, of which 5 were waited for; matrix products, arithmetic and copies ran while one was open for 0% of the time, Pallas kernels for 8%

profile of v6, /device:TPU:6, one launch (start us, length us, event | category | flops | bytes accessed | tf_op | source)
XLA Modules:
  0.0 41.2 jit_solution(11235419692309030757)
XLA Ops:
  0.6 0.6 %collective-permute-start.2 = (f32[96,256]{1,0:T(8,128)}, f32[96,256]{1,0:T(8,128)S(1)}, u32[]{:S(2)}, u32[]{:S(2)}) collective-permute-start(f32[96,256]{1,0:T(8,128)} %refs_0_.1), channel_id=1, source_target_pairs={{2,0},{1,4},{0,8},{3,12},{4,1},{7,5},{6,9},{5,13},{10,2},{9,6},{8,... | collective-permute-start | bytes 294920 | tf_op jit(solution)/shard_map/ppermute | solution.py:264
  1.2 1.1 %collective-permute-start.1 = (f32[96,256]{1,0:T(8,128)}, f32[96,256]{1,0:T(8,128)S(1)}, u32[]{:S(2)}, u32[]{:S(2)}) collective-permute-start(f32[96,256]{1,0:T(8,128)} %refs_0_.1), channel_id=1, source_target_pairs={{3,0},{2,4},{1,8},{0,12},{5,1},{4,5},{7,9},{6,13},{11,2},{10,6},{9... | collective-permute-start | bytes 294920 | tf_op jit(solution)/shard_map/ppermute | solution.py:264
  2.3 5.4 %collective-permute-start = (f32[96,256]{1,0:T(8,128)}, f32[96,256]{1,0:T(8,128)S(1)}, u32[]{:S(2)}, u32[]{:S(2)}) collective-permute-start(f32[96,256]{1,0:T(8,128)} %refs_0_.1), channel_id=1, source_target_pairs={{0,0},{3,4},{2,8},{1,12},{6,1},{5,5},{4,9},{7,13},{8,2},{11,6},{10... | collective-permute-start | bytes 294920 | tf_op jit(solution)/shard_map/ppermute | solution.py:264
  7.7 0.1 collective-permute-start.4
  7.8 3.4 %collective-permute-start.3 = (f32[96,256]{1,0:T(8,128)}, f32[96,256]{1,0:T(8,128)S(1)}, u32[]{:S(2)}, u32[]{:S(2)}) collective-permute-start(f32[96,256]{1,0:T(8,128)} %refs_0_.1), channel_id=1, source_target_pairs={{1,0},{0,4},{3,8},{2,12},{7,1},{6,5},{5,9},{4,13},{9,2},{8,6},{11,... | collective-permute-start | bytes 294920 | tf_op jit(solution)/shard_map/ppermute | solution.py:264
  11.9 0.0 copy-start
  11.9 0.7 %copy-done = s32[1,1,8,2]{2,3,1,0:T(2,128)S(1)} copy-done((s32[1,1,8,2]{2,3,1,0:T(2,128)S(1)}, s32[1,1,8,2]{2,3,1,0:T(2,128)}, u32[]{:S(2)}) %copy-start) | copy-done | bytes 88
  12.6 2.2 %prepare.1 = (s32[5,8]{1,0:T(8,128)S(4)}, f32[96,256]{1,0:T(8,128)S(1)}, f32[1,256,256]{2,1,0:T(8,128)S(1)}, f32[8,256,256]{2,1,0:T(8,128)S(1)}, bf16[8,256,256]...) custom-call(s32[2,8]{1,0:T(2,128)S(1)} %bitcast.5, s32[1,1]{1,0:T(1,128)S(6)} %copy.7.count, f32[96,256]{1,0:T(8,128)} %refs_0_.1, ...), custom_call_target="tpu_custom_call" | custom-call | tf_op jit(solution)/shard_map/prepare/pallas_call | solution.py:77
  14.8 0.0 collective-permute-done.2.refs_2_
  14.8 0.0 collective-permute-done.1.refs_1_
  14.8 0.0 collective-permute-done.refs_0_
  14.9 0.0 collective-permute-done.4.refs_4_.refs_0_
  14.9 0.3 collective-permute-done.3.refs_3_
  15.1 0.9 %partial_image.1 = (f32[2,96,256]{2,1,0:T(8,128)S(1)}, f32[4,96,256]{2,1,0:T(8,128)S(1)}, bf16[4,192,256]{2,1,0:T(8,128)(2,1)S(1)}) custom-call(s32[5,8]{1,0:T(8,128)S(4)} %get-tuple-element.14.guide, f32[96,256]{1,0:T(8,128)S(1)} %get-tuple-element.15.samples, f32[1,256,256]{2,1,0:T(8,128)S(1)} %get-tuple-element.16.diag, ...), custom_call_target="tpu_custom_call" | custom-call | tf_op jit(solution)/shard_map/partial_image/pallas_call | solution.py:129
  16.0 0.1 collective-permute-start.5
  16.1 1.7 %collective-permute-done.5.swapped = f32[4,96,256]{2,1,0:T(8,128)S(1)} collective-permute-done((f32[4,96,256]{2,1,0:T(8,128)S(1)}, f32[4,96,256]{2,1,0:T(8,128)S(1)}, u32[]{:S(2)}, u32[]{:S(2)}) %collective-permute-start.5) | collective-permute-done | bytes 393248 | tf_op jit(solution)/shard_map/ppermute | solution.py:271
  17.9 0.4 %collective-permute-start.6 = (f32[2,96,256]{2,1,0:T(8,128)S(1)}, f32[2,96,256]{2,1,0:T(8,128)S(1)}, u32[]{:S(2)}, u32[]{:S(2)}) collective-permute-start(f32[2,96,256]{2,1,0:T(8,128)S(1)} %slice_add_fusion), channel_id=1, source_target_pairs={{0,2},{2,0},{1,3},{3,1},{4,6},{6,4},{5,7},{7,5},{8,10},{10,8},{9,1... | collective-permute-start | bytes 589832 | tf_op jit(solution)/shard_map/ppermute | solution.py:275
  18.3 6.6 %collective-permute-done.6 = f32[2,96,256]{2,1,0:T(8,128)S(1)} collective-permute-done((f32[2,96,256]{2,1,0:T(8,128)S(1)}, f32[2,96,256]{2,1,0:T(8,128)S(1)}, u32[]{:S(2)}, u32[]{:S(2)}) %collective-permute-start.6) | collective-permute-done | bytes 196640 | tf_op jit(solution)/shard_map/ppermute | solution.py:275
  24.9 0.1 collective-permute-start.7
  25.0 1.3 %collective-permute-start.9 = (f32[2,96,256]{2,1,0:T(8,128)S(1)}, f32[2,96,256]{2,1,0:T(8,128)S(1)}, u32[]{:S(2)}, u32[]{:S(2)}) collective-permute-start(f32[2,96,256]{2,1,0:T(8,128)S(1)} %add.7.own_image), channel_id=1, source_target_pairs={{3,0},{2,4},{1,8},{0,12},{5,1},{4,5},{7,9},{6,13},{11,2},{10,6},{9... | collective-permute-start | bytes 589832 | tf_op jit(solution)/shard_map/ppermute | solution.py:278
  26.3 4.6 %collective-permute-start.8 = (f32[2,96,256]{2,1,0:T(8,128)S(1)}, f32[2,96,256]{2,1,0:T(8,128)S(1)}, u32[]{:S(2)}, u32[]{:S(2)}) collective-permute-start(f32[2,96,256]{2,1,0:T(8,128)S(1)} %add.7.own_image), channel_id=1, source_target_pairs={{0,0},{1,4},{2,8},{3,12},{6,1},{7,5},{4,9},{5,13},{8,2},{9,6},{10,... | collective-permute-start | bytes 589832 | tf_op jit(solution)/shard_map/ppermute | solution.py:278
  30.8 0.0 collective-permute-done.7.other_image
  30.9 1.2 %middle.1 = (bf16[4,256,256]{2,1,0:T(8,128)(2,1)S(1)}, bf16[4,256,256]{2,1,0:T(8,128)(2,1)S(1)}, f32[1,256,256]{2,1,0:T(8,128)}) custom-call(f32[2,96,256]{2,1,0:T(8,128)S(1)} %add.7.own_image, f32[2,96,256]{2,1,0:T(8,128)S(1)} %collective-permute-done.7.other_image, f32[96,256]{1,0:T(8,128)S(1)} %get-tuple-element.15.samples, ...), custom_call_target="tpu_custom_call" | custom-call | tf_op jit(solution)/shard_map/middle/pallas_call | solution.py:184
  32.1 5.1 %collective-permute-done.9.second = f32[2,96,256]{2,1,0:T(8,128)S(1)} collective-permute-done((f32[2,96,256]{2,1,0:T(8,128)S(1)}, f32[2,96,256]{2,1,0:T(8,128)S(1)}, u32[]{:S(2)}, u32[]{:S(2)}) %collective-permute-start.9) | collective-permute-done | bytes 196640 | tf_op jit(solution)/shard_map/ppermute | solution.py:278
  37.3 1.8 %collective-permute-done.8.first = f32[2,96,256]{2,1,0:T(8,128)S(1)} collective-permute-done((f32[2,96,256]{2,1,0:T(8,128)S(1)}, f32[2,96,256]{2,1,0:T(8,128)S(1)}, u32[]{:S(2)}, u32[]{:S(2)}) %collective-permute-start.8) | collective-permute-done | bytes 196640 | tf_op jit(solution)/shard_map/ppermute | solution.py:278
  39.1 2.1 %update_slots.1 = f32[8,256,256]{2,1,0:T(8,128)} custom-call(s32[5,8]{1,0:T(8,128)S(4)} %get-tuple-element.14.guide, bf16[4,256,256]{2,1,0:T(8,128)(2,1)S(1)} %get-tuple-element.21.left_high, bf16[4,256,256]{2,1,0:T(8,128)(2,1)S(1)} %get-tuple-element.22.left_low, bf16[4,192,256]{2,1,0:T(8,128)(2,1)S(1)} %get-tuple-element.23.panel, ...), custom_call_target="tpu_custom_call" | custom-call | tf_op jit(solution)/shard_map/update_slots/pallas_call | solution.py:229
  (2 shorter events, 0.1 us)
Async XLA Ops:
  0.6 14.2 %collective-permute-start.2 = (f32[96,256]{1,0:T(8,128)}, f32[96,256]{1,0:T(8,128)S(1)}, u32[]{:S(2)}, u32[]{:S(2)}) collective-permute-start(f32[96,256]{1,0:T(8,128)} %refs_0_.1), channel_id=1, source_target_pairs={{2,0},{1,4},{0,8},{3,12},{4,1},{7,5},{6,9},{5,13},{10,2},{9,6},{8,... | collective-permute-start | bytes 294920 | tf_op jit(solution)/shard_map/ppermute | solution.py:264
  1.2 13.6 %collective-permute-start.1 = (f32[96,256]{1,0:T(8,128)}, f32[96,256]{1,0:T(8,128)S(1)}, u32[]{:S(2)}, u32[]{:S(2)}) collective-permute-start(f32[96,256]{1,0:T(8,128)} %refs_0_.1), channel_id=1, source_target_pairs={{3,0},{2,4},{1,8},{0,12},{5,1},{4,5},{7,9},{6,13},{11,2},{10,6},{9... | collective-permute-start | bytes 294920 | tf_op jit(solution)/shard_map/ppermute | solution.py:264
  2.3 12.5 %collective-permute-start = (f32[96,256]{1,0:T(8,128)}, f32[96,256]{1,0:T(8,128)S(1)}, u32[]{:S(2)}, u32[]{:S(2)}) collective-permute-start(f32[96,256]{1,0:T(8,128)} %refs_0_.1), channel_id=1, source_target_pairs={{0,0},{3,4},{2,8},{1,12},{6,1},{5,5},{4,9},{7,13},{8,2},{11,6},{10... | collective-permute-start | bytes 294920 | tf_op jit(solution)/shard_map/ppermute | solution.py:264
  7.7 7.1 %collective-permute-start.4 = (f32[96,256]{1,0:T(8,128)}, f32[96,256]{1,0:T(8,128)S(1)}, u32[]{:S(2)}, u32[]{:S(2)}) collective-permute-start(f32[96,256]{1,0:T(8,128)} %refs_0_.1), channel_id=1, source_target_pairs={{0,2},{2,0},{1,3},{3,1},{4,6},{6,4},{5,7},{7,5},{8,10},{10,8},{9,1... | collective-permute-start | bytes 294920 | tf_op jit(solution)/shard_map/ppermute | solution.py:266
  7.8 7.3 %collective-permute-start.3 = (f32[96,256]{1,0:T(8,128)}, f32[96,256]{1,0:T(8,128)S(1)}, u32[]{:S(2)}, u32[]{:S(2)}) collective-permute-start(f32[96,256]{1,0:T(8,128)} %refs_0_.1), channel_id=1, source_target_pairs={{1,0},{0,4},{3,8},{2,12},{7,1},{6,5},{5,9},{4,13},{9,2},{8,6},{11,... | collective-permute-start | bytes 294920 | tf_op jit(solution)/shard_map/ppermute | solution.py:264
  11.9 0.7 %copy-start = (s32[1,1,8,2]{2,3,1,0:T(2,128)S(1)}, s32[1,1,8,2]{2,3,1,0:T(2,128)}, u32[]{:S(2)}) copy-start(s32[1,1,8,2]{2,3,1,0:T(2,128)} %param.8) | copy-start | bytes 196
  16.0 1.8 %collective-permute-start.5 = (f32[4,96,256]{2,1,0:T(8,128)S(1)}, f32[4,96,256]{2,1,0:T(8,128)S(1)}, u32[]{:S(2)}, u32[]{:S(2)}) collective-permute-start(f32[4,96,256]{2,1,0:T(8,128)S(1)} %get-tuple-element.20), channel_id=1, source_target_pairs={{0,1},{1,0},{2,3},{3,2},{4,5},{5,4},{6,7},{7,6},{8,9},{9,8},{10,11... | collective-permute-start | bytes 1179656 | tf_op jit(solution)/shard_map/ppermute | solution.py:271
  17.9 7.0 %collective-permute-start.6 = (f32[2,96,256]{2,1,0:T(8,128)S(1)}, f32[2,96,256]{2,1,0:T(8,128)S(1)}, u32[]{:S(2)}, u32[]{:S(2)}) collective-permute-start(f32[2,96,256]{2,1,0:T(8,128)S(1)} %slice_add_fusion), channel_id=1, source_target_pairs={{0,2},{2,0},{1,3},{3,1},{4,6},{6,4},{5,7},{7,5},{8,10},{10,8},{9,1... | collective-permute-start | bytes 589832 | tf_op jit(solution)/shard_map/ppermute | solution.py:275
  24.9 6.0 %collective-permute-start.7 = (f32[2,96,256]{2,1,0:T(8,128)S(1)}, f32[2,96,256]{2,1,0:T(8,128)S(1)}, u32[]{:S(2)}, u32[]{:S(2)}) collective-permute-start(f32[2,96,256]{2,1,0:T(8,128)S(1)} %add.7.own_image), channel_id=1, source_target_pairs={{0,1},{1,0},{2,3},{3,2},{4,5},{5,4},{6,7},{7,6},{8,9},{9,8},{10,11... | collective-permute-start | bytes 589832 | tf_op jit(solution)/shard_map/ppermute | solution.py:280
  25.0 12.3 %collective-permute-start.9 = (f32[2,96,256]{2,1,0:T(8,128)S(1)}, f32[2,96,256]{2,1,0:T(8,128)S(1)}, u32[]{:S(2)}, u32[]{:S(2)}) collective-permute-start(f32[2,96,256]{2,1,0:T(8,128)S(1)} %add.7.own_image), channel_id=1, source_target_pairs={{3,0},{2,4},{1,8},{0,12},{5,1},{4,5},{7,9},{6,13},{11,2},{10,6},{9... | collective-permute-start | bytes 589832 | tf_op jit(solution)/shard_map/ppermute | solution.py:278
  26.3 12.8 %collective-permute-start.8 = (f32[2,96,256]{2,1,0:T(8,128)S(1)}, f32[2,96,256]{2,1,0:T(8,128)S(1)}, u32[]{:S(2)}, u32[]{:S(2)}) collective-permute-start(f32[2,96,256]{2,1,0:T(8,128)S(1)} %add.7.own_image), channel_id=1, source_target_pairs={{0,0},{1,4},{2,8},{3,12},{6,1},{7,5},{4,9},{5,13},{8,2},{9,6},{10,... | collective-permute-start | bytes 589832 | tf_op jit(solution)/shard_map/ppermute | solution.py:278

commit v7 on v6

--- a/solution.py
+++ b/solution.py
@@ -33,79 +33,84 @@
     return values - jnp.clip(values, -limit_value, limit_value)
 
 
-def sample_source(turn, row, own):
-    return 2 * own - row - turn
-
-
-def image_source(turn, row, own):
-    return 2 * own - 1 - row if turn else row - 2 * own
-
-
-def prepare_kernel(groups, place, count, *refs):
-    arrays, (guide, *held), (high, low, sems) = refs[:3], refs[3:7], refs[7:]
-    tiles = held[2]
+def first_source(row, own, groups):
+    rep = (row // 2 ^ row ^ own // (groups // 2)) & 1
+    return 2 * (row // 2 ^ rep) + rep
+
+
+def sample_source(turn, row, own, groups):
+    return first_source(row, own, groups) ^ (2 * turn + turn % 2)
+
+
+def image_source(turn, row, own, groups):
+    return first_source(row, own, groups) ^ (turn * (groups - 1))
+
+
+def prepare_kernel(groups, *refs):
+    place, count, *arrays = refs[:4]
+    guide, *held, high, low, spots, live, sems = refs[4:]
+    tiles = held[1]
     slots = tiles.shape[0]
-    copies = [
-        pltpu.make_async_copy(arrays[2].at[slot], tiles.at[slot], sems.at[slot])
-        for slot in range(slots)
-    ]
-    for turn in range(2):
-        copies.append(pltpu.make_async_copy(arrays[turn], held[turn], sems.at[slots + turn]))
+    pairs = [(place, spots), (count, live), (arrays[0], held[0])]
+    pairs += [(arrays[1].at[slot], tiles.at[slot]) for slot in range(slots)]
+    copies = [pltpu.make_async_copy(*pair, sems.at[i]) for i, pair in enumerate(pairs)]
     for copy in copies:
         copy.start()
-    for slot in range(slots):
-        guide[0, slot] = place[0, slot]
-        guide[1, slot] = place[1, slot]
     row = lax.axis_index("row")
     own = lax.axis_index("col") * 2 + lax.axis_index("rep")
-    for turn in range(groups):
-        guide[2, turn] = lax.rem(sample_source(turn, row, own) + 4 * groups, groups)
+    for turn in range(groups // 2):
+        guide[2, turn] = sample_source(turn, row, own, groups)
     for turn in range(2):
-        guide[3, turn] = lax.rem(image_source(turn, row, own) + 4 * groups, 2)
-    guide[4, 0] = count[0, 0]
+        guide[3, turn] = image_source(turn, row, own, groups) & 1
     for slot in range(slots):
-        copies[slot].wait()
+        copies[3 + slot].wait()
         high[slot], low[slot] = halves(tiles[slot])
-    for copy in copies[slots:]:
+    for copy in copies[:3]:
         copy.wait()
-
-
-def prepare(groups, place, count, *arrays):
-    width = max(place.shape[1], groups)
-    held = [jax.ShapeDtypeStruct(x.shape, x.dtype) for x in arrays]
+    for slot in range(slots):
+        guide[0, slot] = spots[0, slot]
+        guide[1, slot] = spots[1, slot]
+    guide[4, 0] = live[0, 0]
+
+
+def prepare(groups, *arrays):
+    slots = arrays[-1].shape[0]
+    width = max(slots, groups)
+    held = [jax.ShapeDtypeStruct(x.shape, x.dtype) for x in arrays[2:]]
     half = jax.ShapeDtypeStruct(arrays[-1].shape, bf16)
     return pl.pallas_call(
         functools.partial(prepare_kernel, groups),
         out_shape=(pltpu.SMEM((5, width), jnp.int32), *held, half, half),
-        in_specs=[smem] * 2 + [hbm] * 3,
-        out_specs=(smem,) + (vmem,) * 5,
-        scratch_shapes=[pltpu.SemaphoreType.DMA((arrays[-1].shape[0] + 2,))],
+        in_specs=[hbm, vmem, hbm, hbm],
+        out_specs=(smem,) + (vmem,) * 4,
+        scratch_shapes=[
+            pltpu.SMEM(arrays[0].shape, jnp.int32),
+            pltpu.SMEM(arrays[1].shape, jnp.int32),
+            pltpu.SemaphoreType.DMA((slots + 3,)),
+        ],
         compiler_params=room,
         name="prepare",
-    )(
-        place,
-        count,
-        *[pltpu.with_memory_space_constraint(x, pltpu.HBM) for x in arrays],
-    )
-
-
-def partial_kernel(groups, guide, samples, diag, high, low, *refs):
-    pieces = refs[:groups]
-    beside = refs[groups:-4]
+    )(*[x if i == 1 else pltpu.with_memory_space_constraint(x, pltpu.HBM) for i, x in enumerate(arrays)])
+
+
+def partial_kernel(guide, samples, diag, high, low, *refs):
+    pieces = refs[:-4]
+    groups = 2 * len(pieces)
     kept, sent, panel, total = refs[-4:]
     col = lax.axis_index("col")
     rep = lax.axis_index("rep")
-    rows = samples.shape[0]
-    for turn in range(groups):
-        block = guide[2, turn]
-        panel[block, :rows], panel[block, rows:] = halves(pieces[turn][...])
+    rows = samples.shape[1]
+    for turn, piece in enumerate(pieces):
+        for half in range(2):
+            block = guide[2, turn] ^ half
+            panel[block, :rows], panel[block, rows:] = halves(piece[half])
     total[...] = jnp.zeros_like(total)
 
     def term(x_high, both, w_high, w_low, dims):
         wide = dot(both, w_high, dims)
         return wide[:rows] + wide[rows:] + dot(x_high, w_low, dims)
 
-    own_high, own_low = halves(samples[...])
+    own_high, own_low = halves(samples[0])
     total[col * 2 + rep] = term(
         own_high, jnp.concatenate([own_high, own_low], axis=0), *halves(diag[0]), ((1,), (0,))
     )
@@ -116,44 +121,41 @@
     for pair in range(groups // 2):
         kept[pair] = total[2 * pair + rep]
         sent[pair] = total[2 * pair + 1 - rep]
-    for turn, piece in enumerate((samples, *beside)):
-        sent[groups // 2 + turn] = piece[...]
-
-
-def partial_image(guide, samples, diag, high, low, pieces, beside):
-    groups = len(pieces)
-    rows, side = samples.shape
-    kept = jax.ShapeDtypeStruct((groups // 2, rows, side), f32)
-    sent = jax.ShapeDtypeStruct((groups, rows, side), f32)
+
+
+def partial_image(guide, samples, diag, high, low, pieces):
+    groups = 2 * len(pieces)
+    _, rows, side = samples.shape
+    half = jax.ShapeDtypeStruct((groups // 2, rows, side), f32)
     panel = jax.ShapeDtypeStruct((groups, 2 * rows, side), bf16)
     return pl.pallas_call(
-        functools.partial(partial_kernel, groups),
-        out_shape=(kept, sent, panel),
-        in_specs=[smem] + [vmem] * (3 + groups + groups // 2),
+        partial_kernel,
+        out_shape=(half, half, panel),
+        in_specs=[smem] + [vmem] * (4 + len(pieces)),
         out_specs=(vmem, vmem, vmem),
         scratch_shapes=[pltpu.VMEM((groups, rows, side), f32)],
         compiler_params=room,
         name="partial_image",
-    )(guide, samples, diag, high, low, *pieces, *beside)
-
-
-def middle_kernel(own_image, other_image, samples, diag, swapped, *refs):
-    beside = refs[:-5]
+    )(guide, samples, diag, high, low, *pieces)
+
+
+def middle_kernel(own_image, other_image, diag, *refs):
+    samples = refs[:-5]
     high, low, new_diag, shifted, sem = refs[-5:]
     pairs = own_image.shape[0]
     rep = lax.axis_index("rep")
     col = lax.axis_index("col")
-    rows, side = samples.shape
+    _, rows, side = samples[0].shape
     half = high.shape[2] // 2
     blank = jnp.zeros((side, half - rows), bf16)
-    for turn, piece in enumerate((samples, *beside)):
+    for turn, piece in enumerate(samples):
         line = 2 * lax.rem(col + pairs - turn, pairs)
-        for block, values in ((line + rep, piece[...]), (line + 1 - rep, swapped[pairs + turn])):
-            for ref, part in zip((high, low), halves(values.T)):
+        for block, place in ((line + rep, 0), (line + 1 - rep, 1)):
+            for ref, part in zip((high, low), halves(piece[place].T)):
                 ref[block, :, :rows] = part
                 ref[block, :, rows:half] = blank
                 ref[block, :, half + rows :] = blank
-    left_high, left_low = halves(samples[...].T)
+    left_high, left_low = halves(samples[0][0].T)
     right_high, right_low = halves(own_image[col])
     dims = ((1,), (0,))
     one_side = dot(left_high, right_high, dims) + dot(left_low, right_high, dims)
@@ -176,20 +178,20 @@
     copy.wait()
 
 
-def middle(own_image, other_image, samples, diag, swapped, beside):
-    groups = swapped.shape[0]
-    rows, side = samples.shape
+def middle(own_image, other_image, diag, samples):
+    pairs, rows, side = own_image.shape
+    groups = 2 * pairs
     depth = 2 * -(-rows // 128) * 128
     left = jax.ShapeDtypeStruct((groups, side, depth), bf16)
     return pl.pallas_call(
         middle_kernel,
         out_shape=(left, left, jax.ShapeDtypeStruct(diag.shape, f32)),
-        in_specs=[vmem] * (5 + len(beside)),
+        in_specs=[vmem] * (3 + len(samples)),
         out_specs=(vmem, vmem, hbm),
         scratch_shapes=[pltpu.VMEM(diag.shape, f32), pltpu.SemaphoreType.DMA],
         compiler_params=room,
         name="middle",
-    )(own_image, other_image, samples, diag, swapped, *beside)
+    )(own_image, other_image, diag, *samples)
 
 
 def slots_kernel(
@@ -252,7 +254,7 @@
 
     def links(source, turn):
         return [
-            (line * groups + source(turn, row, line) % groups, row * groups + line)
+            (line * groups + source(turn, row, line, groups), row * groups + line)
             for line in span
             for row in span
         ]
@@ -260,25 +262,24 @@
     def around(size, turn):
         return [(j, (j + turn) % size) for j in range(size)]
 
+    pair = jnp.stack([samples, lax.ppermute(samples, "rep", around(2, 1))])
     col_pieces = [
-        lax.ppermute(samples, grid_axes, links(sample_source, turn)) for turn in span
+        lax.ppermute(pair, grid_axes, links(sample_source, turn)) for turn in range(cols)
     ]
-    beside = [lax.ppermute(samples, "col", around(cols, turn)) for turn in range(1, cols)]
-    guide, own, own_diag, held, high, low = prepare(
-        groups, place, tile_count, samples, diag_tiles, tiles
-    )
-    kept, sent, panel = partial_image(guide, own, own_diag, high, low, col_pieces, beside)
-    swapped = lax.ppermute(sent, "rep", around(2, 1))
-    chip = kept + swapped[:cols]
+    guide, own_diag, held, high, low = prepare(groups, place, tile_count, diag_tiles, tiles)
+    kept, sent, panel = partial_image(guide, pair, own_diag, high, low, col_pieces)
+    chip = kept + lax.ppermute(sent, "rep", around(2, 1))
     image = chip
     for turn in range(1, cols):
         image = image + lax.ppermute(chip, "col", around(cols, turn))
 
+    late, image = lax.optimization_barrier((pair, image))
+    beside = [lax.ppermute(late, "col", around(cols, turn)) for turn in range(1, cols)]
     first, second = [
         lax.ppermute(image, grid_axes, links(image_source, turn)) for turn in range(2)
     ]
     other = lax.ppermute(image, "rep", around(2, 1))
-    left_high, left_low, new_diag = middle(image, other, own, own_diag, swapped, beside)
+    left_high, left_low, new_diag = middle(image, other, own_diag, [pair, *beside])
     new_slots = update_slots(guide, left_high, left_low, panel, first, second, held)
     return new_slots.reshape(omega_slots.shape), new_diag
 

time: 41.7 us -> 40.5 us (0.971)
  starting transfers between devices: 17 us -> 13.7 us
  waiting for transfers between devices: 15.5 us -> 18.3 us
  other arithmetic: 0.05 us -> 0.96 us
  local copies, waits for them, and re-layouts: 0.67 us -> 0 us
  Pallas kernels: 6.48 us -> 5.94 us
    ppermute x6 -> x5, waiting for transfers between devices: 1.99 us -> 9.28 us  [the longest x2 3.63 us: on_device(): lax.ppermute(pair, grid_axes, links(sample_source, turn))]
    ppermute x2, waiting for transfers between devices: 6.98 us -> 2.05 us  [on_device(): lax.ppermute(image, grid_axes, links(image_source, turn))]
    ppermute x6 -> x5, starting transfers between devices: 10.7 us -> 6.93 us  [the longest x2 6.44 us: on_device(): lax.ppermute(pair, grid_axes, links(sample_source, turn))]
    another operation x0 -> x1, other arithmetic: none -> 0.91 us  [on_device(): pair = jnp.stack([samples, lax.ppermute(samples, 'rep', around(2, 1))])]
    ppermute x2, starting transfers between devices: 5.86 us -> 6.73 us  [on_device(): lax.ppermute(image, grid_axes, links(image_source, turn))]
    unnamed x2 -> x0, local copies, waits for them, and re-layouts: 0.67 us -> none
    pallas_call x1, Pallas kernels: 2.25 us -> 1.76 us  [prepare(): pl.pallas_call(functools.partial(prepare_kernel, groups), out_shape=(pltp...]
  transfers between devices with their start and end apart: 10 -> 9, of which waited for: 5 -> 7; matrix products, arithmetic and copies ran while one was open for 0% -> 0% of each run, Pallas kernels for 8% -> 7%
where the time goes in v7:
time: 40.5 us; the launch traced here: 40.3 us
  waiting for transfers between devices  18.3 us (45%)
  starting transfers between devices  13.7 us (34%)
  Pallas kernels  5.94 us (15%)
  between operations  1.36 us (3%)
  other arithmetic  0.96 us (2%)
    ppermute x1, waiting for transfers between devices, on_device(): image = image + lax.ppermute(chip, 'col', around(cols, turn))  6.93 us
    ppermute x2, starting transfers between devices, on_device(): lax.ppermute(image, grid_axes, links(image_source, turn))  6.73 us
    ppermute x2, starting transfers between devices, on_device(): lax.ppermute(pair, grid_axes, links(sample_source, turn))  6.44 us
    ppermute x2, waiting for transfers between devices, on_device(): lax.ppermute(pair, grid_axes, links(sample_source, turn))  3.63 us
    ppermute x1, waiting for transfers between devices, on_device(): lax.ppermute(late, 'col', around(cols, turn))  2.72 us
    pallas_call x1, Pallas kernels, update_slots(): pl.pallas_call(slots_kernel, out_shape=jax.ShapeDtypeStruct(tiles.shape,...  2.06 us
    ppermute x2, waiting for transfers between devices, on_device(): lax.ppermute(image, grid_axes, links(image_source, turn))  2.05 us
    pallas_call x1, Pallas kernels, prepare(): pl.pallas_call(functools.partial(prepare_kernel, groups), out_shape=(pltp...  1.76 us
  transfers between devices with their start and end apart: 9, of which 7 were waited for; matrix products, arithmetic and copies ran while one was open for 0% of the time, Pallas kernels for 7%

profile of v7, /device:TPU:6, one launch (start us, length us, event | category | flops | bytes accessed | tf_op | source)
XLA Modules:
  0.0 40.3 jit_solution(10711851364355976432)
XLA Ops:
  0.6 0.1 collective-permute-start
  0.7 1.5 %collective-permute-done = f32[96,256]{1,0:T(8,128)S(1)} collective-permute-done((f32[96,256]{1,0:T(8,128)}, f32[96,256]{1,0:T(8,128)S(1)}, u32[]{:S(2)}, u32[]{:S(2)}) %collective-permute-start) | collective-permute-done | bytes 98336 | tf_op jit(solution)/shard_map/ppermute | solution.py:265
  2.2 0.9 %pad_maximum_fusion.samples.refs_0_ = f32[2,96,256]{2,1,0:T(8,128)S(1)} fusion(f32[1,96,256]{2,1,0:T(8,128)S(1)} %bitcast.10, f32[1,96,256]{2,1,0:T(8,128)} %bitcast.9), kind=kLoop, calls=%fused_computation | loop fusion | flops 49152 | bytes 393216 | tf_op jit(solution)/shard_map/stack | solution.py:265
  3.1 2.6 %collective-permute-start.2 = (f32[2,96,256]{2,1,0:T(8,128)S(1)}, f32[2,96,256]{2,1,0:T(8,128)S(1)}, u32[]{:S(2)}, u32[]{:S(2)}) collective-permute-start(f32[2,96,256]{2,1,0:T(8,128)S(1)} %pad_maximum_fusion.samples.refs_0_), channel_id=1, source_target_pairs={{3,0},{0,4},{2,8},{1,12},{7,1},{4,5},{6,9},{5,13},{8,2},{11,6},{9,... | collective-permute-start | bytes 589832 | tf_op jit(solution)/shard_map/ppermute | solution.py:267
  5.7 3.8 %collective-permute-start.1 = (f32[2,96,256]{2,1,0:T(8,128)S(1)}, f32[2,96,256]{2,1,0:T(8,128)S(1)}, u32[]{:S(2)}, u32[]{:S(2)}) collective-permute-start(f32[2,96,256]{2,1,0:T(8,128)S(1)} %pad_maximum_fusion.samples.refs_0_), channel_id=1, source_target_pairs={{0,0},{3,4},{1,8},{2,12},{4,1},{7,5},{5,9},{6,13},{11,2},{8,6},{10... | collective-permute-start | bytes 589832 | tf_op jit(solution)/shard_map/ppermute | solution.py:267
  10.2 1.8 %prepare.1 = (s32[5,8]{1,0:T(8,128)S(4)}, f32[1,256,256]{2,1,0:T(8,128)S(1)}, f32[8,256,256]{2,1,0:T(8,128)S(1)}, bf16[8,256,256]{2,1,0:T(8,128)(2,1)S(1)}, bf16[8,256,256]{2,1,0:T(8,128)(2,1)S(1)}) custom-call(s32[2,8]{1,0:T(2,128)} %bitcast.11, s32[1,1]{1,0:T(1,128)S(6)} %copy.7.refs_1_, f32[1,256,256]{2,1,0:T(8,128)} %refs_2_.1, f32[8,256,256]{2,1,0:T(8,128)} %bitcast.7), custom_call_target="tpu_custom_call" | custom-call | tf_op jit(solution)/shard_map/prepare/pallas_call | solution.py:81
  12.0 0.2 collective-permute-done.2.refs_1_
  12.2 3.4 %collective-permute-done.1.refs_0_ = f32[2,96,256]{2,1,0:T(8,128)S(1)} collective-permute-done((f32[2,96,256]{2,1,0:T(8,128)S(1)}, f32[2,96,256]{2,1,0:T(8,128)S(1)}, u32[]{:S(2)}, u32[]{:S(2)}) %collective-permute-start.1) | collective-permute-done | bytes 196640 | tf_op jit(solution)/shard_map/ppermute | solution.py:267
  15.6 0.9 %partial_image.1 = (f32[2,96,256]{2,1,0:T(8,128)S(1)}, f32[2,96,256]{2,1,0:T(8,128)S(1)}, bf16[4,192,256]{2,1,0:T(8,128)(2,1)S(1)}) custom-call(s32[5,8]{1,0:T(8,128)S(4)} %get-tuple-element.15.guide, f32[2,96,256]{2,1,0:T(8,128)S(1)} %pad_maximum_fusion.samples.refs_0_, f32[1,256,256]{2,1,0:T(8,128)S(1)} %get-tuple-element.16.diag, ...), custom_call_target="tpu_custom_call" | custom-call | tf_op jit(solution)/shard_map/partial_image/pallas_call | solution.py:131
  16.5 0.1 collective-permute-start.3
  16.6 1.4 %collective-permute-done.3 = f32[2,96,256]{2,1,0:T(8,128)S(1)} collective-permute-done((f32[2,96,256]{2,1,0:T(8,128)S(1)}, f32[2,96,256]{2,1,0:T(8,128)S(1)}, u32[]{:S(2)}, u32[]{:S(2)}) %collective-permute-start.3) | collective-permute-done | bytes 196640 | tf_op jit(solution)/shard_map/ppermute | solution.py:271
  18.0 0.1 collective-permute-start.4
  18.1 6.9 %collective-permute-done.4 = f32[2,96,256]{2,1,0:T(8,128)S(1)} collective-permute-done((f32[2,96,256]{2,1,0:T(8,128)S(1)}, f32[2,96,256]{2,1,0:T(8,128)S(1)}, u32[]{:S(2)}, u32[]{:S(2)}) %collective-permute-start.4) | collective-permute-done | bytes 196640 | tf_op jit(solution)/shard_map/ppermute | solution.py:274
  25.1 0.4 collective-permute-start.6
  25.4 0.0 collective-permute-start.5
  25.4 2.0 %collective-permute-start.8 = (f32[2,96,256]{2,1,0:T(8,128)S(1)}, f32[2,96,256]{2,1,0:T(8,128)S(1)}, u32[]{:S(2)}, u32[]{:S(2)}) collective-permute-start(f32[2,96,256]{2,1,0:T(8,128)S(1)} %add.7.own_image), channel_id=1, source_target_pairs={{3,0},{0,4},{2,8},{1,12},{7,1},{4,5},{6,9},{5,13},{8,2},{11,6},{9,... | collective-permute-start | bytes 589832 | tf_op jit(solution)/shard_map/ppermute | solution.py:279
  27.4 4.7 %collective-permute-start.7 = (f32[2,96,256]{2,1,0:T(8,128)S(1)}, f32[2,96,256]{2,1,0:T(8,128)S(1)}, u32[]{:S(2)}, u32[]{:S(2)}) collective-permute-start(f32[2,96,256]{2,1,0:T(8,128)S(1)} %add.7.own_image), channel_id=1, source_target_pairs={{0,0},{3,4},{1,8},{2,12},{4,1},{7,5},{5,9},{6,13},{11,2},{8,6},{10... | collective-permute-start | bytes 589832 | tf_op jit(solution)/shard_map/ppermute | solution.py:279
  32.2 2.7 %collective-permute-done.6.refs_1_ = f32[2,96,256]{2,1,0:T(8,128)S(1)} collective-permute-done((f32[2,96,256]{2,1,0:T(8,128)S(1)}, f32[2,96,256]{2,1,0:T(8,128)S(1)}, u32[]{:S(2)}, u32[]{:S(2)}) %collective-permute-start.6) | collective-permute-done | bytes 196640 | tf_op jit(solution)/shard_map/ppermute | solution.py:277
  34.9 0.0 collective-permute-done.5.other_image
  34.9 1.2 %middle.1 = (bf16[4,256,256]{2,1,0:T(8,128)(2,1)S(1)}, bf16[4,256,256]{2,1,0:T(8,128)(2,1)S(1)}, f32[1,256,256]{2,1,0:T(8,128)}) custom-call(f32[2,96,256]{2,1,0:T(8,128)S(1)} %add.7.own_image, f32[2,96,256]{2,1,0:T(8,128)S(1)} %collective-permute-done.5.other_image, f32[1,256,256]{2,1,0:T(8,128)S(1)} %get-tuple-element.16.diag, ...), custom_call_target="tpu_custom_call" | custom-call | tf_op jit(solution)/shard_map/middle/pallas_call | solution.py:186
  36.1 0.0 collective-permute-done.8.second
  36.1 2.0 %collective-permute-done.7.first = f32[2,96,256]{2,1,0:T(8,128)S(1)} collective-permute-done((f32[2,96,256]{2,1,0:T(8,128)S(1)}, f32[2,96,256]{2,1,0:T(8,128)S(1)}, u32[]{:S(2)}, u32[]{:S(2)}) %collective-permute-start.7) | collective-permute-done | bytes 196640 | tf_op jit(solution)/shard_map/ppermute | solution.py:279
  38.2 2.1 %update_slots.1 = f32[8,256,256]{2,1,0:T(8,128)} custom-call(s32[5,8]{1,0:T(8,128)S(4)} %get-tuple-element.15.guide, bf16[4,256,256]{2,1,0:T(8,128)(2,1)S(1)} %get-tuple-element.23.left_high, bf16[4,256,256]{2,1,0:T(8,128)(2,1)S(1)} %get-tuple-element.24.left_low, bf16[4,192,256]{2,1,0:T(8,128)(2,1)S(1)} %get-tuple-element.25.panel, ...), custom_call_target="tpu_custom_call" | custom-call | tf_op jit(solution)/shard_map/update_slots/pallas_call | solution.py:231
  (2 shorter events, 0.1 us)
Async XLA Ops:
  0.6 1.6 %collective-permute-start = (f32[96,256]{1,0:T(8,128)}, f32[96,256]{1,0:T(8,128)S(1)}, u32[]{:S(2)}, u32[]{:S(2)}) collective-permute-start(f32[96,256]{1,0:T(8,128)} %param.5), channel_id=1, source_target_pairs={{0,1},{1,0},{2,3},{3,2},{4,5},{5,4},{6,7},{7,6},{8,9},{9,8},{10,11... | collective-permute-start | bytes 294920 | tf_op jit(solution)/shard_map/ppermute | solution.py:265
  3.1 9.1 %collective-permute-start.2 = (f32[2,96,256]{2,1,0:T(8,128)S(1)}, f32[2,96,256]{2,1,0:T(8,128)S(1)}, u32[]{:S(2)}, u32[]{:S(2)}) collective-permute-start(f32[2,96,256]{2,1,0:T(8,128)S(1)} %pad_maximum_fusion.samples.refs_0_), channel_id=1, source_target_pairs={{3,0},{0,4},{2,8},{1,12},{7,1},{4,5},{6,9},{5,13},{8,2},{11,6},{9,... | collective-permute-start | bytes 589832 | tf_op jit(solution)/shard_map/ppermute | solution.py:267
  5.7 9.9 %collective-permute-start.1 = (f32[2,96,256]{2,1,0:T(8,128)S(1)}, f32[2,96,256]{2,1,0:T(8,128)S(1)}, u32[]{:S(2)}, u32[]{:S(2)}) collective-permute-start(f32[2,96,256]{2,1,0:T(8,128)S(1)} %pad_maximum_fusion.samples.refs_0_), channel_id=1, source_target_pairs={{0,0},{3,4},{1,8},{2,12},{4,1},{7,5},{5,9},{6,13},{11,2},{8,6},{10... | collective-permute-start | bytes 589832 | tf_op jit(solution)/shard_map/ppermute | solution.py:267
  16.5 1.5 %collective-permute-start.3 = (f32[2,96,256]{2,1,0:T(8,128)S(1)}, f32[2,96,256]{2,1,0:T(8,128)S(1)}, u32[]{:S(2)}, u32[]{:S(2)}) collective-permute-start(f32[2,96,256]{2,1,0:T(8,128)S(1)} %get-tuple-element.20), channel_id=1, source_target_pairs={{0,1},{1,0},{2,3},{3,2},{4,5},{5,4},{6,7},{7,6},{8,9},{9,8},{10,11... | collective-permute-start | bytes 589832 | tf_op jit(solution)/shard_map/ppermute | solution.py:271
  18.0 7.0 %collective-permute-start.4 = (f32[2,96,256]{2,1,0:T(8,128)S(1)}, f32[2,96,256]{2,1,0:T(8,128)S(1)}, u32[]{:S(2)}, u32[]{:S(2)}) collective-permute-start(f32[2,96,256]{2,1,0:T(8,128)S(1)} %add.6), channel_id=1, source_target_pairs={{0,2},{2,0},{1,3},{3,1},{4,6},{6,4},{5,7},{7,5},{8,10},{10,8},{9,1... | collective-permute-start | bytes 589832 | tf_op jit(solution)/shard_map/ppermute | solution.py:274
  25.1 9.8 %collective-permute-start.6 = (f32[2,96,256]{2,1,0:T(8,128)S(1)}, f32[2,96,256]{2,1,0:T(8,128)S(1)}, u32[]{:S(2)}, u32[]{:S(2)}) collective-permute-start(f32[2,96,256]{2,1,0:T(8,128)S(1)} %pad_maximum_fusion.samples.refs_0_), channel_id=1, source_target_pairs={{0,2},{2,0},{1,3},{3,1},{4,6},{6,4},{5,7},{7,5},{8,10},{10,8},{9,1... | collective-permute-start | bytes 589832 | tf_op jit(solution)/shard_map/ppermute | solution.py:277
  25.4 9.5 %collective-permute-start.5 = (f32[2,96,256]{2,1,0:T(8,128)S(1)}, f32[2,96,256]{2,1,0:T(8,128)S(1)}, u32[]{:S(2)}, u32[]{:S(2)}) collective-permute-start(f32[2,96,256]{2,1,0:T(8,128)S(1)} %add.7.own_image), channel_id=1, source_target_pairs={{0,1},{1,0},{2,3},{3,2},{4,5},{5,4},{6,7},{7,6},{8,9},{9,8},{10,11... | collective-permute-start | bytes 589832 | tf_op jit(solution)/shard_map/ppermute | solution.py:281
  25.4 10.7 %collective-permute-start.8 = (f32[2,96,256]{2,1,0:T(8,128)S(1)}, f32[2,96,256]{2,1,0:T(8,128)S(1)}, u32[]{:S(2)}, u32[]{:S(2)}) collective-permute-start(f32[2,96,256]{2,1,0:T(8,128)S(1)} %add.7.own_image), channel_id=1, source_target_pairs={{3,0},{0,4},{2,8},{1,12},{7,1},{4,5},{6,9},{5,13},{8,2},{11,6},{9,... | collective-permute-start | bytes 589832 | tf_op jit(solution)/shard_map/ppermute | solution.py:279
  27.4 10.8 %collective-permute-start.7 = (f32[2,96,256]{2,1,0:T(8,128)S(1)}, f32[2,96,256]{2,1,0:T(8,128)S(1)}, u32[]{:S(2)}, u32[]{:S(2)}) collective-permute-start(f32[2,96,256]{2,1,0:T(8,128)S(1)} %add.7.own_image), channel_id=1, source_target_pairs={{0,0},{3,4},{1,8},{2,12},{4,1},{7,5},{5,9},{6,13},{11,2},{8,6},{10... | collective-permute-start | bytes 589832 | tf_op jit(solution)/shard_map/ppermute | solution.py:279

commit v8 on v7

--- a/solution.py
+++ b/solution.py
@@ -24,8 +24,8 @@
     return high, (values - high.astype(f32)).astype(bf16)
 
 
-def dot(left, right, dims):
-    return lax.dot_general(left, right, (dims, ((), ())), preferred_element_type=f32)
+def dot(left, right):
+    return jnp.dot(left, right, preferred_element_type=f32)
 
 
 def soft_limit(values):
@@ -39,11 +39,12 @@
 
 
 def sample_source(turn, row, own, groups):
-    return first_source(row, own, groups) ^ (2 * turn + turn % 2)
+    spot = groups // 2 - 1 - turn
+    return first_source(row, own, groups) ^ (2 * spot + spot % 2)
 
 
 def image_source(turn, row, own, groups):
-    return first_source(row, own, groups) ^ (turn * (groups - 1))
+    return first_source(row, own, groups) ^ ((1 - turn) * (groups - 1))
 
 
 def prepare_kernel(groups, *refs):
@@ -64,7 +65,7 @@
         guide[3, turn] = image_source(turn, row, own, groups) & 1
     for slot in range(slots):
         copies[3 + slot].wait()
-        high[slot], low[slot] = halves(tiles[slot])
+        high[slot], low[slot] = halves(tiles[slot].T)
     for copy in copies[:3]:
         copy.wait()
     for slot in range(slots):
@@ -106,17 +107,17 @@
             panel[block, :rows], panel[block, rows:] = halves(piece[half])
     total[...] = jnp.zeros_like(total)
 
-    def term(x_high, both, w_high, w_low, dims):
-        wide = dot(both, w_high, dims)
-        return wide[:rows] + wide[rows:] + dot(x_high, w_low, dims)
+    def term(x_high, both, w_high, w_low):
+        wide = dot(both, w_high)
+        return wide[:rows] + wide[rows:] + dot(x_high, w_low)
 
     own_high, own_low = halves(samples[0])
     total[col * 2 + rep] = term(
-        own_high, jnp.concatenate([own_high, own_low], axis=0), *halves(diag[0]), ((1,), (0,))
+        own_high, jnp.concatenate([own_high, own_low], axis=0), *halves(diag[0])
     )
     for slot in range(high.shape[0]):
         source = panel.at[guide[1, slot]]
-        value = term(source[:rows], source[...], high[slot], low[slot], ((1,), (1,)))
+        value = term(source[:rows], source[...], high[slot], low[slot])
         total[guide[0, slot]] += jnp.where(slot < guide[4, 0], value, 0.0)
     for pair in range(groups // 2):
         kept[pair] = total[2 * pair + rep]
@@ -139,85 +140,99 @@
     )(guide, samples, diag, high, low, *pieces)
 
 
-def middle_kernel(own_image, other_image, diag, *refs):
-    samples = refs[:-5]
-    high, low, new_diag, shifted, sem = refs[-5:]
-    pairs = own_image.shape[0]
+def half_gradient_kernel(
+    guide, own_image, other_image, samples, panel, diag, tiles, moved, new_diag, wide, low, step, sem
+):
+    pairs, rows, side = own_image.shape
     rep = lax.axis_index("rep")
-    col = lax.axis_index("col")
-    _, rows, side = samples[0].shape
-    half = high.shape[2] // 2
-    blank = jnp.zeros((side, half - rows), bf16)
-    for turn, piece in enumerate(samples):
-        line = 2 * lax.rem(col + pairs - turn, pairs)
-        for block, place in ((line + rep, 0), (line + 1 - rep, 1)):
-            for ref, part in zip((high, low), halves(piece[place].T)):
-                ref[block, :, :rows] = part
-                ref[block, :, rows:half] = blank
-                ref[block, :, half + rows :] = blank
-    left_high, left_low = halves(samples[0][0].T)
-    right_high, right_low = halves(own_image[col])
-    dims = ((1,), (0,))
-    one_side = dot(left_high, right_high, dims) + dot(left_low, right_high, dims)
-    one_side += dot(left_high, right_low, dims)
+    left_high, left_low = halves(samples[0].T)
+    right_high, right_low = halves(own_image[lax.axis_index("col")])
+    one_side = dot(left_high, right_high) + dot(left_low, right_high) + dot(left_high, right_low)
     tile = diag[0]
     line = lax.broadcasted_iota(jnp.int32, (side, side), 0)
     on_diag = line == lax.broadcasted_iota(jnp.int32, (side, side), 1)
-    gradient = (one_side + one_side.T) * (1.0 / (2.0 * rows))
-    moved = tile - step_size * gradient
+    scale = step_size / (2.0 * rows)
+    shifted = tile - (one_side + one_side.T) * scale
     inverse = step_size / jnp.where(on_diag, tile, 1.0)
-    shifted[0] = jnp.where(on_diag, moved + inverse, soft_limit(moved))
-    copy = pltpu.make_async_copy(shifted, new_diag, sem)
+    step[0] = jnp.where(on_diag, shifted + inverse, soft_limit(shifted))
+    copy = pltpu.make_async_copy(step, new_diag, sem)
     copy.start()
     for pair in range(pairs):
         for parity, image in ((rep, own_image), (1 - rep, other_image)):
             block = 2 * pair + parity
-            image_high, image_low = halves(image[pair].T)
-            high[block, :, half : half + rows] = image_high
-            low[block, :, half : half + rows] = image_low
+            image_high, low[block] = halves(image[pair].T)
+            wide[block, :, :rows] = image_high
+            wide[block, :, rows:] = image_high
+    for slot in range(tiles.shape[0]):
+        left, right = guide[0, slot], guide[1, slot]
+        gradient = dot(wide[left], panel[right]) + dot(low[left], panel[right, :rows])
+        moved[slot] = tiles[slot] - gradient * scale
     copy.wait()
 
 
-def middle(own_image, other_image, diag, samples):
-    pairs, rows, side = own_image.shape
-    groups = 2 * pairs
-    depth = 2 * -(-rows // 128) * 128
-    left = jax.ShapeDtypeStruct((groups, side, depth), bf16)
-    return pl.pallas_call(
-        middle_kernel,
-        out_shape=(left, left, jax.ShapeDtypeStruct(diag.shape, f32)),
-        in_specs=[vmem] * (3 + len(samples)),
-        out_specs=(vmem, vmem, hbm),
-        scratch_shapes=[pltpu.VMEM(diag.shape, f32), pltpu.SemaphoreType.DMA],
-        compiler_params=room,
-        name="middle",
-    )(own_image, other_image, diag, *samples)
-
-
-def slots_kernel(
-    guide, left_high, left_low, panel, first, second, tiles, out, high, low, ready, sems
-):
-    groups = panel.shape[0]
-    rows = panel.shape[1] // 2
-    half = high.shape[1] // 2
-    for ref in (high, low):
-        for start in (rows, half + rows):
-            blank = jnp.zeros((groups, half - rows, high.shape[2]), bf16)
-            ref[:, start : start + half - rows] = blank
-    for pair in range(groups // 2):
+def half_gradient(guide, own_image, other_image, samples, panel, diag, tiles):
+    groups, _, side = panel.shape
+    rows = samples.shape[1]
+    return pl.pallas_call(
+        half_gradient_kernel,
+        out_shape=(
+            jax.ShapeDtypeStruct(tiles.shape, f32),
+            jax.ShapeDtypeStruct(diag.shape, f32),
+        ),
+        in_specs=[smem] + [vmem] * 6,
+        out_specs=(vmem, hbm),
+        scratch_shapes=[
+            pltpu.VMEM((groups, side, 2 * rows), bf16),
+            pltpu.VMEM((groups, side, rows), bf16),
+            pltpu.VMEM(diag.shape, f32),
+            pltpu.SemaphoreType.DMA,
+        ],
+        compiler_params=room,
+        name="half_gradient",
+    )(guide, own_image, other_image, samples, panel, diag, tiles)
+
+
+def row_panel_kernel(*refs):
+    samples, (wide, low) = refs[:-2], refs[-2:]
+    rep = lax.axis_index("rep")
+    col = lax.axis_index("col")
+    rows = samples[0].shape[1]
+    pairs = len(samples)
+    for turn, piece in enumerate(samples):
+        line = 2 * lax.rem(col + pairs - turn, pairs)
+        for block, place in ((line + rep, 0), (line + 1 - rep, 1)):
+            high, low[block] = halves(piece[place].T)
+            wide[block, :, :rows] = high
+            wide[block, :, rows:] = high
+
+
+def row_panel(samples):
+    _, rows, side = samples[0].shape
+    groups = 2 * len(samples)
+    return pl.pallas_call(
+        row_panel_kernel,
+        out_shape=(
+            jax.ShapeDtypeStruct((groups, side, 2 * rows), bf16),
+            jax.ShapeDtypeStruct((groups, side, rows), bf16),
+        ),
+        in_specs=[vmem] * len(samples),
+        out_specs=(vmem, vmem),
+        compiler_params=room,
+        name="row_panel",
+    )(*samples)
+
+
+def slots_kernel(guide, wide, low, first, second, moved, out, panel, ready, sems):
+    pairs, rows, _ = first.shape
+    for pair in range(pairs):
         for turn, piece in enumerate((first, second)):
             block = 2 * pair + guide[3, turn]
-            high[block, :rows], low[block, :rows] = halves(piece[pair])
-    high[:, half : half + rows] = panel[:, :rows]
-    low[:, half : half + rows] = panel[:, rows:]
-    dims = ((1,), (0,))
+            panel[block, :rows], panel[block, rows:] = halves(piece[pair])
     copies = []
-    for slot in range(tiles.shape[0]):
+    for slot in range(moved.shape[0]):
         left, right = guide[0, slot], guide[1, slot]
-        gradient = dot(left_high[left], high[right], dims)
-        gradient += dot(left_low[left], high[right], dims)
-        gradient += dot(left_high[left], low[right], dims)
-        value = soft_limit(tiles[slot] - gradient * (step_size / (2.0 * rows)))
+        gradient = dot(wide[left], panel[right]) + dot(low[left], panel[right, :rows])
+        value = soft_limit(moved[slot] - gradient * (step_size / (2.0 * rows)))
         ready[slot] = jnp.where(slot < guide[4, 0], value, 0.0)
         copies.append(pltpu.make_async_copy(ready.at[slot], out.at[slot], sems.at[slot]))
         copies[-1].start()
@@ -225,23 +240,22 @@
         copy.wait()
 
 
-def update_slots(guide, left_high, left_low, panel, first, second, tiles):
-    slots, side, _ = tiles.shape
-    groups, _, depth = left_high.shape
+def update_slots(guide, wide, low, first, second, moved):
+    slots, side, _ = moved.shape
+    groups, _, depth = wide.shape
     return pl.pallas_call(
         slots_kernel,
-        out_shape=jax.ShapeDtypeStruct(tiles.shape, f32),
-        in_specs=[smem] + [vmem] * 6,
+        out_shape=jax.ShapeDtypeStruct(moved.shape, f32),
+        in_specs=[smem] + [vmem] * 5,
         out_specs=hbm,
         scratch_shapes=[
             pltpu.VMEM((groups, depth, side), bf16),
-            pltpu.VMEM((groups, depth, side), bf16),
-            pltpu.VMEM(tiles.shape, f32),
+            pltpu.VMEM(moved.shape, f32),
             pltpu.SemaphoreType.DMA((slots,)),
         ],
         compiler_params=room,
         name="update_slots",
-    )(guide, left_high, left_low, panel, first, second, tiles)
+    )(guide, wide, low, first, second, moved)
 
 
 def on_device(samples, diag_tiles, omega_slots, tile_pos, tile_count):
@@ -279,8 +293,9 @@
         lax.ppermute(image, grid_axes, links(image_source, turn)) for turn in range(2)
     ]
     other = lax.ppermute(image, "rep", around(2, 1))
-    left_high, left_low, new_diag = middle(image, other, own_diag, [pair, *beside])
-    new_slots = update_slots(guide, left_high, left_low, panel, first, second, held)
+    moved, new_diag = half_gradient(guide, image, other, pair, panel, own_diag, held)
+    wide, low = row_panel([pair, *beside])
+    new_slots = update_slots(guide, wide, low, first, second, moved)
     return new_slots.reshape(omega_slots.shape), new_diag
 
 

time: 40.5 us -> 40 us (0.988)
  waiting for transfers between devices: 18.3 us -> 16.9 us
  Pallas kernels: 5.94 us -> 6.65 us
    ppermute x2, waiting for transfers between devices: 2.05 us -> 1.26 us  [on_device(): lax.ppermute(image, grid_axes, links(image_source, turn))]
    ppermute x2, waiting for transfers between devices: 3.63 us -> 3.1 us  [on_device(): lax.ppermute(pair, grid_axes, links(sample_source, turn))]
    pallas_call x1, Pallas kernels: 1.76 us -> 2.28 us  [prepare(): pl.pallas_call(functools.partial(prepare_kernel, groups), out_shape=(pltp...]
    pallas_call x2 -> x3, Pallas kernels: 3.31 us -> 3.75 us  [the longest x1 1.73 us: update_slots(): pl.pallas_call(slots_kernel, out_shape=jax.ShapeDtypeStruct(moved.shape,...]
  transfers between devices with their start and end apart: 9 -> 9, of which waited for: 7 -> 6; matrix products, arithmetic and copies ran while one was open for 0% -> 0% of each run, Pallas kernels for 7% -> 11%
where the time goes in v8:
time: 40 us; the launch traced here: 39.7 us
  waiting for transfers between devices  16.9 us (42%)
  starting transfers between devices  13.7 us (34%)
  Pallas kernels  6.65 us (17%)
  between operations  1.38 us (3%)
  other arithmetic  0.96 us (2%)
    ppermute x1, waiting for transfers between devices, on_device(): image = image + lax.ppermute(chip, 'col', around(cols, turn))  6.93 us
    ppermute x2, starting transfers between devices, on_device(): lax.ppermute(image, grid_axes, links(image_source, turn))  6.73 us
    ppermute x2, starting transfers between devices, on_device(): lax.ppermute(pair, grid_axes, links(sample_source, turn))  6.44 us
    ppermute x2, waiting for transfers between devices, on_device(): lax.ppermute(pair, grid_axes, links(sample_source, turn))  3.1 us
    ppermute x1, waiting for transfers between devices, on_device(): lax.ppermute(late, 'col', around(cols, turn))  2.72 us
    pallas_call x1, Pallas kernels, prepare(): pl.pallas_call(functools.partial(prepare_kernel, groups), out_shape=(pltp...  2.28 us
    pallas_call x1, Pallas kernels, update_slots(): pl.pallas_call(slots_kernel, out_shape=jax.ShapeDtypeStruct(moved.shape,...  1.73 us
    pallas_call x1, Pallas kernels, half_gradient(): pl.pallas_call(half_gradient_kernel, out_shape=(jax.ShapeDtypeStruct(tile...  1.67 us
  transfers between devices with their start and end apart: 9, of which 6 were waited for; matrix products, arithmetic and copies ran while one was open for 0% of the time, Pallas kernels for 11%

profile of v8, /device:TPU:6, one launch (start us, length us, event | category | flops | bytes accessed | tf_op | source)
XLA Modules:
  0.0 39.7 jit_solution(13034199381130963753)
XLA Ops:
  0.6 0.1 collective-permute-start
  0.7 1.5 %collective-permute-done = f32[96,256]{1,0:T(8,128)S(1)} collective-permute-done((f32[96,256]{1,0:T(8,128)}, f32[96,256]{1,0:T(8,128)S(1)}, u32[]{:S(2)}, u32[]{:S(2)}) %collective-permute-start) | collective-permute-done | bytes 98336 | tf_op jit(solution)/shard_map/ppermute | solution.py:279
  2.2 0.9 %pad_maximum_fusion.samples.refs_0_ = f32[2,96,256]{2,1,0:T(8,128)S(1)} fusion(f32[1,96,256]{2,1,0:T(8,128)S(1)} %bitcast.10, f32[1,96,256]{2,1,0:T(8,128)} %bitcast.9), kind=kLoop, calls=%fused_computation | loop fusion | flops 49152 | bytes 393216 | tf_op jit(solution)/shard_map/stack | solution.py:279
  3.1 2.6 %collective-permute-start.1 = (f32[2,96,256]{2,1,0:T(8,128)S(1)}, f32[2,96,256]{2,1,0:T(8,128)S(1)}, u32[]{:S(2)}, u32[]{:S(2)}) collective-permute-start(f32[2,96,256]{2,1,0:T(8,128)S(1)} %pad_maximum_fusion.samples.refs_0_), channel_id=1, source_target_pairs={{3,0},{0,4},{2,8},{1,12},{7,1},{4,5},{6,9},{5,13},{8,2},{11,6},{9,... | collective-permute-start | bytes 589832 | tf_op jit(solution)/shard_map/ppermute | solution.py:281
  5.7 3.8 %collective-permute-start.2 = (f32[2,96,256]{2,1,0:T(8,128)S(1)}, f32[2,96,256]{2,1,0:T(8,128)S(1)}, u32[]{:S(2)}, u32[]{:S(2)}) collective-permute-start(f32[2,96,256]{2,1,0:T(8,128)S(1)} %pad_maximum_fusion.samples.refs_0_), channel_id=1, source_target_pairs={{0,0},{3,4},{1,8},{2,12},{4,1},{7,5},{5,9},{6,13},{11,2},{8,6},{10... | collective-permute-start | bytes 589832 | tf_op jit(solution)/shard_map/ppermute | solution.py:281
  10.2 2.3 %prepare.1 = (s32[5,8]{1,0:T(8,128)S(4)}, f32[1,256,256]{2,1,0:T(8,128)S(1)}, f32[8,256,256]{2,1,0:T(8,128)S(1)}, bf16[8,256,256]{2,1,0:T(8,128)(2,1)S(1)}, bf16[8,256,256]{2,1,0:T(8,128)(2,1)S(1)}) custom-call(s32[2,8]{1,0:T(2,128)} %bitcast.11, s32[1,1]{1,0:T(1,128)S(6)} %copy.7.refs_1_, f32[1,256,256]{2,1,0:T(8,128)} %refs_2_.1, f32[8,256,256]{2,1,0:T(8,128)} %bitcast.7), custom_call_target="tpu_custom_call" | custom-call | tf_op jit(solution)/shard_map/prepare/pallas_call | solution.py:82
  12.5 0.0 collective-permute-done.1.refs_0_
  12.5 3.1 %collective-permute-done.2.refs_1_ = f32[2,96,256]{2,1,0:T(8,128)S(1)} collective-permute-done((f32[2,96,256]{2,1,0:T(8,128)S(1)}, f32[2,96,256]{2,1,0:T(8,128)S(1)}, u32[]{:S(2)}, u32[]{:S(2)}) %collective-permute-start.2) | collective-permute-done | bytes 196640 | tf_op jit(solution)/shard_map/ppermute | solution.py:281
  15.6 0.6 %partial_image.1 = (f32[2,96,256]{2,1,0:T(8,128)S(1)}, f32[2,96,256]{2,1,0:T(8,128)S(1)}, bf16[4,192,256]{2,1,0:T(8,128)(2,1)S(1)}) custom-call(s32[5,8]{1,0:T(8,128)S(4)} %get-tuple-element.16.guide, f32[2,96,256]{2,1,0:T(8,128)S(1)} %pad_maximum_fusion.samples.refs_0_, f32[1,256,256]{2,1,0:T(8,128)S(1)} %get-tuple-element.17.diag, ...), custom_call_target="tpu_custom_call" | custom-call | tf_op jit(solution)/shard_map/partial_image/pallas_call | solution.py:132
  16.2 0.1 collective-permute-start.3
  16.3 1.4 %collective-permute-done.3 = f32[2,96,256]{2,1,0:T(8,128)S(1)} collective-permute-done((f32[2,96,256]{2,1,0:T(8,128)S(1)}, f32[2,96,256]{2,1,0:T(8,128)S(1)}, u32[]{:S(2)}, u32[]{:S(2)}) %collective-permute-start.3) | collective-permute-done | bytes 196640 | tf_op jit(solution)/shard_map/ppermute | solution.py:285
  17.8 0.1 collective-permute-start.4
  17.8 6.9 %collective-permute-done.4 = f32[2,96,256]{2,1,0:T(8,128)S(1)} collective-permute-done((f32[2,96,256]{2,1,0:T(8,128)S(1)}, f32[2,96,256]{2,1,0:T(8,128)S(1)}, u32[]{:S(2)}, u32[]{:S(2)}) %collective-permute-start.4) | collective-permute-done | bytes 196640 | tf_op jit(solution)/shard_map/ppermute | solution.py:288
  24.8 0.4 collective-permute-start.5
  25.1 0.0 collective-permute-start.8
  25.2 2.0 %collective-permute-start.6 = (f32[2,96,256]{2,1,0:T(8,128)S(1)}, f32[2,96,256]{2,1,0:T(8,128)S(1)}, u32[]{:S(2)}, u32[]{:S(2)}) collective-permute-start(f32[2,96,256]{2,1,0:T(8,128)S(1)} %add.7.own_image), channel_id=1, source_target_pairs={{3,0},{0,4},{2,8},{1,12},{7,1},{4,5},{6,9},{5,13},{8,2},{11,6},{9,... | collective-permute-start | bytes 589832 | tf_op jit(solution)/shard_map/ppermute | solution.py:293
  27.2 4.7 %collective-permute-start.7 = (f32[2,96,256]{2,1,0:T(8,128)S(1)}, f32[2,96,256]{2,1,0:T(8,128)S(1)}, u32[]{:S(2)}, u32[]{:S(2)}) collective-permute-start(f32[2,96,256]{2,1,0:T(8,128)S(1)} %add.7.own_image), channel_id=1, source_target_pairs={{0,0},{3,4},{1,8},{2,12},{4,1},{7,5},{5,9},{6,13},{11,2},{8,6},{10... | collective-permute-start | bytes 589832 | tf_op jit(solution)/shard_map/ppermute | solution.py:293
  31.9 2.7 %collective-permute-done.5.refs_1_ = f32[2,96,256]{2,1,0:T(8,128)S(1)} collective-permute-done((f32[2,96,256]{2,1,0:T(8,128)S(1)}, f32[2,96,256]{2,1,0:T(8,128)S(1)}, u32[]{:S(2)}, u32[]{:S(2)}) %collective-permute-start.5) | collective-permute-done | bytes 196640 | tf_op jit(solution)/shard_map/ppermute | solution.py:291
  34.6 0.4 row_panel.1
  35.0 0.0 collective-permute-done.8.other_image
  35.0 1.7 %half_gradient.1 = (f32[8,256,256]{2,1,0:T(8,128)S(1)}, f32[1,256,256]{2,1,0:T(8,128)}) custom-call(s32[5,8]{1,0:T(8,128)S(4)} %get-tuple-element.16.guide, f32[2,96,256]{2,1,0:T(8,128)S(1)} %add.7.own_image, f32[2,96,256]{2,1,0:T(8,128)S(1)} %collective-permute-done.8.other_image, f32[2,96,256]{2,1,0:T(8,128)S(1)} %pad_maximum_fusion.samples.refs_0_, ...), custom_call_target="tpu_custom_call" | custom-call | tf_op jit(solution)/shard_map/half_gradient/pallas_call | solution.py:176
  36.7 0.0 collective-permute-done.6.first
  36.7 1.3 %collective-permute-done.7.second = f32[2,96,256]{2,1,0:T(8,128)S(1)} collective-permute-done((f32[2,96,256]{2,1,0:T(8,128)S(1)}, f32[2,96,256]{2,1,0:T(8,128)S(1)}, u32[]{:S(2)}, u32[]{:S(2)}) %collective-permute-start.7) | collective-permute-done | bytes 196640 | tf_op jit(solution)/shard_map/ppermute | solution.py:293
  37.9 1.7 %update_slots.1 = f32[8,256,256]{2,1,0:T(8,128)} custom-call(s32[5,8]{1,0:T(8,128)S(4)} %get-tuple-element.16.guide, bf16[4,256,192]{2,1,0:T(8,128)(2,1)S(1)} %get-tuple-element.23.wide, bf16[4,256,96]{2,1,0:T(8,128)(2,1)S(1)} %get-tuple-element.24.low, f32[2,96,256]{2,1,0:T(8,128)S(1)} %collective-permute-done.6.first, ...), custom_call_target="tpu_custom_call" | custom-call | tf_op jit(solution)/shard_map/update_slots/pallas_call | solution.py:246
  (2 shorter events, 0.1 us)
Async XLA Ops:
  0.6 1.6 %collective-permute-start = (f32[96,256]{1,0:T(8,128)}, f32[96,256]{1,0:T(8,128)S(1)}, u32[]{:S(2)}, u32[]{:S(2)}) collective-permute-start(f32[96,256]{1,0:T(8,128)} %param.5), channel_id=1, source_target_pairs={{0,1},{1,0},{2,3},{3,2},{4,5},{5,4},{6,7},{7,6},{8,9},{9,8},{10,11... | collective-permute-start | bytes 294920 | tf_op jit(solution)/shard_map/ppermute | solution.py:279
  3.1 9.4 %collective-permute-start.1 = (f32[2,96,256]{2,1,0:T(8,128)S(1)}, f32[2,96,256]{2,1,0:T(8,128)S(1)}, u32[]{:S(2)}, u32[]{:S(2)}) collective-permute-start(f32[2,96,256]{2,1,0:T(8,128)S(1)} %pad_maximum_fusion.samples.refs_0_), channel_id=1, source_target_pairs={{3,0},{0,4},{2,8},{1,12},{7,1},{4,5},{6,9},{5,13},{8,2},{11,6},{9,... | collective-permute-start | bytes 589832 | tf_op jit(solution)/shard_map/ppermute | solution.py:281
  5.7 9.9 %collective-permute-start.2 = (f32[2,96,256]{2,1,0:T(8,128)S(1)}, f32[2,96,256]{2,1,0:T(8,128)S(1)}, u32[]{:S(2)}, u32[]{:S(2)}) collective-permute-start(f32[2,96,256]{2,1,0:T(8,128)S(1)} %pad_maximum_fusion.samples.refs_0_), channel_id=1, source_target_pairs={{0,0},{3,4},{1,8},{2,12},{4,1},{7,5},{5,9},{6,13},{11,2},{8,6},{10... | collective-permute-start | bytes 589832 | tf_op jit(solution)/shard_map/ppermute | solution.py:281
  16.2 1.5 %collective-permute-start.3 = (f32[2,96,256]{2,1,0:T(8,128)S(1)}, f32[2,96,256]{2,1,0:T(8,128)S(1)}, u32[]{:S(2)}, u32[]{:S(2)}) collective-permute-start(f32[2,96,256]{2,1,0:T(8,128)S(1)} %get-tuple-element.21), channel_id=1, source_target_pairs={{0,1},{1,0},{2,3},{3,2},{4,5},{5,4},{6,7},{7,6},{8,9},{9,8},{10,11... | collective-permute-start | bytes 589832 | tf_op jit(solution)/shard_map/ppermute | solution.py:285
  17.8 7.0 %collective-permute-start.4 = (f32[2,96,256]{2,1,0:T(8,128)S(1)}, f32[2,96,256]{2,1,0:T(8,128)S(1)}, u32[]{:S(2)}, u32[]{:S(2)}) collective-permute-start(f32[2,96,256]{2,1,0:T(8,128)S(1)} %add.6), channel_id=1, source_target_pairs={{0,2},{2,0},{1,3},{3,1},{4,6},{6,4},{5,7},{7,5},{8,10},{10,8},{9,1... | collective-permute-start | bytes 589832 | tf_op jit(solution)/shard_map/ppermute | solution.py:288
  24.8 9.8 %collective-permute-start.5 = (f32[2,96,256]{2,1,0:T(8,128)S(1)}, f32[2,96,256]{2,1,0:T(8,128)S(1)}, u32[]{:S(2)}, u32[]{:S(2)}) collective-permute-start(f32[2,96,256]{2,1,0:T(8,128)S(1)} %pad_maximum_fusion.samples.refs_0_), channel_id=1, source_target_pairs={{0,2},{2,0},{1,3},{3,1},{4,6},{6,4},{5,7},{7,5},{8,10},{10,8},{9,1... | collective-permute-start | bytes 589832 | tf_op jit(solution)/shard_map/ppermute | solution.py:291
  25.1 9.8 %collective-permute-start.8 = (f32[2,96,256]{2,1,0:T(8,128)S(1)}, f32[2,96,256]{2,1,0:T(8,128)S(1)}, u32[]{:S(2)}, u32[]{:S(2)}) collective-permute-start(f32[2,96,256]{2,1,0:T(8,128)S(1)} %add.7.own_image), channel_id=1, source_target_pairs={{0,1},{1,0},{2,3},{3,2},{4,5},{5,4},{6,7},{7,6},{8,9},{9,8},{10,11... | collective-permute-start | bytes 589832 | tf_op jit(solution)/shard_map/ppermute | solution.py:295
  25.2 11.5 %collective-permute-start.6 = (f32[2,96,256]{2,1,0:T(8,128)S(1)}, f32[2,96,256]{2,1,0:T(8,128)S(1)}, u32[]{:S(2)}, u32[]{:S(2)}) collective-permute-start(f32[2,96,256]{2,1,0:T(8,128)S(1)} %add.7.own_image), channel_id=1, source_target_pairs={{3,0},{0,4},{2,8},{1,12},{7,1},{4,5},{6,9},{5,13},{8,2},{11,6},{9,... | collective-permute-start | bytes 589832 | tf_op jit(solution)/shard_map/ppermute | solution.py:293
  27.2 10.8 %collective-permute-start.7 = (f32[2,96,256]{2,1,0:T(8,128)S(1)}, f32[2,96,256]{2,1,0:T(8,128)S(1)}, u32[]{:S(2)}, u32[]{:S(2)}) collective-permute-start(f32[2,96,256]{2,1,0:T(8,128)S(1)} %add.7.own_image), channel_id=1, source_target_pairs={{0,0},{3,4},{1,8},{2,12},{4,1},{7,5},{5,9},{6,13},{11,2},{8,6},{10... | collective-permute-start | bytes 589832 | tf_op jit(solution)/shard_map/ppermute | solution.py:293

commit v9 on v8

--- a/solution.py
+++ b/solution.py
@@ -276,7 +276,12 @@
     def around(size, turn):
         return [(j, (j + turn) % size) for j in range(size)]
 
-    pair = jnp.stack([samples, lax.ppermute(samples, "rep", around(2, 1))])
+    first = samples[None]
+    pair = lax.dynamic_update_slice(jnp.zeros((2, *samples.shape), f32), first, (0, 0, 0))
+    pair = lax.optimization_barrier(pair)
+    pair = lax.dynamic_update_slice(
+        pair, lax.ppermute(first, "rep", around(2, 1)), (1, 0, 0)
+    )
     col_pieces = [
         lax.ppermute(pair, grid_axes, links(sample_source, turn)) for turn in range(cols)
     ]

time: 40 us -> 39.1 us (0.978)
  local copies, waits for them, and re-layouts: 0 us -> 0.92 us
  other arithmetic: 0.96 us -> 0.05 us
  waiting for transfers between devices: 16.9 us -> 16 us
    dynamic_update_slice x0 -> x2, local copies, waits for them, and re-layouts: none -> 0.92 us  [the longest x1 0.91 us: on_device(): lax.dynamic_update_slice(jnp.zeros((2, *samples.shape), f32), first, (0,...]
    ppermute x1, waiting for transfers between devices: 1.5 us -> 0.59 us  [on_device(): lax.ppermute(first, 'rep', around(2, 1))]
    another operation x1 -> x0, other arithmetic: 0.91 us -> none  [on_device(): pair = jnp.stack([samples, lax.ppermute(samples, 'rep', around(2, 1))])]
  transfers between devices with their start and end apart: 9 -> 9, of which waited for: 6 -> 6; matrix products, arithmetic and copies ran while one was open for 0% -> 2% of each run, Pallas kernels for 11% -> 11%
where the time goes in v9:
time: 39.1 us; the launch traced here: 38.8 us
  waiting for transfers between devices  16 us (41%)
  starting transfers between devices  13.7 us (35%)
  Pallas kernels  6.65 us (17%)
  between operations  1.39 us (4%)
  local copies, waits for them, and re-layouts  0.92 us (2%)
    ppermute x1, waiting for transfers between devices, on_device(): image = image + lax.ppermute(chip, 'col', around(cols, turn))  6.93 us
    ppermute x2, starting transfers between devices, on_device(): lax.ppermute(image, grid_axes, links(image_source, turn))  6.73 us
    ppermute x2, starting transfers between devices, on_device(): lax.ppermute(pair, grid_axes, links(sample_source, turn))  6.43 us
    ppermute x2, waiting for transfers between devices, on_device(): lax.ppermute(pair, grid_axes, links(sample_source, turn))  3.11 us
    ppermute x1, waiting for transfers between devices, on_device(): lax.ppermute(late, 'col', around(cols, turn))  2.72 us
    pallas_call x1, Pallas kernels, prepare(): pl.pallas_call(functools.partial(prepare_kernel, groups), out_shape=(pltp...  2.28 us
    pallas_call x1, Pallas kernels, update_slots(): pl.pallas_call(slots_kernel, out_shape=jax.ShapeDtypeStruct(moved.shape,...  1.74 us
    pallas_call x1, Pallas kernels, half_gradient(): pl.pallas_call(half_gradient_kernel, out_shape=(jax.ShapeDtypeStruct(tile...  1.67 us
  transfers between devices with their start and end apart: 9, of which 6 were waited for; matrix products, arithmetic and copies ran while one was open for 2% of the time, Pallas kernels for 11%

profile of v9, /device:TPU:6, one launch (start us, length us, event | category | flops | bytes accessed | tf_op | source)
XLA Modules:
  0.0 38.8 jit_solution(8642380002694461750)
XLA Ops:
  0.6 0.1 collective-permute-start
  0.7 0.9 %dynamic_update_slice.6 = f32[2,96,256]{2,1,0:T(8,128)S(1)} pad(f32[1,96,256]{2,1,0:T(8,128)} %bitcast.9, f32[]{:T(128)} %constant.0.clone.1), padding=0_1x0_0x0_0 | pad | bytes 294916 | tf_op jit(solution)/shard_map/dynamic_update_slice | solution.py:280
  1.6 0.6 %collective-permute-done = f32[1,96,256]{2,1,0:T(8,128)S(1)} collective-permute-done((f32[1,96,256]{2,1,0:T(8,128)}, f32[1,96,256]{2,1,0:T(8,128)S(1)}, u32[]{:S(2)}, u32[]{:S(2)}) %collective-permute-start) | collective-permute-done | bytes 98336 | tf_op jit(solution)/shard_map/ppermute | solution.py:283
  2.2 2.6 %collective-permute-start.1 = (f32[2,96,256]{2,1,0:T(8,128)S(1)}, f32[2,96,256]{2,1,0:T(8,128)S(1)}, u32[]{:S(2)}, u32[]{:S(2)}) collective-permute-start(f32[2,96,256]{2,1,0:T(8,128)S(1)} %constant_dynamic-update-slice_fusion.samples.refs_0_), channel_id=1, source_target_pairs={{3,0},{0,4},{2,8},{1,12},{7,1},{4,5},{6,9},{5,13},{8,2},{11,6},{9,... | collective-permute-start | bytes 589832 | tf_op jit(solution)/shard_map/ppermute | solution.py:286
  4.8 3.8 %collective-permute-start.2 = (f32[2,96,256]{2,1,0:T(8,128)S(1)}, f32[2,96,256]{2,1,0:T(8,128)S(1)}, u32[]{:S(2)}, u32[]{:S(2)}) collective-permute-start(f32[2,96,256]{2,1,0:T(8,128)S(1)} %constant_dynamic-update-slice_fusion.samples.refs_0_), channel_id=1, source_target_pairs={{0,0},{3,4},{1,8},{2,12},{4,1},{7,5},{5,9},{6,13},{11,2},{8,6},{10... | collective-permute-start | bytes 589832 | tf_op jit(solution)/shard_map/ppermute | solution.py:286
  9.3 2.3 %prepare.1 = (s32[5,8]{1,0:T(8,128)S(4)}, f32[1,256,256]{2,1,0:T(8,128)S(1)}, f32[8,256,256]{2,1,0:T(8,128)S(1)}, bf16[8,256,256]{2,1,0:T(8,128)(2,1)S(1)}, bf16[8,256,256]{2,1,0:T(8,128)(2,1)S(1)}) custom-call(s32[2,8]{1,0:T(2,128)} %bitcast.10, s32[1,1]{1,0:T(1,128)S(6)} %copy.8.refs_1_, f32[1,256,256]{2,1,0:T(8,128)} %refs_2_.1, f32[8,256,256]{2,1,0:T(8,128)} %bitcast.6), custom_call_target="tpu_custom_call" | custom-call | tf_op jit(solution)/shard_map/prepare/pallas_call | solution.py:82
  11.6 0.0 collective-permute-done.1.refs_0_
  11.6 3.1 %collective-permute-done.2.refs_1_ = f32[2,96,256]{2,1,0:T(8,128)S(1)} collective-permute-done((f32[2,96,256]{2,1,0:T(8,128)S(1)}, f32[2,96,256]{2,1,0:T(8,128)S(1)}, u32[]{:S(2)}, u32[]{:S(2)}) %collective-permute-start.2) | collective-permute-done | bytes 196640 | tf_op jit(solution)/shard_map/ppermute | solution.py:286
  14.7 0.6 %partial_image.1 = (f32[2,96,256]{2,1,0:T(8,128)S(1)}, f32[2,96,256]{2,1,0:T(8,128)S(1)}, bf16[4,192,256]{2,1,0:T(8,128)(2,1)S(1)}) custom-call(s32[5,8]{1,0:T(8,128)S(4)} %get-tuple-element.16.guide, f32[2,96,256]{2,1,0:T(8,128)S(1)} %constant_dynamic-update-slice_fusion.samples.refs_0_, f32[1,256,256]{2,1,0:T(8,128)S(1)} %get-tuple-element.17.diag, ...), custom_call_target="tpu_custom_call" | custom-call | tf_op jit(solution)/shard_map/partial_image/pallas_call | solution.py:132
  15.3 0.1 collective-permute-start.3
  15.4 1.4 %collective-permute-done.3 = f32[2,96,256]{2,1,0:T(8,128)S(1)} collective-permute-done((f32[2,96,256]{2,1,0:T(8,128)S(1)}, f32[2,96,256]{2,1,0:T(8,128)S(1)}, u32[]{:S(2)}, u32[]{:S(2)}) %collective-permute-start.3) | collective-permute-done | bytes 196640 | tf_op jit(solution)/shard_map/ppermute | solution.py:290
  16.9 0.1 collective-permute-start.4
  16.9 6.9 %collective-permute-done.4 = f32[2,96,256]{2,1,0:T(8,128)S(1)} collective-permute-done((f32[2,96,256]{2,1,0:T(8,128)S(1)}, f32[2,96,256]{2,1,0:T(8,128)S(1)}, u32[]{:S(2)}, u32[]{:S(2)}) %collective-permute-start.4) | collective-permute-done | bytes 196640 | tf_op jit(solution)/shard_map/ppermute | solution.py:293
  23.9 0.4 collective-permute-start.5
  24.3 0.0 collective-permute-start.8
  24.3 2.0 %collective-permute-start.6 = (f32[2,96,256]{2,1,0:T(8,128)S(1)}, f32[2,96,256]{2,1,0:T(8,128)S(1)}, u32[]{:S(2)}, u32[]{:S(2)}) collective-permute-start(f32[2,96,256]{2,1,0:T(8,128)S(1)} %add.9.own_image), channel_id=1, source_target_pairs={{3,0},{0,4},{2,8},{1,12},{7,1},{4,5},{6,9},{5,13},{8,2},{11,6},{9,... | collective-permute-start | bytes 589832 | tf_op jit(solution)/shard_map/ppermute | solution.py:298
  26.3 4.7 %collective-permute-start.7 = (f32[2,96,256]{2,1,0:T(8,128)S(1)}, f32[2,96,256]{2,1,0:T(8,128)S(1)}, u32[]{:S(2)}, u32[]{:S(2)}) collective-permute-start(f32[2,96,256]{2,1,0:T(8,128)S(1)} %add.9.own_image), channel_id=1, source_target_pairs={{0,0},{3,4},{1,8},{2,12},{4,1},{7,5},{5,9},{6,13},{11,2},{8,6},{10... | collective-permute-start | bytes 589832 | tf_op jit(solution)/shard_map/ppermute | solution.py:298
  31.0 2.7 %collective-permute-done.5.refs_1_ = f32[2,96,256]{2,1,0:T(8,128)S(1)} collective-permute-done((f32[2,96,256]{2,1,0:T(8,128)S(1)}, f32[2,96,256]{2,1,0:T(8,128)S(1)}, u32[]{:S(2)}, u32[]{:S(2)}) %collective-permute-start.5) | collective-permute-done | bytes 196640 | tf_op jit(solution)/shard_map/ppermute | solution.py:296
  33.7 0.4 row_panel.1
  34.1 0.0 collective-permute-done.8.other_image
  34.1 1.7 %half_gradient.1 = (f32[8,256,256]{2,1,0:T(8,128)S(1)}, f32[1,256,256]{2,1,0:T(8,128)}) custom-call(s32[5,8]{1,0:T(8,128)S(4)} %get-tuple-element.16.guide, f32[2,96,256]{2,1,0:T(8,128)S(1)} %add.9.own_image, f32[2,96,256]{2,1,0:T(8,128)S(1)} %collective-permute-done.8.other_image, f32[2,96,256]{2,1,0:T(8,128)S(1)} %constant_dynamic-update-slice_fusion.samples.refs_0_, ...), custom_call_target="tpu_custom_call" | custom-call | tf_op jit(solution)/shard_map/half_gradient/pallas_call | solution.py:176
  35.8 0.0 collective-permute-done.6.first
  35.8 1.3 %collective-permute-done.7.second = f32[2,96,256]{2,1,0:T(8,128)S(1)} collective-permute-done((f32[2,96,256]{2,1,0:T(8,128)S(1)}, f32[2,96,256]{2,1,0:T(8,128)S(1)}, u32[]{:S(2)}, u32[]{:S(2)}) %collective-permute-start.7) | collective-permute-done | bytes 196640 | tf_op jit(solution)/shard_map/ppermute | solution.py:298
  37.0 1.7 %update_slots.1 = f32[8,256,256]{2,1,0:T(8,128)} custom-call(s32[5,8]{1,0:T(8,128)S(4)} %get-tuple-element.16.guide, bf16[4,256,192]{2,1,0:T(8,128)(2,1)S(1)} %get-tuple-element.23.wide, bf16[4,256,96]{2,1,0:T(8,128)(2,1)S(1)} %get-tuple-element.24.low, f32[2,96,256]{2,1,0:T(8,128)S(1)} %collective-permute-done.6.first, ...), custom_call_target="tpu_custom_call" | custom-call | tf_op jit(solution)/shard_map/update_slots/pallas_call | solution.py:246
  (3 shorter events, 0.1 us)
Async XLA Ops:
  0.6 1.6 %collective-permute-start = (f32[1,96,256]{2,1,0:T(8,128)}, f32[1,96,256]{2,1,0:T(8,128)S(1)}, u32[]{:S(2)}, u32[]{:S(2)}) collective-permute-start(f32[1,96,256]{2,1,0:T(8,128)} %bitcast.8), channel_id=1, source_target_pairs={{0,1},{1,0},{2,3},{3,2},{4,5},{5,4},{6,7},{7,6},{8,9},{9,8},{10,11... | collective-permute-start | bytes 294920 | tf_op jit(solution)/shard_map/ppermute | solution.py:283
  2.2 9.4 %collective-permute-start.1 = (f32[2,96,256]{2,1,0:T(8,128)S(1)}, f32[2,96,256]{2,1,0:T(8,128)S(1)}, u32[]{:S(2)}, u32[]{:S(2)}) collective-permute-start(f32[2,96,256]{2,1,0:T(8,128)S(1)} %constant_dynamic-update-slice_fusion.samples.refs_0_), channel_id=1, source_target_pairs={{3,0},{0,4},{2,8},{1,12},{7,1},{4,5},{6,9},{5,13},{8,2},{11,6},{9,... | collective-permute-start | bytes 589832 | tf_op jit(solution)/shard_map/ppermute | solution.py:286
  4.8 9.9 %collective-permute-start.2 = (f32[2,96,256]{2,1,0:T(8,128)S(1)}, f32[2,96,256]{2,1,0:T(8,128)S(1)}, u32[]{:S(2)}, u32[]{:S(2)}) collective-permute-start(f32[2,96,256]{2,1,0:T(8,128)S(1)} %constant_dynamic-update-slice_fusion.samples.refs_0_), channel_id=1, source_target_pairs={{0,0},{3,4},{1,8},{2,12},{4,1},{7,5},{5,9},{6,13},{11,2},{8,6},{10... | collective-permute-start | bytes 589832 | tf_op jit(solution)/shard_map/ppermute | solution.py:286
  15.3 1.5 %collective-permute-start.3 = (f32[2,96,256]{2,1,0:T(8,128)S(1)}, f32[2,96,256]{2,1,0:T(8,128)S(1)}, u32[]{:S(2)}, u32[]{:S(2)}) collective-permute-start(f32[2,96,256]{2,1,0:T(8,128)S(1)} %get-tuple-element.21), channel_id=1, source_target_pairs={{0,1},{1,0},{2,3},{3,2},{4,5},{5,4},{6,7},{7,6},{8,9},{9,8},{10,11... | collective-permute-start | bytes 589832 | tf_op jit(solution)/shard_map/ppermute | solution.py:290
  16.9 7.0 %collective-permute-start.4 = (f32[2,96,256]{2,1,0:T(8,128)S(1)}, f32[2,96,256]{2,1,0:T(8,128)S(1)}, u32[]{:S(2)}, u32[]{:S(2)}) collective-permute-start(f32[2,96,256]{2,1,0:T(8,128)S(1)} %add.8), channel_id=1, source_target_pairs={{0,2},{2,0},{1,3},{3,1},{4,6},{6,4},{5,7},{7,5},{8,10},{10,8},{9,1... | collective-permute-start | bytes 589832 | tf_op jit(solution)/shard_map/ppermute | solution.py:293
  23.9 9.8 %collective-permute-start.5 = (f32[2,96,256]{2,1,0:T(8,128)S(1)}, f32[2,96,256]{2,1,0:T(8,128)S(1)}, u32[]{:S(2)}, u32[]{:S(2)}) collective-permute-start(f32[2,96,256]{2,1,0:T(8,128)S(1)} %constant_dynamic-update-slice_fusion.samples.refs_0_), channel_id=1, source_target_pairs={{0,2},{2,0},{1,3},{3,1},{4,6},{6,4},{5,7},{7,5},{8,10},{10,8},{9,1... | collective-permute-start | bytes 589832 | tf_op jit(solution)/shard_map/ppermute | solution.py:296
  24.3 9.8 %collective-permute-start.8 = (f32[2,96,256]{2,1,0:T(8,128)S(1)}, f32[2,96,256]{2,1,0:T(8,128)S(1)}, u32[]{:S(2)}, u32[]{:S(2)}) collective-permute-start(f32[2,96,256]{2,1,0:T(8,128)S(1)} %add.9.own_image), channel_id=1, source_target_pairs={{0,1},{1,0},{2,3},{3,2},{4,5},{5,4},{6,7},{7,6},{8,9},{9,8},{10,11... | collective-permute-start | bytes 589832 | tf_op jit(solution)/shard_map/ppermute | solution.py:300
  24.3 11.5 %collective-permute-start.6 = (f32[2,96,256]{2,1,0:T(8,128)S(1)}, f32[2,96,256]{2,1,0:T(8,128)S(1)}, u32[]{:S(2)}, u32[]{:S(2)}) collective-permute-start(f32[2,96,256]{2,1,0:T(8,128)S(1)} %add.9.own_image), channel_id=1, source_target_pairs={{3,0},{0,4},{2,8},{1,12},{7,1},{4,5},{6,9},{5,13},{8,2},{11,6},{9,... | collective-permute-start | bytes 589832 | tf_op jit(solution)/shard_map/ppermute | solution.py:298
  26.3 10.8 %collective-permute-start.7 = (f32[2,96,256]{2,1,0:T(8,128)S(1)}, f32[2,96,256]{2,1,0:T(8,128)S(1)}, u32[]{:S(2)}, u32[]{:S(2)}) collective-permute-start(f32[2,96,256]{2,1,0:T(8,128)S(1)} %add.9.own_image), channel_id=1, source_target_pairs={{0,0},{3,4},{1,8},{2,12},{4,1},{7,5},{5,9},{6,13},{11,2},{8,6},{10... | collective-permute-start | bytes 589832 | tf_op jit(solution)/shard_map/ppermute | solution.py:298

commit v10 on v9

--- a/solution.py
+++ b/solution.py
@@ -299,6 +299,7 @@
     ]
     other = lax.ppermute(image, "rep", around(2, 1))
     moved, new_diag = half_gradient(guide, image, other, pair, panel, own_diag, held)
+    beside, moved = lax.optimization_barrier((beside, moved))
     wide, low = row_panel([pair, *beside])
     new_slots = update_slots(guide, wide, low, first, second, moved)
     return new_slots.reshape(omega_slots.shape), new_diag

time: 39.1 us -> 39 us (level)
  waiting for transfers between devices: 16 us -> 16.4 us
where the time goes in v10:
time: 39 us; the launch traced here: 38.8 us
  waiting for transfers between devices  16.4 us (42%)
  starting transfers between devices  13.5 us (35%)
  Pallas kernels  6.65 us (17%)
  between operations  1.4 us (4%)
  local copies, waits for them, and re-layouts  0.92 us (2%)
    ppermute x1, waiting for transfers between devices, on_device(): image = image + lax.ppermute(chip, 'col', around(cols, turn))  6.93 us
    ppermute x2, starting transfers between devices, on_device(): lax.ppermute(pair, grid_axes, links(sample_source, turn))  6.43 us
    ppermute x2, starting transfers between devices, on_device(): lax.ppermute(image, grid_axes, links(image_source, turn))  6.39 us
    ppermute x2, waiting for transfers between devices, on_device(): lax.ppermute(pair, grid_axes, links(sample_source, turn))  3.11 us
    ppermute x1, waiting for transfers between devices, on_device(): lax.ppermute(late, 'col', around(cols, turn))  3.1 us
    pallas_call x1, Pallas kernels, prepare(): pl.pallas_call(functools.partial(prepare_kernel, groups), out_shape=(pltp...  2.28 us
    pallas_call x1, Pallas kernels, update_slots(): pl.pallas_call(slots_kernel, out_shape=jax.ShapeDtypeStruct(moved.shape,...  1.74 us
    pallas_call x1, Pallas kernels, half_gradient(): pl.pallas_call(half_gradient_kernel, out_shape=(jax.ShapeDtypeStruct(tile...  1.67 us
  transfers between devices with their start and end apart: 9, of which 6 were waited for; matrix products, arithmetic and copies ran while one was open for 2% of the time, Pallas kernels for 11%

profile of v10, /device:TPU:6, one launch (start us, length us, event | category | flops | bytes accessed | tf_op | source)
XLA Modules:
  0.0 38.8 jit_solution(9392498837740021929)
XLA Ops:
  0.6 0.1 collective-permute-start
  0.7 0.9 %dynamic_update_slice.6 = f32[2,96,256]{2,1,0:T(8,128)S(1)} pad(f32[1,96,256]{2,1,0:T(8,128)} %bitcast.9, f32[]{:T(128)} %constant.0.clone.1), padding=0_1x0_0x0_0 | pad | bytes 294916 | tf_op jit(solution)/shard_map/dynamic_update_slice | solution.py:280
  1.6 0.6 %collective-permute-done = f32[1,96,256]{2,1,0:T(8,128)S(1)} collective-permute-done((f32[1,96,256]{2,1,0:T(8,128)}, f32[1,96,256]{2,1,0:T(8,128)S(1)}, u32[]{:S(2)}, u32[]{:S(2)}) %collective-permute-start) | collective-permute-done | bytes 98336 | tf_op jit(solution)/shard_map/ppermute | solution.py:283
  2.2 2.6 %collective-permute-start.1 = (f32[2,96,256]{2,1,0:T(8,128)S(1)}, f32[2,96,256]{2,1,0:T(8,128)S(1)}, u32[]{:S(2)}, u32[]{:S(2)}) collective-permute-start(f32[2,96,256]{2,1,0:T(8,128)S(1)} %constant_dynamic-update-slice_fusion.samples.refs_0_), channel_id=1, source_target_pairs={{3,0},{0,4},{2,8},{1,12},{7,1},{4,5},{6,9},{5,13},{8,2},{11,6},{9,... | collective-permute-start | bytes 589832 | tf_op jit(solution)/shard_map/ppermute | solution.py:286
  4.8 3.8 %collective-permute-start.2 = (f32[2,96,256]{2,1,0:T(8,128)S(1)}, f32[2,96,256]{2,1,0:T(8,128)S(1)}, u32[]{:S(2)}, u32[]{:S(2)}) collective-permute-start(f32[2,96,256]{2,1,0:T(8,128)S(1)} %constant_dynamic-update-slice_fusion.samples.refs_0_), channel_id=1, source_target_pairs={{0,0},{3,4},{1,8},{2,12},{4,1},{7,5},{5,9},{6,13},{11,2},{8,6},{10... | collective-permute-start | bytes 589832 | tf_op jit(solution)/shard_map/ppermute | solution.py:286
  9.3 2.3 %prepare.1 = (s32[5,8]{1,0:T(8,128)S(4)}, f32[1,256,256]{2,1,0:T(8,128)S(1)}, f32[8,256,256]{2,1,0:T(8,128)S(1)}, bf16[8,256,256]{2,1,0:T(8,128)(2,1)S(1)}, bf16[8,256,256]{2,1,0:T(8,128)(2,1)S(1)}) custom-call(s32[2,8]{1,0:T(2,128)} %bitcast.10, s32[1,1]{1,0:T(1,128)S(6)} %copy.8.refs_1_, f32[1,256,256]{2,1,0:T(8,128)} %refs_2_.1, f32[8,256,256]{2,1,0:T(8,128)} %bitcast.6), custom_call_target="tpu_custom_call" | custom-call | tf_op jit(solution)/shard_map/prepare/pallas_call | solution.py:82
  11.6 0.0 collective-permute-done.1.refs_0_
  11.6 3.1 %collective-permute-done.2.refs_1_ = f32[2,96,256]{2,1,0:T(8,128)S(1)} collective-permute-done((f32[2,96,256]{2,1,0:T(8,128)S(1)}, f32[2,96,256]{2,1,0:T(8,128)S(1)}, u32[]{:S(2)}, u32[]{:S(2)}) %collective-permute-start.2) | collective-permute-done | bytes 196640 | tf_op jit(solution)/shard_map/ppermute | solution.py:286
  14.7 0.6 %partial_image.1 = (f32[2,96,256]{2,1,0:T(8,128)S(1)}, f32[2,96,256]{2,1,0:T(8,128)S(1)}, bf16[4,192,256]{2,1,0:T(8,128)(2,1)S(1)}) custom-call(s32[5,8]{1,0:T(8,128)S(4)} %get-tuple-element.18.guide, f32[2,96,256]{2,1,0:T(8,128)S(1)} %constant_dynamic-update-slice_fusion.samples.refs_0_, f32[1,256,256]{2,1,0:T(8,128)S(1)} %get-tuple-element.19.diag, ...), custom_call_target="tpu_custom_call" | custom-call | tf_op jit(solution)/shard_map/partial_image/pallas_call | solution.py:132
  15.3 0.1 collective-permute-start.3
  15.4 1.4 %collective-permute-done.3 = f32[2,96,256]{2,1,0:T(8,128)S(1)} collective-permute-done((f32[2,96,256]{2,1,0:T(8,128)S(1)}, f32[2,96,256]{2,1,0:T(8,128)S(1)}, u32[]{:S(2)}, u32[]{:S(2)}) %collective-permute-start.3) | collective-permute-done | bytes 196640 | tf_op jit(solution)/shard_map/ppermute | solution.py:290
  16.9 0.1 collective-permute-start.4
  16.9 6.9 %collective-permute-done.4 = f32[2,96,256]{2,1,0:T(8,128)S(1)} collective-permute-done((f32[2,96,256]{2,1,0:T(8,128)S(1)}, f32[2,96,256]{2,1,0:T(8,128)S(1)}, u32[]{:S(2)}, u32[]{:S(2)}) %collective-permute-start.4) | collective-permute-done | bytes 196640 | tf_op jit(solution)/shard_map/ppermute | solution.py:293
  23.9 0.1 collective-permute-start.6
  24.0 0.4 collective-permute-start.5
  24.3 2.0 %collective-permute-start.7 = (f32[2,96,256]{2,1,0:T(8,128)S(1)}, f32[2,96,256]{2,1,0:T(8,128)S(1)}, u32[]{:S(2)}, u32[]{:S(2)}) collective-permute-start(f32[2,96,256]{2,1,0:T(8,128)S(1)} %add.9.own_image), channel_id=1, source_target_pairs={{3,0},{0,4},{2,8},{1,12},{7,1},{4,5},{6,9},{5,13},{8,2},{11,6},{9,... | collective-permute-start | bytes 589832 | tf_op jit(solution)/shard_map/ppermute | solution.py:298
  26.3 4.4 %collective-permute-start.8 = (f32[2,96,256]{2,1,0:T(8,128)S(1)}, f32[2,96,256]{2,1,0:T(8,128)S(1)}, u32[]{:S(2)}, u32[]{:S(2)}) collective-permute-start(f32[2,96,256]{2,1,0:T(8,128)S(1)} %add.9.own_image), channel_id=1, source_target_pairs={{0,0},{3,4},{1,8},{2,12},{4,1},{7,5},{5,9},{6,13},{11,2},{8,6},{10... | collective-permute-start | bytes 589832 | tf_op jit(solution)/shard_map/ppermute | solution.py:298
  30.7 0.0 collective-permute-done.6.other_image
  30.7 1.7 %half_gradient.1 = (f32[8,256,256]{2,1,0:T(8,128)S(1)}, f32[1,256,256]{2,1,0:T(8,128)}) custom-call(s32[5,8]{1,0:T(8,128)S(4)} %get-tuple-element.18.guide, f32[2,96,256]{2,1,0:T(8,128)S(1)} %add.9.own_image, f32[2,96,256]{2,1,0:T(8,128)S(1)} %collective-permute-done.6.other_image, f32[2,96,256]{2,1,0:T(8,128)S(1)} %constant_dynamic-update-slice_fusion.samples.refs_0_, ...), custom_call_target="tpu_custom_call" | custom-call | tf_op jit(solution)/shard_map/half_gradient/pallas_call | solution.py:176
  32.4 3.1 %collective-permute-done.5.refs_1_ = f32[2,96,256]{2,1,0:T(8,128)S(1)} collective-permute-done((f32[2,96,256]{2,1,0:T(8,128)S(1)}, f32[2,96,256]{2,1,0:T(8,128)S(1)}, u32[]{:S(2)}, u32[]{:S(2)}) %collective-permute-start.5) | collective-permute-done | bytes 196640 | tf_op jit(solution)/shard_map/ppermute | solution.py:296
  35.5 0.4 row_panel.1
  35.9 0.0 collective-permute-done.7.first
  35.9 1.2 %collective-permute-done.8.second = f32[2,96,256]{2,1,0:T(8,128)S(1)} collective-permute-done((f32[2,96,256]{2,1,0:T(8,128)S(1)}, f32[2,96,256]{2,1,0:T(8,128)S(1)}, u32[]{:S(2)}, u32[]{:S(2)}) %collective-permute-start.8) | collective-permute-done | bytes 196640 | tf_op jit(solution)/shard_map/ppermute | solution.py:298
  37.1 1.7 %update_slots.1 = f32[8,256,256]{2,1,0:T(8,128)} custom-call(s32[5,8]{1,0:T(8,128)S(4)} %get-tuple-element.18.guide, bf16[4,256,192]{2,1,0:T(8,128)(2,1)S(1)} %get-tuple-element.30.wide, bf16[4,256,96]{2,1,0:T(8,128)(2,1)S(1)} %get-tuple-element.31.low, f32[2,96,256]{2,1,0:T(8,128)S(1)} %collective-permute-done.7.first, ...), custom_call_target="tpu_custom_call" | custom-call | tf_op jit(solution)/shard_map/update_slots/pallas_call | solution.py:246
  (3 shorter events, 0.1 us)
Async XLA Ops:
  0.6 1.6 %collective-permute-start = (f32[1,96,256]{2,1,0:T(8,128)}, f32[1,96,256]{2,1,0:T(8,128)S(1)}, u32[]{:S(2)}, u32[]{:S(2)}) collective-permute-start(f32[1,96,256]{2,1,0:T(8,128)} %bitcast.8), channel_id=1, source_target_pairs={{0,1},{1,0},{2,3},{3,2},{4,5},{5,4},{6,7},{7,6},{8,9},{9,8},{10,11... | collective-permute-start | bytes 294920 | tf_op jit(solution)/shard_map/ppermute | solution.py:283
  2.2 9.4 %collective-permute-start.1 = (f32[2,96,256]{2,1,0:T(8,128)S(1)}, f32[2,96,256]{2,1,0:T(8,128)S(1)}, u32[]{:S(2)}, u32[]{:S(2)}) collective-permute-start(f32[2,96,256]{2,1,0:T(8,128)S(1)} %constant_dynamic-update-slice_fusion.samples.refs_0_), channel_id=1, source_target_pairs={{3,0},{0,4},{2,8},{1,12},{7,1},{4,5},{6,9},{5,13},{8,2},{11,6},{9,... | collective-permute-start | bytes 589832 | tf_op jit(solution)/shard_map/ppermute | solution.py:286
  4.8 9.9 %collective-permute-start.2 = (f32[2,96,256]{2,1,0:T(8,128)S(1)}, f32[2,96,256]{2,1,0:T(8,128)S(1)}, u32[]{:S(2)}, u32[]{:S(2)}) collective-permute-start(f32[2,96,256]{2,1,0:T(8,128)S(1)} %constant_dynamic-update-slice_fusion.samples.refs_0_), channel_id=1, source_target_pairs={{0,0},{3,4},{1,8},{2,12},{4,1},{7,5},{5,9},{6,13},{11,2},{8,6},{10... | collective-permute-start | bytes 589832 | tf_op jit(solution)/shard_map/ppermute | solution.py:286
  15.3 1.5 %collective-permute-start.3 = (f32[2,96,256]{2,1,0:T(8,128)S(1)}, f32[2,96,256]{2,1,0:T(8,128)S(1)}, u32[]{:S(2)}, u32[]{:S(2)}) collective-permute-start(f32[2,96,256]{2,1,0:T(8,128)S(1)} %get-tuple-element.23), channel_id=1, source_target_pairs={{0,1},{1,0},{2,3},{3,2},{4,5},{5,4},{6,7},{7,6},{8,9},{9,8},{10,11... | collective-permute-start | bytes 589832 | tf_op jit(solution)/shard_map/ppermute | solution.py:290
  16.9 7.0 %collective-permute-start.4 = (f32[2,96,256]{2,1,0:T(8,128)S(1)}, f32[2,96,256]{2,1,0:T(8,128)S(1)}, u32[]{:S(2)}, u32[]{:S(2)}) collective-permute-start(f32[2,96,256]{2,1,0:T(8,128)S(1)} %add.8), channel_id=1, source_target_pairs={{0,2},{2,0},{1,3},{3,1},{4,6},{6,4},{5,7},{7,5},{8,10},{10,8},{9,1... | collective-permute-start | bytes 589832 | tf_op jit(solution)/shard_map/ppermute | solution.py:293
  23.9 6.8 %collective-permute-start.6 = (f32[2,96,256]{2,1,0:T(8,128)S(1)}, f32[2,96,256]{2,1,0:T(8,128)S(1)}, u32[]{:S(2)}, u32[]{:S(2)}) collective-permute-start(f32[2,96,256]{2,1,0:T(8,128)S(1)} %add.9.own_image), channel_id=1, source_target_pairs={{0,1},{1,0},{2,3},{3,2},{4,5},{5,4},{6,7},{7,6},{8,9},{9,8},{10,11... | collective-permute-start | bytes 589832 | tf_op jit(solution)/shard_map/ppermute | solution.py:300
  24.0 11.5 %collective-permute-start.5 = (f32[2,96,256]{2,1,0:T(8,128)S(1)}, f32[2,96,256]{2,1,0:T(8,128)S(1)}, u32[]{:S(2)}, u32[]{:S(2)}) collective-permute-start(f32[2,96,256]{2,1,0:T(8,128)S(1)} %constant_dynamic-update-slice_fusion.samples.refs_0_), channel_id=1, source_target_pairs={{0,2},{2,0},{1,3},{3,1},{4,6},{6,4},{5,7},{7,5},{8,10},{10,8},{9,1... | collective-permute-start | bytes 589832 | tf_op jit(solution)/shard_map/ppermute | solution.py:296
  24.3 11.5 %collective-permute-start.7 = (f32[2,96,256]{2,1,0:T(8,128)S(1)}, f32[2,96,256]{2,1,0:T(8,128)S(1)}, u32[]{:S(2)}, u32[]{:S(2)}) collective-permute-start(f32[2,96,256]{2,1,0:T(8,128)S(1)} %add.9.own_image), channel_id=1, source_target_pairs={{3,0},{0,4},{2,8},{1,12},{7,1},{4,5},{6,9},{5,13},{8,2},{11,6},{9,... | collective-permute-start | bytes 589832 | tf_op jit(solution)/shard_map/ppermute | solution.py:298
  26.3 10.8 %collective-permute-start.8 = (f32[2,96,256]{2,1,0:T(8,128)S(1)}, f32[2,96,256]{2,1,0:T(8,128)S(1)}, u32[]{:S(2)}, u32[]{:S(2)}) collective-permute-start(f32[2,96,256]{2,1,0:T(8,128)S(1)} %add.9.own_image), channel_id=1, source_target_pairs={{0,0},{3,4},{1,8},{2,12},{4,1},{7,5},{5,9},{6,13},{11,2},{8,6},{10... | collective-permute-start | bytes 589832 | tf_op jit(solution)/shard_map/ppermute | solution.py:298

commit v11 on v9

--- a/solution.py
+++ b/solution.py
@@ -192,34 +192,35 @@
     )(guide, own_image, other_image, samples, panel, diag, tiles)
 
 
-def row_panel_kernel(*refs):
-    samples, (wide, low) = refs[:-2], refs[-2:]
+def row_panel_kernel(pair, *refs):
+    pieces, (wide, low) = refs[:-2], refs[-2:]
     rep = lax.axis_index("rep")
     col = lax.axis_index("col")
-    rows = samples[0].shape[1]
-    pairs = len(samples)
-    for turn, piece in enumerate(samples):
+    pairs, rows = len(pieces) // 2 + 1, pair.shape[1]
+    lines = [(pair[0], pair[1])]
+    lines += [(pieces[k][...], pieces[k + pairs - 1][...]) for k in range(pairs - 1)]
+    for turn, (same, other) in enumerate(lines):
         line = 2 * lax.rem(col + pairs - turn, pairs)
-        for block, place in ((line + rep, 0), (line + 1 - rep, 1)):
-            high, low[block] = halves(piece[place].T)
+        for block, values in ((line + rep, same), (line + 1 - rep, other)):
+            high, low[block] = halves(values.T)
             wide[block, :, :rows] = high
             wide[block, :, rows:] = high
 
 
-def row_panel(samples):
-    _, rows, side = samples[0].shape
-    groups = 2 * len(samples)
+def row_panel(pair, pieces):
+    _, rows, side = pair.shape
+    groups = len(pieces) + 2
     return pl.pallas_call(
         row_panel_kernel,
         out_shape=(
             jax.ShapeDtypeStruct((groups, side, 2 * rows), bf16),
             jax.ShapeDtypeStruct((groups, side, rows), bf16),
         ),
-        in_specs=[vmem] * len(samples),
+        in_specs=[vmem] * (1 + len(pieces)),
         out_specs=(vmem, vmem),
         compiler_params=room,
         name="row_panel",
-    )(*samples)
+    )(pair, *pieces)
 
 
 def slots_kernel(guide, wide, low, first, second, moved, out, panel, ready, sems):
@@ -292,14 +293,16 @@
     for turn in range(1, cols):
         image = image + lax.ppermute(chip, "col", around(cols, turn))
 
-    late, image = lax.optimization_barrier((pair, image))
-    beside = [lax.ppermute(late, "col", around(cols, turn)) for turn in range(1, cols)]
+    samples_late, image = lax.optimization_barrier((samples, image))
+    beside = [lax.ppermute(samples_late, "col", around(cols, turn)) for turn in range(1, cols)]
+    across = [lax.ppermute(block, "rep", around(2, 1)) for block in beside]
     first, second = [
         lax.ppermute(image, grid_axes, links(image_source, turn)) for turn in range(2)
     ]
     other = lax.ppermute(image, "rep", around(2, 1))
     moved, new_diag = half_gradient(guide, image, other, pair, panel, own_diag, held)
-    wide, low = row_panel([pair, *beside])
+    beside, moved = lax.optimization_barrier((beside + across, moved))
+    wide, low = row_panel(pair, beside)
     new_slots = update_slots(guide, wide, low, first, second, moved)
     return new_slots.reshape(omega_slots.shape), new_diag
 

time: 39.1 us -> 39 us (level)
    ppermute x2, waiting for transfers between devices: 1.26 us -> 4.24 us  [on_device(): lax.ppermute(image, grid_axes, links(image_source, turn))]
    ppermute x1 -> x2, waiting for transfers between devices: 2.72 us -> 0.01 us  [the longest x1 0.01 us: on_device(): lax.ppermute(samples_late, 'col', around(cols, turn))]
  transfers between devices with their start and end apart: 9 -> 10, of which waited for: 6 -> 6; matrix products, arithmetic and copies ran while one was open for 2% -> 2% of each run, Pallas kernels for 11% -> 11%
where the time goes in v11:
time: 39 us; the launch traced here: 38.9 us
  waiting for transfers between devices  16.3 us (42%)
  starting transfers between devices  13.5 us (35%)
  Pallas kernels  6.65 us (17%)
  between operations  1.43 us (4%)
  local copies, waits for them, and re-layouts  0.92 us (2%)
    ppermute x1, waiting for transfers between devices, on_device(): image = image + lax.ppermute(chip, 'col', around(cols, turn))  6.93 us
    ppermute x2, starting transfers between devices, on_device(): lax.ppermute(pair, grid_axes, links(sample_source, turn))  6.43 us
    ppermute x2, starting transfers between devices, on_device(): lax.ppermute(image, grid_axes, links(image_source, turn))  6.38 us
    ppermute x2, waiting for transfers between devices, on_device(): lax.ppermute(image, grid_axes, links(image_source, turn))  4.24 us
    ppermute x2, waiting for transfers between devices, on_device(): lax.ppermute(pair, grid_axes, links(sample_source, turn))  3.09 us
    pallas_call x1, Pallas kernels, prepare(): pl.pallas_call(functools.partial(prepare_kernel, groups), out_shape=(pltp...  2.28 us
    pallas_call x1, Pallas kernels, update_slots(): pl.pallas_call(slots_kernel, out_shape=jax.ShapeDtypeStruct(moved.shape,...  1.73 us
    pallas_call x1, Pallas kernels, half_gradient(): pl.pallas_call(half_gradient_kernel, out_shape=(jax.ShapeDtypeStruct(tile...  1.67 us
  transfers between devices with their start and end apart: 10, of which 6 were waited for; matrix products, arithmetic and copies ran while one was open for 2% of the time, Pallas kernels for 11%

profile of v11, /device:TPU:6, one launch (start us, length us, event | category | flops | bytes accessed | tf_op | source)
XLA Modules:
  0.0 38.9 jit_solution(6237369713341317857)
XLA Ops:
  0.6 0.1 collective-permute-start
  0.7 0.9 %dynamic_update_slice.6 = f32[2,96,256]{2,1,0:T(8,128)S(1)} pad(f32[1,96,256]{2,1,0:T(8,128)} %bitcast.9, f32[]{:T(128)} %constant.0.clone.1), padding=0_1x0_0x0_0 | pad | bytes 294916 | tf_op jit(solution)/shard_map/dynamic_update_slice | solution.py:281
  1.6 0.6 %collective-permute-done = f32[1,96,256]{2,1,0:T(8,128)S(1)} collective-permute-done((f32[1,96,256]{2,1,0:T(8,128)}, f32[1,96,256]{2,1,0:T(8,128)S(1)}, u32[]{:S(2)}, u32[]{:S(2)}) %collective-permute-start) | collective-permute-done | bytes 98336 | tf_op jit(solution)/shard_map/ppermute | solution.py:284
  2.2 2.6 %collective-permute-start.1 = (f32[2,96,256]{2,1,0:T(8,128)S(1)}, f32[2,96,256]{2,1,0:T(8,128)S(1)}, u32[]{:S(2)}, u32[]{:S(2)}) collective-permute-start(f32[2,96,256]{2,1,0:T(8,128)S(1)} %constant_dynamic-update-slice_fusion.samples.pair), channel_id=1, source_target_pairs={{3,0},{0,4},{2,8},{1,12},{7,1},{4,5},{6,9},{5,13},{8,2},{11,6},{9,... | collective-permute-start | bytes 589832 | tf_op jit(solution)/shard_map/ppermute | solution.py:287
  4.8 3.8 %collective-permute-start.2 = (f32[2,96,256]{2,1,0:T(8,128)S(1)}, f32[2,96,256]{2,1,0:T(8,128)S(1)}, u32[]{:S(2)}, u32[]{:S(2)}) collective-permute-start(f32[2,96,256]{2,1,0:T(8,128)S(1)} %constant_dynamic-update-slice_fusion.samples.pair), channel_id=1, source_target_pairs={{0,0},{3,4},{1,8},{2,12},{4,1},{7,5},{5,9},{6,13},{11,2},{8,6},{10... | collective-permute-start | bytes 589832 | tf_op jit(solution)/shard_map/ppermute | solution.py:287
  9.3 2.3 %prepare.1 = (s32[5,8]{1,0:T(8,128)S(4)}, f32[1,256,256]{2,1,0:T(8,128)S(1)}, f32[8,256,256]{2,1,0:T(8,128)S(1)}, bf16[8,256,256]{2,1,0:T(8,128)(2,1)S(1)}, bf16[8,256,256]{2,1,0:T(8,128)(2,1)S(1)}) custom-call(s32[2,8]{1,0:T(2,128)} %bitcast.10, s32[1,1]{1,0:T(1,128)S(6)} %copy.8.refs_1_, f32[1,256,256]{2,1,0:T(8,128)} %refs_2_.1, f32[8,256,256]{2,1,0:T(8,128)} %bitcast.6), custom_call_target="tpu_custom_call" | custom-call | tf_op jit(solution)/shard_map/prepare/pallas_call | solution.py:82
  11.6 0.0 copy-start
  11.6 0.0 collective-permute-done.1.refs_0_
  11.6 3.1 %collective-permute-done.2.refs_1_ = f32[2,96,256]{2,1,0:T(8,128)S(1)} collective-permute-done((f32[2,96,256]{2,1,0:T(8,128)S(1)}, f32[2,96,256]{2,1,0:T(8,128)S(1)}, u32[]{:S(2)}, u32[]{:S(2)}) %collective-permute-start.2) | collective-permute-done | bytes 196640 | tf_op jit(solution)/shard_map/ppermute | solution.py:287
  14.7 0.6 %partial_image.1 = (f32[2,96,256]{2,1,0:T(8,128)S(1)}, f32[2,96,256]{2,1,0:T(8,128)S(1)}, bf16[4,192,256]{2,1,0:T(8,128)(2,1)S(1)}) custom-call(s32[5,8]{1,0:T(8,128)S(4)} %get-tuple-element.19.guide, f32[2,96,256]{2,1,0:T(8,128)S(1)} %constant_dynamic-update-slice_fusion.samples.pair, f32[1,256,256]{2,1,0:T(8,128)S(1)} %get-tuple-element.20.diag, ...), custom_call_target="tpu_custom_call" | custom-call | tf_op jit(solution)/shard_map/partial_image/pallas_call | solution.py:132
  15.3 0.1 collective-permute-start.3
  15.4 1.4 %collective-permute-done.3 = f32[2,96,256]{2,1,0:T(8,128)S(1)} collective-permute-done((f32[2,96,256]{2,1,0:T(8,128)S(1)}, f32[2,96,256]{2,1,0:T(8,128)S(1)}, u32[]{:S(2)}, u32[]{:S(2)}) %collective-permute-start.3) | collective-permute-done | bytes 196640 | tf_op jit(solution)/shard_map/ppermute | solution.py:291
  16.9 0.1 collective-permute-start.4
  16.9 6.9 %collective-permute-done.4 = f32[2,96,256]{2,1,0:T(8,128)S(1)} collective-permute-done((f32[2,96,256]{2,1,0:T(8,128)S(1)}, f32[2,96,256]{2,1,0:T(8,128)S(1)}, u32[]{:S(2)}, u32[]{:S(2)}) %collective-permute-start.4) | collective-permute-done | bytes 196640 | tf_op jit(solution)/shard_map/ppermute | solution.py:294
  23.9 0.1 collective-permute-start.7
  24.0 0.0 copy-done
  24.0 0.4 collective-permute-start.5
  24.3 2.0 %collective-permute-start.8 = (f32[2,96,256]{2,1,0:T(8,128)S(1)}, f32[2,96,256]{2,1,0:T(8,128)S(1)}, u32[]{:S(2)}, u32[]{:S(2)}) collective-permute-start(f32[2,96,256]{2,1,0:T(8,128)S(1)} %add.9.own_image), channel_id=1, source_target_pairs={{3,0},{0,4},{2,8},{1,12},{7,1},{4,5},{6,9},{5,13},{8,2},{11,6},{9,... | collective-permute-start | bytes 589832 | tf_op jit(solution)/shard_map/ppermute | solution.py:300
  26.4 4.4 %collective-permute-start.9 = (f32[2,96,256]{2,1,0:T(8,128)S(1)}, f32[2,96,256]{2,1,0:T(8,128)S(1)}, u32[]{:S(2)}, u32[]{:S(2)}) collective-permute-start(f32[2,96,256]{2,1,0:T(8,128)S(1)} %add.9.own_image), channel_id=1, source_target_pairs={{0,0},{3,4},{1,8},{2,12},{4,1},{7,5},{5,9},{6,13},{11,2},{8,6},{10... | collective-permute-start | bytes 589832 | tf_op jit(solution)/shard_map/ppermute | solution.py:300
  30.7 0.0 collective-permute-done.5.refs_0_
  30.7 0.1 collective-permute-start.6
  30.8 0.0 collective-permute-done.7.other_image
  30.8 1.7 %half_gradient.1 = (f32[8,256,256]{2,1,0:T(8,128)S(1)}, f32[1,256,256]{2,1,0:T(8,128)}) custom-call(s32[5,8]{1,0:T(8,128)S(4)} %get-tuple-element.19.guide, f32[2,96,256]{2,1,0:T(8,128)S(1)} %add.9.own_image, f32[2,96,256]{2,1,0:T(8,128)S(1)} %collective-permute-done.7.other_image, f32[2,96,256]{2,1,0:T(8,128)S(1)} %constant_dynamic-update-slice_fusion.samples.pair, ...), custom_call_target="tpu_custom_call" | custom-call | tf_op jit(solution)/shard_map/half_gradient/pallas_call | solution.py:176
  32.5 0.0 collective-permute-done.6.refs_1_
  32.5 0.4 row_panel.1
  32.9 0.4 %collective-permute-done.8.first = f32[2,96,256]{2,1,0:T(8,128)S(1)} collective-permute-done((f32[2,96,256]{2,1,0:T(8,128)S(1)}, f32[2,96,256]{2,1,0:T(8,128)S(1)}, u32[]{:S(2)}, u32[]{:S(2)}) %collective-permute-start.8) | collective-permute-done | bytes 196640 | tf_op jit(solution)/shard_map/ppermute | solution.py:300
  33.3 3.8 %collective-permute-done.9.second = f32[2,96,256]{2,1,0:T(8,128)S(1)} collective-permute-done((f32[2,96,256]{2,1,0:T(8,128)S(1)}, f32[2,96,256]{2,1,0:T(8,128)S(1)}, u32[]{:S(2)}, u32[]{:S(2)}) %collective-permute-start.9) | collective-permute-done | bytes 196640 | tf_op jit(solution)/shard_map/ppermute | solution.py:300
  37.1 1.7 %update_slots.1 = f32[8,256,256]{2,1,0:T(8,128)} custom-call(s32[5,8]{1,0:T(8,128)S(4)} %get-tuple-element.19.guide, bf16[4,256,192]{2,1,0:T(8,128)(2,1)S(1)} %get-tuple-element.32.wide, bf16[4,256,96]{2,1,0:T(8,128)(2,1)S(1)} %get-tuple-element.33.low, f32[2,96,256]{2,1,0:T(8,128)S(1)} %collective-permute-done.8.first, ...), custom_call_target="tpu_custom_call" | custom-call | tf_op jit(solution)/shard_map/update_slots/pallas_call | solution.py:247
  (3 shorter events, 0.1 us)
Async XLA Ops:
  0.6 1.6 %collective-permute-start = (f32[1,96,256]{2,1,0:T(8,128)}, f32[1,96,256]{2,1,0:T(8,128)S(1)}, u32[]{:S(2)}, u32[]{:S(2)}) collective-permute-start(f32[1,96,256]{2,1,0:T(8,128)} %bitcast.8), channel_id=1, source_target_pairs={{0,1},{1,0},{2,3},{3,2},{4,5},{5,4},{6,7},{7,6},{8,9},{9,8},{10,11... | collective-permute-start | bytes 294920 | tf_op jit(solution)/shard_map/ppermute | solution.py:284
  2.2 9.4 %collective-permute-start.1 = (f32[2,96,256]{2,1,0:T(8,128)S(1)}, f32[2,96,256]{2,1,0:T(8,128)S(1)}, u32[]{:S(2)}, u32[]{:S(2)}) collective-permute-start(f32[2,96,256]{2,1,0:T(8,128)S(1)} %constant_dynamic-update-slice_fusion.samples.pair), channel_id=1, source_target_pairs={{3,0},{0,4},{2,8},{1,12},{7,1},{4,5},{6,9},{5,13},{8,2},{11,6},{9,... | collective-permute-start | bytes 589832 | tf_op jit(solution)/shard_map/ppermute | solution.py:287
  4.8 9.9 %collective-permute-start.2 = (f32[2,96,256]{2,1,0:T(8,128)S(1)}, f32[2,96,256]{2,1,0:T(8,128)S(1)}, u32[]{:S(2)}, u32[]{:S(2)}) collective-permute-start(f32[2,96,256]{2,1,0:T(8,128)S(1)} %constant_dynamic-update-slice_fusion.samples.pair), channel_id=1, source_target_pairs={{0,0},{3,4},{1,8},{2,12},{4,1},{7,5},{5,9},{6,13},{11,2},{8,6},{10... | collective-permute-start | bytes 589832 | tf_op jit(solution)/shard_map/ppermute | solution.py:287
  11.6 12.4 %copy-start = (f32[96,256]{1,0:T(8,128)S(1)}, f32[96,256]{1,0:T(8,128)}, u32[]{:S(2)}) copy-start(f32[96,256]{1,0:T(8,128)} %param.5) | copy-start | bytes 294916
  15.3 1.5 %collective-permute-start.3 = (f32[2,96,256]{2,1,0:T(8,128)S(1)}, f32[2,96,256]{2,1,0:T(8,128)S(1)}, u32[]{:S(2)}, u32[]{:S(2)}) collective-permute-start(f32[2,96,256]{2,1,0:T(8,128)S(1)} %get-tuple-element.24), channel_id=1, source_target_pairs={{0,1},{1,0},{2,3},{3,2},{4,5},{5,4},{6,7},{7,6},{8,9},{9,8},{10,11... | collective-permute-start | bytes 589832 | tf_op jit(solution)/shard_map/ppermute | solution.py:291
  16.9 7.0 %collective-permute-start.4 = (f32[2,96,256]{2,1,0:T(8,128)S(1)}, f32[2,96,256]{2,1,0:T(8,128)S(1)}, u32[]{:S(2)}, u32[]{:S(2)}) collective-permute-start(f32[2,96,256]{2,1,0:T(8,128)S(1)} %add.8), channel_id=1, source_target_pairs={{0,2},{2,0},{1,3},{3,1},{4,6},{6,4},{5,7},{7,5},{8,10},{10,8},{9,1... | collective-permute-start | bytes 589832 | tf_op jit(solution)/shard_map/ppermute | solution.py:294
  23.9 6.9 %collective-permute-start.7 = (f32[2,96,256]{2,1,0:T(8,128)S(1)}, f32[2,96,256]{2,1,0:T(8,128)S(1)}, u32[]{:S(2)}, u32[]{:S(2)}) collective-permute-start(f32[2,96,256]{2,1,0:T(8,128)S(1)} %add.9.own_image), channel_id=1, source_target_pairs={{0,1},{1,0},{2,3},{3,2},{4,5},{5,4},{6,7},{7,6},{8,9},{9,8},{10,11... | collective-permute-start | bytes 589832 | tf_op jit(solution)/shard_map/ppermute | solution.py:302
  24.0 6.7 %collective-permute-start.5 = (f32[96,256]{1,0:T(8,128)S(1)}, f32[96,256]{1,0:T(8,128)S(1)}, u32[]{:S(2)}, u32[]{:S(2)}) collective-permute-start(f32[96,256]{1,0:T(8,128)S(1)} %copy-done), channel_id=1, source_target_pairs={{0,2},{2,0},{1,3},{3,1},{4,6},{6,4},{5,7},{7,5},{8,10},{10,8},{9,1... | collective-permute-start | bytes 294920 | tf_op jit(solution)/shard_map/ppermute | solution.py:297
  24.3 9.0 %collective-permute-start.8 = (f32[2,96,256]{2,1,0:T(8,128)S(1)}, f32[2,96,256]{2,1,0:T(8,128)S(1)}, u32[]{:S(2)}, u32[]{:S(2)}) collective-permute-start(f32[2,96,256]{2,1,0:T(8,128)S(1)} %add.9.own_image), channel_id=1, source_target_pairs={{3,0},{0,4},{2,8},{1,12},{7,1},{4,5},{6,9},{5,13},{8,2},{11,6},{9,... | collective-permute-start | bytes 589832 | tf_op jit(solution)/shard_map/ppermute | solution.py:300
  26.4 10.8 %collective-permute-start.9 = (f32[2,96,256]{2,1,0:T(8,128)S(1)}, f32[2,96,256]{2,1,0:T(8,128)S(1)}, u32[]{:S(2)}, u32[]{:S(2)}) collective-permute-start(f32[2,96,256]{2,1,0:T(8,128)S(1)} %add.9.own_image), channel_id=1, source_target_pairs={{0,0},{3,4},{1,8},{2,12},{4,1},{7,5},{5,9},{6,13},{11,2},{8,6},{10... | collective-permute-start | bytes 589832 | tf_op jit(solution)/shard_map/ppermute | solution.py:300
  30.7 1.8 %collective-permute-start.6 = (f32[96,256]{1,0:T(8,128)S(1)}, f32[96,256]{1,0:T(8,128)S(1)}, u32[]{:S(2)}, u32[]{:S(2)}) collective-permute-start(f32[96,256]{1,0:T(8,128)S(1)} %collective-permute-done.5.refs_0_), channel_id=1, source_target_pairs={{0,1},{1,0},{2,3},{3,2},{4,5},{5,4},{6,7},{7,6},{8,9},{9,8},{10,11... | collective-permute-start | bytes 294920 | tf_op jit(solution)/shard_map/ppermute | solution.py:298

commit v12 on v11

--- a/solution.py
+++ b/solution.py
@@ -39,8 +39,7 @@
 
 
 def sample_source(turn, row, own, groups):
-    spot = groups // 2 - 1 - turn
-    return first_source(row, own, groups) ^ (2 * spot + spot % 2)
+    return first_source(row, own, groups) ^ (2 * turn + turn % 2)
 
 
 def image_source(turn, row, own, groups):
@@ -223,40 +222,43 @@
     )(pair, *pieces)
 
 
-def slots_kernel(guide, wide, low, first, second, moved, out, panel, ready, sems):
-    pairs, rows, _ = first.shape
+def slots_kernel(turn, guide, wide, low, piece, moved, *refs):
+    out, panel, ready, sems = refs[-4:]
+    pairs, rows, _ = piece.shape
     for pair in range(pairs):
-        for turn, piece in enumerate((first, second)):
-            block = 2 * pair + guide[3, turn]
-            panel[block, :rows], panel[block, rows:] = halves(piece[pair])
-    copies = []
-    for slot in range(moved.shape[0]):
-        left, right = guide[0, slot], guide[1, slot]
+        panel[pair, :rows], panel[pair, rows:] = halves(piece[pair])
+    parity = guide[3, turn]
+    copies = [
+        pltpu.make_async_copy(ready.at[slot], out.at[slot], sems.at[slot])
+        for slot in range(moved.shape[0])
+    ]
+    for slot, copy in enumerate(copies):
+        left, right = guide[0, slot], lax.div(guide[1, slot], 2)
         gradient = dot(wide[left], panel[right]) + dot(low[left], panel[right, :rows])
         value = soft_limit(moved[slot] - gradient * (step_size / (2.0 * rows)))
         ready[slot] = jnp.where(slot < guide[4, 0], value, 0.0)
-        copies.append(pltpu.make_async_copy(ready.at[slot], out.at[slot], sems.at[slot]))
-        copies[-1].start()
-    for copy in copies:
-        copy.wait()
-
-
-def update_slots(guide, wide, low, first, second, moved):
+        pl.when(guide[1, slot] & 1 == parity)(copy.start)
+    for slot, copy in enumerate(copies):
+        pl.when(guide[1, slot] & 1 == parity)(copy.wait)
+
+
+def update_slots(turn, guide, wide, low, piece, moved, *begun):
     slots, side, _ = moved.shape
     groups, _, depth = wide.shape
     return pl.pallas_call(
-        slots_kernel,
+        functools.partial(slots_kernel, turn),
         out_shape=jax.ShapeDtypeStruct(moved.shape, f32),
-        in_specs=[smem] + [vmem] * 5,
+        in_specs=[smem] + [vmem] * 4 + [hbm] * len(begun),
         out_specs=hbm,
+        input_output_aliases={5: 0} if begun else {},
         scratch_shapes=[
-            pltpu.VMEM((groups, depth, side), bf16),
+            pltpu.VMEM((groups // 2, depth, side), bf16),
             pltpu.VMEM(moved.shape, f32),
             pltpu.SemaphoreType.DMA((slots,)),
         ],
         compiler_params=room,
         name="update_slots",
-    )(guide, wide, low, first, second, moved)
+    )(guide, wide, low, piece, moved, *begun)
 
 
 def on_device(samples, diag_tiles, omega_slots, tile_pos, tile_count):
@@ -303,7 +305,8 @@
     moved, new_diag = half_gradient(guide, image, other, pair, panel, own_diag, held)
     beside, moved = lax.optimization_barrier((beside + across, moved))
     wide, low = row_panel(pair, beside)
-    new_slots = update_slots(guide, wide, low, first, second, moved)
+    begun = update_slots(0, guide, wide, low, first, moved)
+    new_slots = update_slots(1, guide, wide, low, second, moved, begun)
     return new_slots.reshape(omega_slots.shape), new_diag
 
 

time: 39 us -> 39 us (level)
  waiting for transfers between devices: 16.3 us -> 14.6 us
  Pallas kernels: 6.65 us -> 8.09 us
    ppermute x2, waiting for transfers between devices: 4.24 us -> 2.58 us  [on_device(): lax.ppermute(image, grid_axes, links(image_source, turn))]
    pallas_call x1 -> x2, Pallas kernels: 1.73 us -> 3.18 us  [update_slots(): pl.pallas_call(functools.partial(slots_kernel, turn), out_shape=jax.Shape...]
  transfers between devices with their start and end apart: 10 -> 10, of which waited for: 6 -> 6; matrix products, arithmetic and copies ran while one was open for 2% -> 2% of each run, Pallas kernels for 11% -> 15%
where the time goes in v12:
time: 39 us; the launch traced here: 38.6 us
  waiting for transfers between devices  14.6 us (37%)
  starting transfers between devices  13.5 us (35%)
  Pallas kernels  8.09 us (21%)
  between operations  1.43 us (4%)
  local copies, waits for them, and re-layouts  0.92 us (2%)
    ppermute x1, waiting for transfers between devices, on_device(): image = image + lax.ppermute(chip, 'col', around(cols, turn))  6.93 us
    ppermute x2, starting transfers between devices, on_device(): lax.ppermute(pair, grid_axes, links(sample_source, turn))  6.43 us
    ppermute x2, starting transfers between devices, on_device(): lax.ppermute(image, grid_axes, links(image_source, turn))  6.38 us
    pallas_call x2, Pallas kernels, update_slots(): pl.pallas_call(functools.partial(slots_kernel, turn), out_shape=jax.Shape...  3.18 us
    ppermute x2, waiting for transfers between devices, on_device(): lax.ppermute(pair, grid_axes, links(sample_source, turn))  3.09 us
    ppermute x2, waiting for transfers between devices, on_device(): lax.ppermute(image, grid_axes, links(image_source, turn))  2.58 us
    pallas_call x1, Pallas kernels, prepare(): pl.pallas_call(functools.partial(prepare_kernel, groups), out_shape=(pltp...  2.28 us
    pallas_call x1, Pallas kernels, half_gradient(): pl.pallas_call(half_gradient_kernel, out_shape=(jax.ShapeDtypeStruct(tile...  1.67 us
  transfers between devices with their start and end apart: 10, of which 6 were waited for; matrix products, arithmetic and copies ran while one was open for 2% of the time, Pallas kernels for 15%

profile of v12, /device:TPU:6, one launch (start us, length us, event | category | flops | bytes accessed | tf_op | source)
XLA Modules:
  0.0 38.6 jit_solution(17389096275313882046)
XLA Ops:
  0.6 0.1 collective-permute-start
  0.7 0.9 %dynamic_update_slice.6 = f32[2,96,256]{2,1,0:T(8,128)S(1)} pad(f32[1,96,256]{2,1,0:T(8,128)} %bitcast.9, f32[]{:T(128)} %constant.0.clone.1), padding=0_1x0_0x0_0 | pad | bytes 294916 | tf_op jit(solution)/shard_map/dynamic_update_slice | solution.py:283
  1.6 0.6 %collective-permute-done = f32[1,96,256]{2,1,0:T(8,128)S(1)} collective-permute-done((f32[1,96,256]{2,1,0:T(8,128)}, f32[1,96,256]{2,1,0:T(8,128)S(1)}, u32[]{:S(2)}, u32[]{:S(2)}) %collective-permute-start) | collective-permute-done | bytes 98336 | tf_op jit(solution)/shard_map/ppermute | solution.py:286
  2.2 2.6 %collective-permute-start.2 = (f32[2,96,256]{2,1,0:T(8,128)S(1)}, f32[2,96,256]{2,1,0:T(8,128)S(1)}, u32[]{:S(2)}, u32[]{:S(2)}) collective-permute-start(f32[2,96,256]{2,1,0:T(8,128)S(1)} %constant_dynamic-update-slice_fusion.samples.pair), channel_id=1, source_target_pairs={{3,0},{0,4},{2,8},{1,12},{7,1},{4,5},{6,9},{5,13},{8,2},{11,6},{9,... | collective-permute-start | bytes 589832 | tf_op jit(solution)/shard_map/ppermute | solution.py:289
  4.8 3.8 %collective-permute-start.1 = (f32[2,96,256]{2,1,0:T(8,128)S(1)}, f32[2,96,256]{2,1,0:T(8,128)S(1)}, u32[]{:S(2)}, u32[]{:S(2)}) collective-permute-start(f32[2,96,256]{2,1,0:T(8,128)S(1)} %constant_dynamic-update-slice_fusion.samples.pair), channel_id=1, source_target_pairs={{0,0},{3,4},{1,8},{2,12},{4,1},{7,5},{5,9},{6,13},{11,2},{8,6},{10... | collective-permute-start | bytes 589832 | tf_op jit(solution)/shard_map/ppermute | solution.py:289
  9.3 2.3 %prepare.1 = (s32[5,8]{1,0:T(8,128)S(4)}, f32[1,256,256]{2,1,0:T(8,128)S(1)}, f32[8,256,256]{2,1,0:T(8,128)S(1)}, bf16[8,256,256]{2,1,0:T(8,128)(2,1)S(1)}, bf16[8,256,256]{2,1,0:T(8,128)(2,1)S(1)}) custom-call(s32[2,8]{1,0:T(2,128)} %bitcast.10, s32[1,1]{1,0:T(1,128)S(6)} %copy.10.refs_1_, f32[1,256,256]{2,1,0:T(8,128)} %refs_2_.1, f32[8,256,256]{2,1,0:T(8,128)} %bitcast.7), custom_call_target="tpu_custom_call" | custom-call | tf_op jit(solution)/shard_map/prepare/pallas_call | solution.py:81
  11.6 0.0 copy-start
  11.6 0.0 collective-permute-done.2.refs_1_
  11.6 3.1 %collective-permute-done.1.refs_0_ = f32[2,96,256]{2,1,0:T(8,128)S(1)} collective-permute-done((f32[2,96,256]{2,1,0:T(8,128)S(1)}, f32[2,96,256]{2,1,0:T(8,128)S(1)}, u32[]{:S(2)}, u32[]{:S(2)}) %collective-permute-start.1) | collective-permute-done | bytes 196640 | tf_op jit(solution)/shard_map/ppermute | solution.py:289
  14.7 0.6 %partial_image.1 = (f32[2,96,256]{2,1,0:T(8,128)S(1)}, f32[2,96,256]{2,1,0:T(8,128)S(1)}, bf16[4,192,256]{2,1,0:T(8,128)(2,1)S(1)}) custom-call(s32[5,8]{1,0:T(8,128)S(4)} %get-tuple-element.19.guide, f32[2,96,256]{2,1,0:T(8,128)S(1)} %constant_dynamic-update-slice_fusion.samples.pair, f32[1,256,256]{2,1,0:T(8,128)S(1)} %get-tuple-element.20.diag, ...), custom_call_target="tpu_custom_call" | custom-call | tf_op jit(solution)/shard_map/partial_image/pallas_call | solution.py:131
  15.3 0.1 collective-permute-start.3
  15.4 1.4 %collective-permute-done.3 = f32[2,96,256]{2,1,0:T(8,128)S(1)} collective-permute-done((f32[2,96,256]{2,1,0:T(8,128)S(1)}, f32[2,96,256]{2,1,0:T(8,128)S(1)}, u32[]{:S(2)}, u32[]{:S(2)}) %collective-permute-start.3) | collective-permute-done | bytes 196640 | tf_op jit(solution)/shard_map/ppermute | solution.py:293
  16.9 0.1 collective-permute-start.4
  16.9 6.9 %collective-permute-done.4 = f32[2,96,256]{2,1,0:T(8,128)S(1)} collective-permute-done((f32[2,96,256]{2,1,0:T(8,128)S(1)}, f32[2,96,256]{2,1,0:T(8,128)S(1)}, u32[]{:S(2)}, u32[]{:S(2)}) %collective-permute-start.4) | collective-permute-done | bytes 196640 | tf_op jit(solution)/shard_map/ppermute | solution.py:296
  23.9 0.1 collective-permute-start.7
  24.0 0.0 copy-done
  24.0 0.4 collective-permute-start.5
  24.3 2.0 %collective-permute-start.9 = (f32[2,96,256]{2,1,0:T(8,128)S(1)}, f32[2,96,256]{2,1,0:T(8,128)S(1)}, u32[]{:S(2)}, u32[]{:S(2)}) collective-permute-start(f32[2,96,256]{2,1,0:T(8,128)S(1)} %add.9.own_image), channel_id=1, source_target_pairs={{3,0},{0,4},{2,8},{1,12},{7,1},{4,5},{6,9},{5,13},{8,2},{11,6},{9,... | collective-permute-start | bytes 589832 | tf_op jit(solution)/shard_map/ppermute | solution.py:302
  26.4 4.4 %collective-permute-start.8 = (f32[2,96,256]{2,1,0:T(8,128)S(1)}, f32[2,96,256]{2,1,0:T(8,128)S(1)}, u32[]{:S(2)}, u32[]{:S(2)}) collective-permute-start(f32[2,96,256]{2,1,0:T(8,128)S(1)} %add.9.own_image), channel_id=1, source_target_pairs={{0,0},{3,4},{1,8},{2,12},{4,1},{7,5},{5,9},{6,13},{11,2},{8,6},{10... | collective-permute-start | bytes 589832 | tf_op jit(solution)/shard_map/ppermute | solution.py:302
  30.7 0.0 collective-permute-done.5.refs_0_
  30.7 0.1 collective-permute-start.6
  30.8 0.0 collective-permute-done.7.other_image
  30.8 1.7 %half_gradient.1 = (f32[8,256,256]{2,1,0:T(8,128)S(1)}, f32[1,256,256]{2,1,0:T(8,128)}) custom-call(s32[5,8]{1,0:T(8,128)S(4)} %get-tuple-element.19.guide, f32[2,96,256]{2,1,0:T(8,128)S(1)} %add.9.own_image, f32[2,96,256]{2,1,0:T(8,128)S(1)} %collective-permute-done.7.other_image, f32[2,96,256]{2,1,0:T(8,128)S(1)} %constant_dynamic-update-slice_fusion.samples.pair, ...), custom_call_target="tpu_custom_call" | custom-call | tf_op jit(solution)/shard_map/half_gradient/pallas_call | solution.py:175
  32.5 0.0 collective-permute-done.6.refs_1_
  32.5 0.4 row_panel.1
  32.9 0.4 %collective-permute-done.9.piece = f32[2,96,256]{2,1,0:T(8,128)S(1)} collective-permute-done((f32[2,96,256]{2,1,0:T(8,128)S(1)}, f32[2,96,256]{2,1,0:T(8,128)S(1)}, u32[]{:S(2)}, u32[]{:S(2)}) %collective-permute-start.9) | collective-permute-done | bytes 196640 | tf_op jit(solution)/shard_map/ppermute | solution.py:302
  33.3 1.7 %update_slots.2.refs_0_ = f32[8,256,256]{2,1,0:T(8,128)} custom-call(s32[5,8]{1,0:T(8,128)S(4)} %get-tuple-element.19.guide, bf16[4,256,192]{2,1,0:T(8,128)(2,1)S(1)} %get-tuple-element.32.wide, bf16[4,256,96]{2,1,0:T(8,128)(2,1)S(1)} %get-tuple-element.33.low, f32[2,96,256]{2,1,0:T(8,128)S(1)} %collective-permute-done.9.piece, ...), custom_call_target="tpu_custom_call" | custom-call | tf_op jit(solution)/shard_map/update_slots/pallas_call | solution.py:248
  35.0 2.1 %collective-permute-done.8.piece = f32[2,96,256]{2,1,0:T(8,128)S(1)} collective-permute-done((f32[2,96,256]{2,1,0:T(8,128)S(1)}, f32[2,96,256]{2,1,0:T(8,128)S(1)}, u32[]{:S(2)}, u32[]{:S(2)}) %collective-permute-start.8) | collective-permute-done | bytes 196640 | tf_op jit(solution)/shard_map/ppermute | solution.py:302
  37.1 1.5 %update_slots.3 = f32[8,256,256]{2,1,0:T(8,128)} custom-call(s32[5,8]{1,0:T(8,128)S(4)} %get-tuple-element.19.guide, bf16[4,256,192]{2,1,0:T(8,128)(2,1)S(1)} %get-tuple-element.32.wide, bf16[4,256,96]{2,1,0:T(8,128)(2,1)S(1)} %get-tuple-element.33.low, f32[2,96,256]{2,1,0:T(8,128)S(1)} %collective-permute-done.8.piece, ...), custom_call_target="tpu_custom_call", output_to_operand_aliasing={{}: (5, {})} | custom-call | tf_op jit(solution)/shard_map/update_slots/pallas_call | solution.py:248
  (3 shorter events, 0.1 us)
Async XLA Ops:
  0.6 1.6 %collective-permute-start = (f32[1,96,256]{2,1,0:T(8,128)}, f32[1,96,256]{2,1,0:T(8,128)S(1)}, u32[]{:S(2)}, u32[]{:S(2)}) collective-permute-start(f32[1,96,256]{2,1,0:T(8,128)} %bitcast.8), channel_id=1, source_target_pairs={{0,1},{1,0},{2,3},{3,2},{4,5},{5,4},{6,7},{7,6},{8,9},{9,8},{10,11... | collective-permute-start | bytes 294920 | tf_op jit(solution)/shard_map/ppermute | solution.py:286
  2.2 9.4 %collective-permute-start.2 = (f32[2,96,256]{2,1,0:T(8,128)S(1)}, f32[2,96,256]{2,1,0:T(8,128)S(1)}, u32[]{:S(2)}, u32[]{:S(2)}) collective-permute-start(f32[2,96,256]{2,1,0:T(8,128)S(1)} %constant_dynamic-update-slice_fusion.samples.pair), channel_id=1, source_target_pairs={{3,0},{0,4},{2,8},{1,12},{7,1},{4,5},{6,9},{5,13},{8,2},{11,6},{9,... | collective-permute-start | bytes 589832 | tf_op jit(solution)/shard_map/ppermute | solution.py:289
  4.8 9.9 %collective-permute-start.1 = (f32[2,96,256]{2,1,0:T(8,128)S(1)}, f32[2,96,256]{2,1,0:T(8,128)S(1)}, u32[]{:S(2)}, u32[]{:S(2)}) collective-permute-start(f32[2,96,256]{2,1,0:T(8,128)S(1)} %constant_dynamic-update-slice_fusion.samples.pair), channel_id=1, source_target_pairs={{0,0},{3,4},{1,8},{2,12},{4,1},{7,5},{5,9},{6,13},{11,2},{8,6},{10... | collective-permute-start | bytes 589832 | tf_op jit(solution)/shard_map/ppermute | solution.py:289
  11.6 12.4 %copy-start = (f32[96,256]{1,0:T(8,128)S(1)}, f32[96,256]{1,0:T(8,128)}, u32[]{:S(2)}) copy-start(f32[96,256]{1,0:T(8,128)} %param.5) | copy-start | bytes 294916
  15.3 1.5 %collective-permute-start.3 = (f32[2,96,256]{2,1,0:T(8,128)S(1)}, f32[2,96,256]{2,1,0:T(8,128)S(1)}, u32[]{:S(2)}, u32[]{:S(2)}) collective-permute-start(f32[2,96,256]{2,1,0:T(8,128)S(1)} %get-tuple-element.24), channel_id=1, source_target_pairs={{0,1},{1,0},{2,3},{3,2},{4,5},{5,4},{6,7},{7,6},{8,9},{9,8},{10,11... | collective-permute-start | bytes 589832 | tf_op jit(solution)/shard_map/ppermute | solution.py:293
  16.9 7.0 %collective-permute-start.4 = (f32[2,96,256]{2,1,0:T(8,128)S(1)}, f32[2,96,256]{2,1,0:T(8,128)S(1)}, u32[]{:S(2)}, u32[]{:S(2)}) collective-permute-start(f32[2,96,256]{2,1,0:T(8,128)S(1)} %add.8), channel_id=1, source_target_pairs={{0,2},{2,0},{1,3},{3,1},{4,6},{6,4},{5,7},{7,5},{8,10},{10,8},{9,1... | collective-permute-start | bytes 589832 | tf_op jit(solution)/shard_map/ppermute | solution.py:296
  23.9 6.9 %collective-permute-start.7 = (f32[2,96,256]{2,1,0:T(8,128)S(1)}, f32[2,96,256]{2,1,0:T(8,128)S(1)}, u32[]{:S(2)}, u32[]{:S(2)}) collective-permute-start(f32[2,96,256]{2,1,0:T(8,128)S(1)} %add.9.own_image), channel_id=1, source_target_pairs={{0,1},{1,0},{2,3},{3,2},{4,5},{5,4},{6,7},{7,6},{8,9},{9,8},{10,11... | collective-permute-start | bytes 589832 | tf_op jit(solution)/shard_map/ppermute | solution.py:304
  24.0 6.7 %collective-permute-start.5 = (f32[96,256]{1,0:T(8,128)S(1)}, f32[96,256]{1,0:T(8,128)S(1)}, u32[]{:S(2)}, u32[]{:S(2)}) collective-permute-start(f32[96,256]{1,0:T(8,128)S(1)} %copy-done), channel_id=1, source_target_pairs={{0,2},{2,0},{1,3},{3,1},{4,6},{6,4},{5,7},{7,5},{8,10},{10,8},{9,1... | collective-permute-start | bytes 294920 | tf_op jit(solution)/shard_map/ppermute | solution.py:299
  24.3 9.0 %collective-permute-start.9 = (f32[2,96,256]{2,1,0:T(8,128)S(1)}, f32[2,96,256]{2,1,0:T(8,128)S(1)}, u32[]{:S(2)}, u32[]{:S(2)}) collective-permute-start(f32[2,96,256]{2,1,0:T(8,128)S(1)} %add.9.own_image), channel_id=1, source_target_pairs={{3,0},{0,4},{2,8},{1,12},{7,1},{4,5},{6,9},{5,13},{8,2},{11,6},{9,... | collective-permute-start | bytes 589832 | tf_op jit(solution)/shard_map/ppermute | solution.py:302
  26.4 10.8 %collective-permute-start.8 = (f32[2,96,256]{2,1,0:T(8,128)S(1)}, f32[2,96,256]{2,1,0:T(8,128)S(1)}, u32[]{:S(2)}, u32[]{:S(2)}) collective-permute-start(f32[2,96,256]{2,1,0:T(8,128)S(1)} %add.9.own_image), channel_id=1, source_target_pairs={{0,0},{3,4},{1,8},{2,12},{4,1},{7,5},{5,9},{6,13},{11,2},{8,6},{10... | collective-permute-start | bytes 589832 | tf_op jit(solution)/shard_map/ppermute | solution.py:302
  30.7 1.8 %collective-permute-start.6 = (f32[96,256]{1,0:T(8,128)S(1)}, f32[96,256]{1,0:T(8,128)S(1)}, u32[]{:S(2)}, u32[]{:S(2)}) collective-permute-start(f32[96,256]{1,0:T(8,128)S(1)} %collective-permute-done.5.refs_0_), channel_id=1, source_target_pairs={{0,1},{1,0},{2,3},{3,2},{4,5},{5,4},{6,7},{7,6},{8,9},{9,8},{10,11... | collective-permute-start | bytes 294920 | tf_op jit(solution)/shard_map/ppermute | solution.py:300

commit v13 on v12

--- a/solution.py
+++ b/solution.py
@@ -201,7 +201,7 @@
     for turn, (same, other) in enumerate(lines):
         line = 2 * lax.rem(col + pairs - turn, pairs)
         for block, values in ((line + rep, same), (line + 1 - rep, other)):
-            high, low[block] = halves(values.T)
+            high, low[block] = halves(values.T * (step_size / (2.0 * rows)))
             wide[block, :, :rows] = high
             wide[block, :, rows:] = high
 
@@ -235,7 +235,7 @@
     for slot, copy in enumerate(copies):
         left, right = guide[0, slot], lax.div(guide[1, slot], 2)
         gradient = dot(wide[left], panel[right]) + dot(low[left], panel[right, :rows])
-        value = soft_limit(moved[slot] - gradient * (step_size / (2.0 * rows)))
+        value = soft_limit(moved[slot] - gradient)
         ready[slot] = jnp.where(slot < guide[4, 0], value, 0.0)
         pl.when(guide[1, slot] & 1 == parity)(copy.start)
     for slot, copy in enumerate(copies):

time: 39 us -> 38.9 us (level)
  no operation moved by 1% of the time
where the time goes in v13:
time: 38.9 us; the launch traced here: 38.6 us
  waiting for transfers between devices  14.7 us (38%)
  starting transfers between devices  13.5 us (35%)
  Pallas kernels  7.97 us (20%)
  between operations  1.43 us (4%)
  local copies, waits for them, and re-layouts  0.92 us (2%)
    ppermute x1, waiting for transfers between devices, on_device(): image = image + lax.ppermute(chip, 'col', around(cols, turn))  6.93 us
    ppermute x2, starting transfers between devices, on_device(): lax.ppermute(pair, grid_axes, links(sample_source, turn))  6.43 us
    ppermute x2, starting transfers between devices, on_device(): lax.ppermute(image, grid_axes, links(image_source, turn))  6.38 us
    ppermute x2, waiting for transfers between devices, on_device(): lax.ppermute(pair, grid_axes, links(sample_source, turn))  3.09 us
    pallas_call x2, Pallas kernels, update_slots(): pl.pallas_call(functools.partial(slots_kernel, turn), out_shape=jax.Shape...  3.05 us
    ppermute x2, waiting for transfers between devices, on_device(): lax.ppermute(image, grid_axes, links(image_source, turn))  2.63 us
    pallas_call x1, Pallas kernels, prepare(): pl.pallas_call(functools.partial(prepare_kernel, groups), out_shape=(pltp...  2.28 us
    pallas_call x1, Pallas kernels, half_gradient(): pl.pallas_call(half_gradient_kernel, out_shape=(jax.ShapeDtypeStruct(tile...  1.67 us
  transfers between devices with their start and end apart: 10, of which 6 were waited for; matrix products, arithmetic and copies ran while one was open for 2% of the time, Pallas kernels for 15%

profile of v13, /device:TPU:6, one launch (start us, length us, event | category | flops | bytes accessed | tf_op | source)
XLA Modules:
  0.0 38.6 jit_solution(7947480435921087107)
XLA Ops:
  0.6 0.1 collective-permute-start
  0.7 0.9 %dynamic_update_slice.6 = f32[2,96,256]{2,1,0:T(8,128)S(1)} pad(f32[1,96,256]{2,1,0:T(8,128)} %bitcast.9, f32[]{:T(128)} %constant.0.clone.1), padding=0_1x0_0x0_0 | pad | bytes 294916 | tf_op jit(solution)/shard_map/dynamic_update_slice | solution.py:283
  1.6 0.6 %collective-permute-done = f32[1,96,256]{2,1,0:T(8,128)S(1)} collective-permute-done((f32[1,96,256]{2,1,0:T(8,128)}, f32[1,96,256]{2,1,0:T(8,128)S(1)}, u32[]{:S(2)}, u32[]{:S(2)}) %collective-permute-start) | collective-permute-done | bytes 98336 | tf_op jit(solution)/shard_map/ppermute | solution.py:286
  2.2 2.6 %collective-permute-start.2 = (f32[2,96,256]{2,1,0:T(8,128)S(1)}, f32[2,96,256]{2,1,0:T(8,128)S(1)}, u32[]{:S(2)}, u32[]{:S(2)}) collective-permute-start(f32[2,96,256]{2,1,0:T(8,128)S(1)} %constant_dynamic-update-slice_fusion.samples.pair), channel_id=1, source_target_pairs={{3,0},{0,4},{2,8},{1,12},{7,1},{4,5},{6,9},{5,13},{8,2},{11,6},{9,... | collective-permute-start | bytes 589832 | tf_op jit(solution)/shard_map/ppermute | solution.py:289
  4.8 3.8 %collective-permute-start.1 = (f32[2,96,256]{2,1,0:T(8,128)S(1)}, f32[2,96,256]{2,1,0:T(8,128)S(1)}, u32[]{:S(2)}, u32[]{:S(2)}) collective-permute-start(f32[2,96,256]{2,1,0:T(8,128)S(1)} %constant_dynamic-update-slice_fusion.samples.pair), channel_id=1, source_target_pairs={{0,0},{3,4},{1,8},{2,12},{4,1},{7,5},{5,9},{6,13},{11,2},{8,6},{10... | collective-permute-start | bytes 589832 | tf_op jit(solution)/shard_map/ppermute | solution.py:289
  9.3 2.3 %prepare.1 = (s32[5,8]{1,0:T(8,128)S(4)}, f32[1,256,256]{2,1,0:T(8,128)S(1)}, f32[8,256,256]{2,1,0:T(8,128)S(1)}, bf16[8,256,256]{2,1,0:T(8,128)(2,1)S(1)}, bf16[8,256,256]{2,1,0:T(8,128)(2,1)S(1)}) custom-call(s32[2,8]{1,0:T(2,128)} %bitcast.10, s32[1,1]{1,0:T(1,128)S(6)} %copy.10.refs_1_, f32[1,256,256]{2,1,0:T(8,128)} %refs_2_.1, f32[8,256,256]{2,1,0:T(8,128)} %bitcast.7), custom_call_target="tpu_custom_call" | custom-call | tf_op jit(solution)/shard_map/prepare/pallas_call | solution.py:81
  11.6 0.0 copy-start
  11.6 0.0 collective-permute-done.2.refs_1_
  11.6 3.1 %collective-permute-done.1.refs_0_ = f32[2,96,256]{2,1,0:T(8,128)S(1)} collective-permute-done((f32[2,96,256]{2,1,0:T(8,128)S(1)}, f32[2,96,256]{2,1,0:T(8,128)S(1)}, u32[]{:S(2)}, u32[]{:S(2)}) %collective-permute-start.1) | collective-permute-done | bytes 196640 | tf_op jit(solution)/shard_map/ppermute | solution.py:289
  14.7 0.6 %partial_image.1 = (f32[2,96,256]{2,1,0:T(8,128)S(1)}, f32[2,96,256]{2,1,0:T(8,128)S(1)}, bf16[4,192,256]{2,1,0:T(8,128)(2,1)S(1)}) custom-call(s32[5,8]{1,0:T(8,128)S(4)} %get-tuple-element.19.guide, f32[2,96,256]{2,1,0:T(8,128)S(1)} %constant_dynamic-update-slice_fusion.samples.pair, f32[1,256,256]{2,1,0:T(8,128)S(1)} %get-tuple-element.20.diag, ...), custom_call_target="tpu_custom_call" | custom-call | tf_op jit(solution)/shard_map/partial_image/pallas_call | solution.py:131
  15.3 0.1 collective-permute-start.3
  15.4 1.4 %collective-permute-done.3 = f32[2,96,256]{2,1,0:T(8,128)S(1)} collective-permute-done((f32[2,96,256]{2,1,0:T(8,128)S(1)}, f32[2,96,256]{2,1,0:T(8,128)S(1)}, u32[]{:S(2)}, u32[]{:S(2)}) %collective-permute-start.3) | collective-permute-done | bytes 196640 | tf_op jit(solution)/shard_map/ppermute | solution.py:293
  16.9 0.1 collective-permute-start.4
  16.9 6.9 %collective-permute-done.4 = f32[2,96,256]{2,1,0:T(8,128)S(1)} collective-permute-done((f32[2,96,256]{2,1,0:T(8,128)S(1)}, f32[2,96,256]{2,1,0:T(8,128)S(1)}, u32[]{:S(2)}, u32[]{:S(2)}) %collective-permute-start.4) | collective-permute-done | bytes 196640 | tf_op jit(solution)/shard_map/ppermute | solution.py:296
  23.9 0.1 collective-permute-start.7
  24.0 0.0 copy-done
  24.0 0.4 collective-permute-start.5
  24.3 2.0 %collective-permute-start.9 = (f32[2,96,256]{2,1,0:T(8,128)S(1)}, f32[2,96,256]{2,1,0:T(8,128)S(1)}, u32[]{:S(2)}, u32[]{:S(2)}) collective-permute-start(f32[2,96,256]{2,1,0:T(8,128)S(1)} %add.9.own_image), channel_id=1, source_target_pairs={{3,0},{0,4},{2,8},{1,12},{7,1},{4,5},{6,9},{5,13},{8,2},{11,6},{9,... | collective-permute-start | bytes 589832 | tf_op jit(solution)/shard_map/ppermute | solution.py:302
  26.4 4.4 %collective-permute-start.8 = (f32[2,96,256]{2,1,0:T(8,128)S(1)}, f32[2,96,256]{2,1,0:T(8,128)S(1)}, u32[]{:S(2)}, u32[]{:S(2)}) collective-permute-start(f32[2,96,256]{2,1,0:T(8,128)S(1)} %add.9.own_image), channel_id=1, source_target_pairs={{0,0},{3,4},{1,8},{2,12},{4,1},{7,5},{5,9},{6,13},{11,2},{8,6},{10... | collective-permute-start | bytes 589832 | tf_op jit(solution)/shard_map/ppermute | solution.py:302
  30.7 0.0 collective-permute-done.5.refs_0_
  30.7 0.1 collective-permute-start.6
  30.8 0.0 collective-permute-done.7.other_image
  30.8 1.7 %half_gradient.1 = (f32[8,256,256]{2,1,0:T(8,128)S(1)}, f32[1,256,256]{2,1,0:T(8,128)}) custom-call(s32[5,8]{1,0:T(8,128)S(4)} %get-tuple-element.19.guide, f32[2,96,256]{2,1,0:T(8,128)S(1)} %add.9.own_image, f32[2,96,256]{2,1,0:T(8,128)S(1)} %collective-permute-done.7.other_image, f32[2,96,256]{2,1,0:T(8,128)S(1)} %constant_dynamic-update-slice_fusion.samples.pair, ...), custom_call_target="tpu_custom_call" | custom-call | tf_op jit(solution)/shard_map/half_gradient/pallas_call | solution.py:175
  32.5 0.0 collective-permute-done.6.refs_1_
  32.5 0.4 row_panel.1
  32.9 0.4 %collective-permute-done.9.piece = f32[2,96,256]{2,1,0:T(8,128)S(1)} collective-permute-done((f32[2,96,256]{2,1,0:T(8,128)S(1)}, f32[2,96,256]{2,1,0:T(8,128)S(1)}, u32[]{:S(2)}, u32[]{:S(2)}) %collective-permute-start.9) | collective-permute-done | bytes 196640 | tf_op jit(solution)/shard_map/ppermute | solution.py:302
  33.3 1.6 %update_slots.2.refs_0_ = f32[8,256,256]{2,1,0:T(8,128)} custom-call(s32[5,8]{1,0:T(8,128)S(4)} %get-tuple-element.19.guide, bf16[4,256,192]{2,1,0:T(8,128)(2,1)S(1)} %get-tuple-element.32.wide, bf16[4,256,96]{2,1,0:T(8,128)(2,1)S(1)} %get-tuple-element.33.low, f32[2,96,256]{2,1,0:T(8,128)S(1)} %collective-permute-done.9.piece, ...), custom_call_target="tpu_custom_call" | custom-call | tf_op jit(solution)/shard_map/update_slots/pallas_call | solution.py:248
  34.9 2.2 %collective-permute-done.8.piece = f32[2,96,256]{2,1,0:T(8,128)S(1)} collective-permute-done((f32[2,96,256]{2,1,0:T(8,128)S(1)}, f32[2,96,256]{2,1,0:T(8,128)S(1)}, u32[]{:S(2)}, u32[]{:S(2)}) %collective-permute-start.8) | collective-permute-done | bytes 196640 | tf_op jit(solution)/shard_map/ppermute | solution.py:302
  37.1 1.5 %update_slots.3 = f32[8,256,256]{2,1,0:T(8,128)} custom-call(s32[5,8]{1,0:T(8,128)S(4)} %get-tuple-element.19.guide, bf16[4,256,192]{2,1,0:T(8,128)(2,1)S(1)} %get-tuple-element.32.wide, bf16[4,256,96]{2,1,0:T(8,128)(2,1)S(1)} %get-tuple-element.33.low, f32[2,96,256]{2,1,0:T(8,128)S(1)} %collective-permute-done.8.piece, ...), custom_call_target="tpu_custom_call", output_to_operand_aliasing={{}: (5, {})} | custom-call | tf_op jit(solution)/shard_map/update_slots/pallas_call | solution.py:248
  (3 shorter events, 0.1 us)
Async XLA Ops:
  0.6 1.6 %collective-permute-start = (f32[1,96,256]{2,1,0:T(8,128)}, f32[1,96,256]{2,1,0:T(8,128)S(1)}, u32[]{:S(2)}, u32[]{:S(2)}) collective-permute-start(f32[1,96,256]{2,1,0:T(8,128)} %bitcast.8), channel_id=1, source_target_pairs={{0,1},{1,0},{2,3},{3,2},{4,5},{5,4},{6,7},{7,6},{8,9},{9,8},{10,11... | collective-permute-start | bytes 294920 | tf_op jit(solution)/shard_map/ppermute | solution.py:286
  2.2 9.4 %collective-permute-start.2 = (f32[2,96,256]{2,1,0:T(8,128)S(1)}, f32[2,96,256]{2,1,0:T(8,128)S(1)}, u32[]{:S(2)}, u32[]{:S(2)}) collective-permute-start(f32[2,96,256]{2,1,0:T(8,128)S(1)} %constant_dynamic-update-slice_fusion.samples.pair), channel_id=1, source_target_pairs={{3,0},{0,4},{2,8},{1,12},{7,1},{4,5},{6,9},{5,13},{8,2},{11,6},{9,... | collective-permute-start | bytes 589832 | tf_op jit(solution)/shard_map/ppermute | solution.py:289
  4.8 9.9 %collective-permute-start.1 = (f32[2,96,256]{2,1,0:T(8,128)S(1)}, f32[2,96,256]{2,1,0:T(8,128)S(1)}, u32[]{:S(2)}, u32[]{:S(2)}) collective-permute-start(f32[2,96,256]{2,1,0:T(8,128)S(1)} %constant_dynamic-update-slice_fusion.samples.pair), channel_id=1, source_target_pairs={{0,0},{3,4},{1,8},{2,12},{4,1},{7,5},{5,9},{6,13},{11,2},{8,6},{10... | collective-permute-start | bytes 589832 | tf_op jit(solution)/shard_map/ppermute | solution.py:289
  11.6 12.4 %copy-start = (f32[96,256]{1,0:T(8,128)S(1)}, f32[96,256]{1,0:T(8,128)}, u32[]{:S(2)}) copy-start(f32[96,256]{1,0:T(8,128)} %param.5) | copy-start | bytes 294916
  15.3 1.5 %collective-permute-start.3 = (f32[2,96,256]{2,1,0:T(8,128)S(1)}, f32[2,96,256]{2,1,0:T(8,128)S(1)}, u32[]{:S(2)}, u32[]{:S(2)}) collective-permute-start(f32[2,96,256]{2,1,0:T(8,128)S(1)} %get-tuple-element.24), channel_id=1, source_target_pairs={{0,1},{1,0},{2,3},{3,2},{4,5},{5,4},{6,7},{7,6},{8,9},{9,8},{10,11... | collective-permute-start | bytes 589832 | tf_op jit(solution)/shard_map/ppermute | solution.py:293
  16.9 7.0 %collective-permute-start.4 = (f32[2,96,256]{2,1,0:T(8,128)S(1)}, f32[2,96,256]{2,1,0:T(8,128)S(1)}, u32[]{:S(2)}, u32[]{:S(2)}) collective-permute-start(f32[2,96,256]{2,1,0:T(8,128)S(1)} %add.8), channel_id=1, source_target_pairs={{0,2},{2,0},{1,3},{3,1},{4,6},{6,4},{5,7},{7,5},{8,10},{10,8},{9,1... | collective-permute-start | bytes 589832 | tf_op jit(solution)/shard_map/ppermute | solution.py:296
  23.9 6.9 %collective-permute-start.7 = (f32[2,96,256]{2,1,0:T(8,128)S(1)}, f32[2,96,256]{2,1,0:T(8,128)S(1)}, u32[]{:S(2)}, u32[]{:S(2)}) collective-permute-start(f32[2,96,256]{2,1,0:T(8,128)S(1)} %add.9.own_image), channel_id=1, source_target_pairs={{0,1},{1,0},{2,3},{3,2},{4,5},{5,4},{6,7},{7,6},{8,9},{9,8},{10,11... | collective-permute-start | bytes 589832 | tf_op jit(solution)/shard_map/ppermute | solution.py:304
  24.0 6.7 %collective-permute-start.5 = (f32[96,256]{1,0:T(8,128)S(1)}, f32[96,256]{1,0:T(8,128)S(1)}, u32[]{:S(2)}, u32[]{:S(2)}) collective-permute-start(f32[96,256]{1,0:T(8,128)S(1)} %copy-done), channel_id=1, source_target_pairs={{0,2},{2,0},{1,3},{3,1},{4,6},{6,4},{5,7},{7,5},{8,10},{10,8},{9,1... | collective-permute-start | bytes 294920 | tf_op jit(solution)/shard_map/ppermute | solution.py:299
  24.3 9.0 %collective-permute-start.9 = (f32[2,96,256]{2,1,0:T(8,128)S(1)}, f32[2,96,256]{2,1,0:T(8,128)S(1)}, u32[]{:S(2)}, u32[]{:S(2)}) collective-permute-start(f32[2,96,256]{2,1,0:T(8,128)S(1)} %add.9.own_image), channel_id=1, source_target_pairs={{3,0},{0,4},{2,8},{1,12},{7,1},{4,5},{6,9},{5,13},{8,2},{11,6},{9,... | collective-permute-start | bytes 589832 | tf_op jit(solution)/shard_map/ppermute | solution.py:302
  26.4 10.8 %collective-permute-start.8 = (f32[2,96,256]{2,1,0:T(8,128)S(1)}, f32[2,96,256]{2,1,0:T(8,128)S(1)}, u32[]{:S(2)}, u32[]{:S(2)}) collective-permute-start(f32[2,96,256]{2,1,0:T(8,128)S(1)} %add.9.own_image), channel_id=1, source_target_pairs={{0,0},{3,4},{1,8},{2,12},{4,1},{7,5},{5,9},{6,13},{11,2},{8,6},{10... | collective-permute-start | bytes 589832 | tf_op jit(solution)/shard_map/ppermute | solution.py:302
  30.7 1.8 %collective-permute-start.6 = (f32[96,256]{1,0:T(8,128)S(1)}, f32[96,256]{1,0:T(8,128)S(1)}, u32[]{:S(2)}, u32[]{:S(2)}) collective-permute-start(f32[96,256]{1,0:T(8,128)S(1)} %collective-permute-done.5.refs_0_), channel_id=1, source_target_pairs={{0,1},{1,0},{2,3},{3,2},{4,5},{5,4},{6,7},{7,6},{8,9},{9,8},{10,11... | collective-permute-start | bytes 294920 | tf_op jit(solution)/shard_map/ppermute | solution.py:300
